TPU v7x, 32 devices: a whole 2x2x4 slice. The times are simulated.
32 devices in a mesh: groups: 1, ep: 32 (over z, y, x, core).
Axes of the slice: x: 2, y: 2, z: 4, core: 2. Of those that a mesh axis runs over, the one named last changes fastest.
Arguments:
- hidden_rows: bfloat16 [256, 7168], P(('groups', 'ep')), may hold values from -6 to 6
- expert_ids: int32 [256, 2], P(('groups', 'ep')), may hold values from 0 to 3, all different within a row; in each aligned block of 8 rows (0 to 7, 8 to 15, ...) at most 8 rows name the same one
- gate_weights: float32 [256, 2], P(('groups', 'ep')), may hold values from 0.2 to 1
- w_gate: bfloat16 [7168, 8192], P(None, 'ep'), may hold values from -0.0625 to 0.0625
- w_up: bfloat16 [7168, 8192], P(None, 'ep'), may hold values from -0.0625 to 0.0625
- w_down: bfloat16 [8192, 7168], P('ep'), may hold values from -0.125 to 0.125
- latent_cache: bfloat16 [256, 48, 576], P(('groups', 'ep')), may hold values from -6 to 6
- new_latent: bfloat16 [256, 576], P(('groups', 'ep')), may hold values from -6 to 6
- parents: int32 [256, 1], P(('groups', 'ep')), may hold values from 0 to 7; in each aligned block of 8 rows (0 to 7, 8 to 15, ...) at most 2 rows name the same one
- lengths: int32 [256], P(('groups', 'ep')), may hold values from 1 to 47
Outputs:
- moe_out: bfloat16 [256, 7168], P(('groups', 'ep'))
- new_cache: bfloat16 [256, 48, 576], P(('groups', 'ep'))
Inputs may be any that keep to these rules, and one draw needn't show every extreme that they name: `parents`: among the rows of one device (aligned blocks of 8 rows) no parent beam is named more than 2 times; in some blocks one is named exactly 2 times. `expert_ids`: each row names 2 different experts; among the rows of one device (aligned blocks of 8 rows) no expert is named more than 8 times, and in some blocks one is named exactly 8 times.
All inputs are finite; a program needn't handle non-finite values.
Results may differ from a plain program's by a relative error of at most 0.0064.
Values may be sent and summed in bfloat16 or wider, within the bound.
No kernel may reach another device: no remote copies, remote signals or barrier semaphores. Data moves between devices by JAX's collectives and lax.ppermute only.
A program may use at most 64 MiB of HBM per device.

v0:
```python
import jax
import jax.numpy as jnp
from jax import lax
from jax.sharding import PartitionSpec as P

D = 7168
TOP = 2
BEAMS = 8
SPLIT = 8
CAP = 2


def passed_along(value, axis, by):
    peers = lax.axis_size(axis)
    return lax.ppermute(value, axis, [(i, (i + by) % peers) for i in range(peers)])


def local(
    hidden_rows,
    expert_ids,
    gate_weights,
    w_gate,
    w_up,
    w_down,
    latent_cache,
    new_latent,
    parents,
    lengths,
):
    device_count = lax.axis_size("ep")
    device_index = lax.axis_index("ep")
    beam_stride = device_count // BEAMS
    own_beam = device_index // beam_stride
    request_block = device_index % beam_stride
    local_rows = hidden_rows.shape[0]
    experts = device_count // SPLIT
    capacity = max(2, min(local_rows, (2 * local_rows * TOP + experts - 1) // experts))
    expert_range = jnp.arange(experts, dtype=jnp.int32)
    chosen = expert_ids[:, :, None] == expert_range[None, None, :]
    hit_count = jnp.sum(chosen.astype(jnp.int32), axis=1)
    before = jnp.cumsum(hit_count, axis=0) - hit_count
    position = jnp.sum(jnp.where(chosen, before[:, None, :], 0), axis=2)
    slot_range = jnp.arange(capacity, dtype=jnp.int32)
    placer = (hit_count.T[:, None, :] == 1) & (before.T[:, None, :] == slot_range[None, :, None])
    outgoing = jnp.einsum(
        "ecr,rd->ecd", placer.astype(jnp.bfloat16), hidden_rows, preferred_element_type=jnp.float32
    ).astype(jnp.bfloat16)
    copies = jnp.broadcast_to(outgoing[:, None], (experts, SPLIT, capacity, D)).reshape(
        device_count, capacity, D
    )
    received = lax.all_to_all(copies, "ep", split_axis=0, concat_axis=0, tiled=True)
    item_count = received.shape[1]
    flat_rows = received.reshape(device_count * item_count, D)
    gate_proj = jnp.dot(flat_rows, w_gate, preferred_element_type=jnp.float32)
    up_proj = jnp.dot(flat_rows, w_up, preferred_element_type=jnp.float32)
    activated = (jax.nn.silu(gate_proj) * up_proj).astype(jnp.bfloat16)
    partial_value = jnp.dot(activated, w_down, preferred_element_type=jnp.float32).astype(
        jnp.bfloat16
    )
    partial_value = partial_value.reshape(device_count, item_count, D)
    result = lax.all_to_all(partial_value, "ep", split_axis=0, concat_axis=0, tiled=True)
    all_parents, all_lengths = (
        lax.all_gather(parents[:, 0], "ep", axis=0, tiled=True),
        lax.all_gather(lengths, "ep", axis=0, tiled=True),
    )
    parent_grid = lax.dynamic_index_in_dim(
        all_parents.reshape(BEAMS, beam_stride, local_rows), request_block, 1, keepdims=False
    )
    length_grid = lax.dynamic_index_in_dim(
        all_lengths.reshape(BEAMS, beam_stride, local_rows), request_block, 1, keepdims=False
    )
    cache_flat = latent_cache.reshape(local_rows, latent_cache.shape[1] * latent_cache.shape[2])
    packet_range = jnp.arange(CAP, dtype=jnp.int32)

    def selector(target_beam, source_beam):
        wanted = jnp.take(parent_grid, target_beam, axis=0) == source_beam
        ranked = jnp.cumsum(wanted.astype(jnp.int32)) - 1
        return ((ranked[None, :] == packet_range[:, None]) & wanted[None, :]).astype(jnp.bfloat16)

    def packet(target_beam):
        return jnp.dot(
            selector(target_beam, own_beam), cache_flat, preferred_element_type=jnp.float32
        ).astype(jnp.bfloat16)

    arrived = [packet(own_beam)]
    sources = [own_beam]
    for offset in range(1, BEAMS):
        arrived.append(
            passed_along(packet((own_beam + offset) % BEAMS), "ep", offset * beam_stride)
        )
        sources.append((own_beam - offset) % BEAMS)
    stacked = jnp.stack(arrived)
    pickers = jnp.stack([selector(own_beam, source_beam) for source_beam in sources])
    migrated = jnp.einsum(
        "acr,acf->rf", pickers, stacked, preferred_element_type=jnp.float32
    ).reshape(latent_cache.shape)
    own_parents = jnp.take(parent_grid, own_beam, axis=0)
    parent_len = jnp.sum(
        jnp.where(
            jnp.arange(BEAMS, dtype=jnp.int32)[:, None] == own_parents[None, :], length_grid, 0
        ),
        axis=0,
    )
    token_place = jnp.arange(latent_cache.shape[1], dtype=jnp.int32)[None, :, None]
    parent_bound = parent_len[:, None, None]
    appended = new_latent.astype(jnp.float32)[:, None, :]
    new_cache = jnp.where(
        token_place < parent_bound, migrated, jnp.where(token_place == parent_bound, appended, 0.0)
    ).astype(jnp.bfloat16)
    grouped = result.reshape(experts, SPLIT, capacity, D)
    expert_out = jnp.sum(grouped.astype(jnp.float32), axis=1).astype(jnp.bfloat16)
    flat_out = expert_out.reshape(experts * capacity, D)
    picked = flat_out[expert_ids * capacity + position]
    moe_out = jnp.sum(gate_weights[:, :, None] * picked.astype(jnp.float32), axis=1).astype(
        jnp.bfloat16
    )
    return (moe_out, new_cache)


def solution(mesh):
    placed = (
        P(("groups", "ep"), None),
        P(("groups", "ep"), None),
        P(("groups", "ep"), None),
        P(None, "ep"),
        P(None, "ep"),
        P("ep", None),
        P(("groups", "ep"), None, None),
        P(("groups", "ep"), None),
        P(("groups", "ep"), None),
        P(("groups", "ep")),
    )
    return jax.shard_map(
        local,
        mesh=mesh,
        in_specs=placed,
        out_specs=(P(("groups", "ep"), None), P(("groups", "ep"), None, None)),
        check_vma=False,
    )
```

profile of v0, /device:TPU:0, one launch (start us, length us, event | category | flops | bytes accessed | tf_op | source)
XLA Modules:
  0.0 244.2 jit_solution(2352580112374808694)
XLA Ops:
  0.6 0.7 convert_reduce_fusion
  1.8 2.3 broadcast_in_dim.43
  4.1 7.4 %all-to-all-start = ((bf16[32,8,7168]{2,1,0:T(8,128)(2,1)}), bf16[32,8,7168]{2,1,0:T(8,128)(2,1)}, u32[]{:S(2)}, u32[]{:S(2)}) async-start(bf16[32,8,7168]{2,1,0:T(8,128)(2,1)} %bitcast.157), calls=%async_computation | async-start | bytes 7340032 | tf_op jit(solution)/shard_map/all_to_all | solution.py:51
  12.4 0.4 reshape.997
  12.8 101.8 %all-reduce.4 = (s32[8,4,8]{2,1,0:T(4,128)S(1)}, s32[8,4,8]{2,1,0:T(4,128)S(1)}) all-reduce(s32[8,4,8]{2,1,0:T(4,128)S(1)} %reshape.987, s32[8,4,8]{2,1,0:T(4,128)S(1)} %reshape.988), channel_id=2, replica_groups=mesh['groups'=1,'ep'=32] {'ep'}, use_global_device_ids=true, to_apply=%add | all-reduce | flops 512 | bytes 4096
  115.2 2.3 collective-permute-start
  118.6 1.8 collective-permute-start.2
  120.8 2.2 collective-permute-start.3
  123.4 2.6 %collective-permute-start.4 = (bf16[2,27648]{1,0:T(2,128)(2,1)S(1)}, bf16[2,27648]{1,0:T(2,128)(2,1)S(1)}, u32[]{:S(2)}, u32[]{:S(2)}) collective-permute-start(bf16[2,27648]{1,0:T(2,128)(2,1)S(1)} %convolution_convert_fusion.2), channel_id=1, source_target_pairs={{0,20},{1,21},{2,22},{3,23},{4,24},{5,25},{6,26},{7,27},{8,28},{9,... | collective-permute-start | bytes 331784 | tf_op jit(solution)/shard_map/ppermute | solution.py:15
  129.3 0.3 convolution_convert_fusion.1
  130.0 1.3 collective-permute-start.5
  131.4 0.6 collective-permute-start.6
  132.2 1.0 collective-permute-done.3
  133.4 4.3 %fusion.5 = f32[256,256]{1,0:T(8,128)S(1)} fusion(bf16[7168,256]{1,0:T(8,128)(2,1)} %param.15, bf16[32,8,7168]{2,1,0:T(8,128)(2,1)} %all-to-all-done), kind=kOutput, calls=%fused_computation.18 | convolution fusion | flops 939524096 | bytes 7602176 | tf_op jit(solution)/shard_map/dot_general | solution.py:54
  137.7 10.0 %fusion.2 = bf16[32,8,7168]{2,1,0:T(8,128)(2,1)} fusion(bf16[256,7168]{1,0:T(8,128)(2,1)} %param.17, bf16[7168,256]{1,0:T(8,128)(2,1)} %param.16, bf16[32,8,7168]{2,1,0:T(8,128)(2,1)} %all-to-all-done, f32[256,256]{1,0:T(8,128)S(1)} %fusion.5), kind=kOutput, calls=%fused_computation.13 | convolution fusion | flops 1881276416 | bytes 14942208 | tf_op jit(solution)/shard_map/dot_general | solution.py:57
  147.7 9.1 %all-to-all-start.1 = ((bf16[32,8,7168]{2,1,0:T(8,128)(2,1)}), bf16[32,8,7168]{2,1,0:T(8,128)(2,1)}, u32[]{:S(2)}, u32[]{:S(2)}) async-start(bf16[32,8,7168]{2,1,0:T(8,128)(2,1)} %fusion.2), calls=%async_computation.1 | async-start | bytes 7340032 | tf_op jit(solution)/shard_map/all_to_all | solution.py:61
  157.0 0.3 convolution_bitcast_fusion
  157.3 0.4 reshape.1005
  157.8 1.0 select_convert_fusion
  158.8 80.6 %all-to-all-done.1 = bf16[32,8,7168]{2,1,0:T(8,128)(2,1)} async-done(((bf16[32,8,7168]{2,1,0:T(8,128)(2,1)}), bf16[32,8,7168]{2,1,0:T(8,128)(2,1)}, u32[]{:S(2)}, u32[]{:S(2)}) %all-to-all-start.1) | async-done | bytes 3670048 | tf_op jit(solution)/shard_map/all_to_all | solution.py:61
  239.3 2.6 %bitcast_reduce_fusion = bf16[4,8,7168]{2,1,0:T(8,128)(2,1)S(1)} fusion(bf16[32,8,7168]{2,1,0:T(8,128)(2,1)} %all-to-all-done.1), kind=kLoop, calls=%fused_computation.15 | loop fusion | flops 1605632 | bytes 4128768 | tf_op jit(solution)/shard_map/reduce_sum | solution.py:111
  241.9 0.7 gather_fusion
  242.6 0.3 reshape.1154
  242.9 1.3 multiply_reduce_fusion
  (96 shorter events, 7.6 us)
Async XLA Ops:
  0.6 0.9 copy-start
  4.1 7.5 %copy-start.5 = (s32[8,1]{0,1:T(1,128)S(1)}, s32[8,1]{0,1:T(1,128)}, u32[]{:S(2)}) copy-start(s32[8,1]{0,1:T(1,128)} %param.20) | copy-start | bytes 100
  4.1 7.7 %copy-start.6 = (s32[8]{0:T(128)S(1)}, s32[8]{0:T(128)}, u32[]{:S(2)}) copy-start(s32[8]{0:T(128)} %param.21) | copy-start | bytes 100
  4.1 8.3 %copy-start.1 = (bf16[8,48,576]{2,1,0:T(8,128)(2,1)S(1)}, bf16[8,48,576]{2,1,0:T(8,128)(2,1)}, u32[]{:S(2)}) copy-start(bf16[8,48,576]{2,1,0:T(8,128)(2,1)} %param.18) | copy-start | bytes 1327108
  4.1 129.3 %all-to-all-start = ((bf16[32,8,7168]{2,1,0:T(8,128)(2,1)}), bf16[32,8,7168]{2,1,0:T(8,128)(2,1)}, u32[]{:S(2)}, u32[]{:S(2)}) async-start(bf16[32,8,7168]{2,1,0:T(8,128)(2,1)} %bitcast.157), calls=%async_computation | async-start | bytes 7340032 | tf_op jit(solution)/shard_map/all_to_all | solution.py:51
  11.5 114.5 %copy-start.3 = (s32[8,2]{0,1:T(2,128)S(1)}, s32[8,2]{0,1:T(2,128)}, u32[]{:S(2)}) copy-start(s32[8,2]{0,1:T(2,128)} %param.13) | copy-start | bytes 196
  11.5 115.4 %copy-start.4 = (f32[8,2]{0,1:T(2,128)S(1)}, f32[8,2]{0,1:T(2,128)}, u32[]{:S(2)}) copy-start(f32[8,2]{0,1:T(2,128)} %param.14) | copy-start | bytes 196
  115.2 14.7 %collective-permute-start = (bf16[2,27648]{1,0:T(2,128)(2,1)S(1)}, bf16[2,27648]{1,0:T(2,128)(2,1)S(1)}, u32[]{:S(2)}, u32[]{:S(2)}) collective-permute-start(bf16[2,27648]{1,0:T(2,128)(2,1)S(1)} %convolution_convert_fusion.6), channel_id=1, source_target_pairs={{0,4},{1,5},{2,6},{3,7},{4,8},{5,9},{6,10},{7,11},{8,12},{9,13},{1... | collective-permute-start | bytes 331784 | tf_op jit(solution)/shard_map/ppermute | solution.py:15
  118.0 13.4 %collective-permute-start.1 = (bf16[2,27648]{1,0:T(2,128)(2,1)S(1)}, bf16[2,27648]{1,0:T(2,128)(2,1)S(1)}, u32[]{:S(2)}, u32[]{:S(2)}) collective-permute-start(bf16[2,27648]{1,0:T(2,128)(2,1)S(1)} %convolution_convert_fusion.5), channel_id=1, source_target_pairs={{0,8},{1,9},{2,10},{3,11},{4,12},{5,13},{6,14},{7,15},{8,16},{9,17... | collective-permute-start | bytes 331784 | tf_op jit(solution)/shard_map/ppermute | solution.py:15
  118.6 13.6 %collective-permute-start.2 = (bf16[2,27648]{1,0:T(2,128)(2,1)S(1)}, bf16[2,27648]{1,0:T(2,128)(2,1)S(1)}, u32[]{:S(2)}, u32[]{:S(2)}) collective-permute-start(bf16[2,27648]{1,0:T(2,128)(2,1)S(1)} %convolution_convert_fusion.4), channel_id=1, source_target_pairs={{0,12},{1,13},{2,14},{3,15},{4,16},{5,17},{6,18},{7,19},{8,20},{9,... | collective-permute-start | bytes 331784 | tf_op jit(solution)/shard_map/ppermute | solution.py:15
  120.8 12.4 %collective-permute-start.3 = (bf16[2,27648]{1,0:T(2,128)(2,1)S(1)}, bf16[2,27648]{1,0:T(2,128)(2,1)S(1)}, u32[]{:S(2)}, u32[]{:S(2)}) collective-permute-start(bf16[2,27648]{1,0:T(2,128)(2,1)S(1)} %convolution_convert_fusion.3), channel_id=1, source_target_pairs={{0,16},{1,17},{2,18},{3,19},{4,20},{5,21},{6,22},{7,23},{8,24},{9,... | collective-permute-start | bytes 331784 | tf_op jit(solution)/shard_map/ppermute | solution.py:15
  123.4 9.9 %collective-permute-start.4 = (bf16[2,27648]{1,0:T(2,128)(2,1)S(1)}, bf16[2,27648]{1,0:T(2,128)(2,1)S(1)}, u32[]{:S(2)}, u32[]{:S(2)}) collective-permute-start(bf16[2,27648]{1,0:T(2,128)(2,1)S(1)} %convolution_convert_fusion.2), channel_id=1, source_target_pairs={{0,20},{1,21},{2,22},{3,23},{4,24},{5,25},{6,26},{7,27},{8,28},{9,... | collective-permute-start | bytes 331784 | tf_op jit(solution)/shard_map/ppermute | solution.py:15
  130.0 26.8 %collective-permute-start.5 = (bf16[2,27648]{1,0:T(2,128)(2,1)S(1)}, bf16[2,27648]{1,0:T(2,128)(2,1)S(1)}, u32[]{:S(2)}, u32[]{:S(2)}) collective-permute-start(bf16[2,27648]{1,0:T(2,128)(2,1)S(1)} %convolution_convert_fusion.1), channel_id=1, source_target_pairs={{0,24},{1,25},{2,26},{3,27},{4,28},{5,29},{6,30},{7,31},{8,0},{9,1... | collective-permute-start | bytes 331784 | tf_op jit(solution)/shard_map/ppermute | solution.py:15
  131.4 25.5 %collective-permute-start.6 = (bf16[2,27648]{1,0:T(2,128)(2,1)S(1)}, bf16[2,27648]{1,0:T(2,128)(2,1)S(1)}, u32[]{:S(2)}, u32[]{:S(2)}) collective-permute-start(bf16[2,27648]{1,0:T(2,128)(2,1)S(1)} %convolution_convert_fusion), channel_id=1, source_target_pairs={{0,28},{1,29},{2,30},{3,31},{4,0},{5,1},{6,2},{7,3},{8,4},{9,5},{1... | collective-permute-start | bytes 331784 | tf_op jit(solution)/shard_map/ppermute | solution.py:15
  147.7 10.0 %copy-start.2 = (bf16[8,576]{1,0:T(8,128)(2,1)S(1)}, bf16[8,576]{1,0:T(8,128)(2,1)}, u32[]{:S(2)}) copy-start(bf16[8,576]{1,0:T(8,128)(2,1)} %param.19) | copy-start | bytes 27652
  147.7 91.6 %all-to-all-start.1 = ((bf16[32,8,7168]{2,1,0:T(8,128)(2,1)}), bf16[32,8,7168]{2,1,0:T(8,128)(2,1)}, u32[]{:S(2)}, u32[]{:S(2)}) async-start(bf16[32,8,7168]{2,1,0:T(8,128)(2,1)} %fusion.2), calls=%async_computation.1 | async-start | bytes 7340032 | tf_op jit(solution)/shard_map/all_to_all | solution.py:61
where the time goes:
time: 245 us; the launch traced here: 244 us
  blocking collectives  102 us (42%)
  waiting for transfers between devices  81.6 us (33%)
  starting transfers between devices  27.4 us (11%)
  matrix products  17 us (7%)
  other arithmetic  9.43 us (4%)
  local copies, waits for them, and re-layouts  5.64 us (2%)
    unnamed x1, blocking collectives  102 us
    all_to_all x1, waiting for transfers between devices, local(): lax.all_to_all(partial_value, 'ep', split_axis=0, concat_axis=0, tiled=True)  80.6 us
    ppermute x7, starting transfers between devices, passed_along(): lax.ppermute(value, axis, [(i, (i + by) % peers) for i in range(peers)])  10.9 us
    dot_general x1, matrix products, local(): jnp.dot(activated, w_down, preferred_element_type=jnp.float32)  10 us
    all_to_all x1, starting transfers between devices, local(): lax.all_to_all(partial_value, 'ep', split_axis=0, concat_axis=0, tiled=True)  9.06 us
    all_to_all x1, starting transfers between devices, local(): lax.all_to_all(copies, 'ep', split_axis=0, concat_axis=0, tiled=True)  7.41 us
  transfers between devices with their start and end apart: 9, of which 2 were waited for; matrix products, arithmetic and copies ran while one was open for 10% of the time, Pallas kernels for 0%

commit v1 on v0

--- a/solution.py
+++ b/solution.py
@@ -8,11 +8,132 @@
 BEAMS = 8
 SPLIT = 8
 CAP = 2
+LANES = 128
 
 
 def passed_along(value, axis, by):
     peers = lax.axis_size(axis)
     return lax.ppermute(value, axis, [(i, (i + by) % peers) for i in range(peers)])
+
+
+def swapped(value, mask):
+    peers = lax.axis_size("ep")
+    return lax.ppermute(value, "ep", [(i, i ^ mask) for i in range(peers)])
+
+
+def dot32(a, b):
+    return jnp.dot(a, b, preferred_element_type=jnp.float32)
+
+
+def dense_local(
+    hidden_rows,
+    expert_ids,
+    gate_weights,
+    w_gate,
+    w_up,
+    w_down,
+    latent_cache,
+    new_latent,
+    parents,
+    lengths,
+):
+    device_count = lax.axis_size("ep")
+    device_index = lax.axis_index("ep")
+    experts = device_count // SPLIT
+    rows = hidden_rows.shape[0]
+    beam_stride = device_count // BEAMS
+    own_beam = device_index // beam_stride
+    own_expert = device_index // SPLIT
+    bf16 = jnp.bfloat16
+
+    tail = jnp.concatenate([parents, lengths[:, None]], axis=1).astype(bf16)
+    tail = jnp.pad(tail, ((0, 0), (0, LANES - 2)))
+    carried = jnp.concatenate([hidden_rows, tail], axis=1)
+    own = jnp.concatenate(
+        [carried] + [swapped(carried, SPLIT * k) for k in range(1, experts)], axis=0
+    )
+    quad = own.shape[0]
+    half = quad // 2
+    from_x = swapped(own, 2)
+    from_y = swapped(own, 4)
+    diag_a = swapped(from_x[:half, :D], 4)
+    diag_b = swapped(from_y[half:, :D], 2)
+    chip_rows = jnp.concatenate([own[:, :D], from_x[:, :D], from_y[:, :D], diag_a, diag_b], axis=0)
+    other_rows = swapped(chip_rows, 1)
+
+    meta = jnp.stack(
+        [own[:, D : D + 2].reshape(experts, rows, 2), from_y[:, D : D + 2].reshape(experts, rows, 2)],
+        axis=1,
+    ).reshape(BEAMS, rows, 2)
+    meta = meta.astype(jnp.int32)
+    place = jnp.arange(BEAMS, dtype=jnp.int32)
+    rank_range = jnp.arange(CAP, dtype=jnp.int32)
+    wanted = meta[:, :, 0] == own_beam
+    ranked = jnp.cumsum(wanted.astype(jnp.int32), axis=1) - 1
+    selector = (
+        (ranked[:, None, :] == rank_range[None, :, None]) & wanted[:, None, :]
+    ).astype(bf16)
+    selector = selector[place ^ own_beam]
+    cache_flat = latent_cache.reshape(rows, -1)
+    packets = dot32(selector.reshape(BEAMS * CAP, rows), cache_flat).astype(bf16)
+    groups = [
+        [b * beam_stride + r for b in range(BEAMS)] for r in range(beam_stride)
+    ]
+    arrived = lax.all_to_all(
+        packets, "ep", split_axis=0, concat_axis=0, axis_index_groups=groups, tiled=True
+    )
+
+    def hidden_units(block):
+        gate = dot32(block, w_gate)
+        up = dot32(block, w_up)
+        return (jax.nn.silu(gate) * up).astype(bf16)
+
+    every = jnp.concatenate([chip_rows, other_rows], axis=0)
+    act = hidden_units(every)
+    chip = chip_rows.shape[0]
+    leaving = dot32(act[chip:], w_down).astype(bf16)
+    total = (dot32(act[:chip], w_down) + swapped(leaving, 1).astype(jnp.float32)).astype(bf16)
+    mine, for_x, for_y, for_d = (total[i * quad : (i + 1) * quad] for i in range(4))
+    got_a = swapped(for_d[:half], 2)
+    got_b = swapped(for_d[half:], 4)
+    f32 = jnp.float32
+    for_y = jnp.concatenate(
+        [(for_y[:half].astype(f32) + got_a.astype(f32)).astype(bf16), for_y[half:]], axis=0
+    )
+    for_x = jnp.concatenate(
+        [for_x[:half], (for_x[half:].astype(f32) + got_b.astype(f32)).astype(bf16)], axis=0
+    )
+    back_x = swapped(for_x, 2)
+    back_y = swapped(for_y, 4)
+    summed = (mine.astype(f32) + back_x.astype(f32) + back_y.astype(f32)).astype(bf16)
+    moe = None
+    for k in range(experts):
+        piece = summed[k * rows : (k + 1) * rows]
+        if k:
+            piece = swapped(piece, SPLIT * k)
+        weight = jnp.sum(
+            jnp.where(expert_ids == (own_expert ^ k), gate_weights, 0.0), axis=1, keepdims=True
+        )
+        term = weight * piece.astype(f32)
+        moe = term if moe is None else moe + term
+    moe_out = moe.astype(bf16)
+
+    own_parents = parents[:, 0]
+    from_beam = own_parents[None, :] == place[:, None]
+    rank_in = jnp.cumsum(from_beam.astype(jnp.int32), axis=1) - 1
+    picker = (
+        from_beam[:, None, :] & (rank_in[:, None, :] == rank_range[None, :, None])
+    ).astype(bf16)
+    migrated = dot32(picker.reshape(BEAMS * CAP, rows).T, arrived).reshape(latent_cache.shape)
+    by_place = (own_parents ^ own_beam)[None, :] == place[:, None]
+    parent_len = jnp.sum(jnp.where(by_place, meta[:, :, 1], 0), axis=0)
+    token_place = jnp.arange(latent_cache.shape[1], dtype=jnp.int32)[None, :, None]
+    parent_bound = parent_len[:, None, None]
+    appended = new_latent.astype(f32)[:, None, :]
+    new_cache = jnp.where(
+        token_place < parent_bound, migrated, jnp.where(token_place == parent_bound, appended, 0.0)
+    ).astype(bf16)
+    return (moe_out, new_cache)
 
 
 def local(
@@ -35,6 +156,19 @@
     local_rows = hidden_rows.shape[0]
     experts = device_count // SPLIT
     capacity = max(2, min(local_rows, (2 * local_rows * TOP + experts - 1) // experts))
+    if capacity == local_rows and experts & (experts - 1) == 0 and beam_stride * 2 == SPLIT:
+        return dense_local(
+            hidden_rows,
+            expert_ids,
+            gate_weights,
+            w_gate,
+            w_up,
+            w_down,
+            latent_cache,
+            new_latent,
+            parents,
+            lengths,
+        )
     expert_range = jnp.arange(experts, dtype=jnp.int32)
     chosen = expert_ids[:, :, None] == expert_range[None, None, :]
     hit_count = jnp.sum(chosen.astype(jnp.int32), axis=1)

time: 245 us -> 109 us (0.44)
  blocking collectives: 102 us -> 0 us
  waiting for transfers between devices: 81.6 us -> 45.1 us
  local copies, waits for them, and re-layouts: 5.64 us -> 18.3 us
  matrix products: 17 us -> 10.4 us
    unnamed x1 -> x0, blocking collectives: 102 us -> none
    all_to_all x2 -> x1, waiting for transfers between devices: 80.6 us -> 16.7 us  [dense_local(): lax.all_to_all(packets, 'ep', split_axis=0, concat_axis=0, axis_index_gro...]
    ppermute x7 -> x16, waiting for transfers between devices: 0.99 us -> 28.4 us  [swapped(): return lax.ppermute(value, 'ep', [(i, i ^ mask) for i in range(peers)])]
    all_to_all x2 -> x1, starting transfers between devices: 16.5 us -> 5.4 us  [dense_local(): lax.all_to_all(packets, 'ep', split_axis=0, concat_axis=0, axis_index_gro...]
    ppermute x7 -> x16, starting transfers between devices: 10.9 us -> 19.7 us  [swapped(): return lax.ppermute(value, 'ep', [(i, i ^ mask) for i in range(peers)])]
    unnamed x25 -> x28, local copies, waits for them, and re-layouts: 1.05 us -> 7.76 us
    dot_general x12 -> x6, matrix products: 17 us -> 10.4 us  [dot32(): return jnp.dot(a, b, preferred_element_type=jnp.float32)]
    reduce_sum x5 -> x2, other arithmetic: 4.63 us -> 0.05 us  [the longest x1 0.03 us: dense_local(): jnp.sum(jnp.where(expert_ids == own_expert ^ k, gate_weights, 0.0), axis=...]
  transfers between devices with their start and end apart: 9 -> 17, of which waited for: 2 -> 10; matrix products, arithmetic and copies ran while one was open for 10% -> 13% of each run, Pallas kernels for 0% -> 0%
where the time goes in v1:
time: 109 us; the launch traced here: 108 us
  waiting for transfers between devices  45.1 us (41%)
  starting transfers between devices  25.1 us (23%)
  local copies, waits for them, and re-layouts  18.3 us (17%)
  matrix products  10.4 us (10%)
  other arithmetic  8.38 us (8%)
    ppermute x16, waiting for transfers between devices, swapped(): return lax.ppermute(value, 'ep', [(i, i ^ mask) for i in range(peers)])  28.4 us
    ppermute x16, starting transfers between devices, swapped(): return lax.ppermute(value, 'ep', [(i, i ^ mask) for i in range(peers)])  19.7 us
    all_to_all x1, waiting for transfers between devices, dense_local(): lax.all_to_all(packets, 'ep', split_axis=0, concat_axis=0, axis_index_gro...  16.7 us
    dot_general x6, matrix products, dot32(): return jnp.dot(a, b, preferred_element_type=jnp.float32)  10.4 us
    unnamed x28, local copies, waits for them, and re-layouts  7.76 us
    all_to_all x1, starting transfers between devices, dense_local(): lax.all_to_all(packets, 'ep', split_axis=0, concat_axis=0, axis_index_gro...  5.4 us
    all_to_all x2, local copies, waits for them, and re-layouts, dense_local(): lax.all_to_all(packets, 'ep', split_axis=0, concat_axis=0, axis_index_gro...  2.81 us
  transfers between devices with their start and end apart: 17, of which 10 were waited for; matrix products, arithmetic and copies ran while one was open for 13% of the time, Pallas kernels for 0%

profile of v1, /device:TPU:0, one launch (start us, length us, event | category | flops | bytes accessed | tf_op | source)
XLA Modules:
  0.0 108.1 jit_solution(9386596552688088757)
XLA Ops:
  3.0 3.1 %collective-permute-start = (bf16[8,7296]{1,0:T(8,128)(2,1)S(1)}, bf16[8,7296]{1,0:T(8,128)(2,1)S(1)}, u32[]{:S(2)}, u32[]{:S(2)}) collective-permute-start(bf16[8,7296]{1,0:T(8,128)(2,1)S(1)} %pad_maximum_fusion.3), channel_id=1, source_target_pairs={{0,8},{1,9},{2,10},{3,11},{4,12},{5,13},{6,14},{7,15},{8,0},{9,1},... | collective-permute-start | bytes 350216 | tf_op jit(solution)/shard_map/ppermute | solution.py:21
  6.1 2.6 %collective-permute-start.1 = (bf16[8,7296]{1,0:T(8,128)(2,1)S(1)}, bf16[8,7296]{1,0:T(8,128)(2,1)S(1)}, u32[]{:S(2)}, u32[]{:S(2)}) collective-permute-start(bf16[8,7296]{1,0:T(8,128)(2,1)S(1)} %pad_maximum_fusion.3), channel_id=1, source_target_pairs={{0,16},{1,17},{2,18},{3,19},{4,20},{5,21},{6,22},{7,23},{8,24},{9,... | collective-permute-start | bytes 350216 | tf_op jit(solution)/shard_map/ppermute | solution.py:21
  8.7 1.8 %collective-permute-done = bf16[8,7296]{1,0:T(8,128)(2,1)S(1)} collective-permute-done((bf16[8,7296]{1,0:T(8,128)(2,1)S(1)}, bf16[8,7296]{1,0:T(8,128)(2,1)S(1)}, u32[]{:S(2)}, u32[]{:S(2)}) %collective-permute-start) | collective-permute-done | bytes 116768 | tf_op jit(solution)/shard_map/ppermute | solution.py:21
  10.5 7.4 %collective-permute-done.1 = bf16[8,7296]{1,0:T(8,128)(2,1)S(1)} collective-permute-done((bf16[8,7296]{1,0:T(8,128)(2,1)S(1)}, bf16[8,7296]{1,0:T(8,128)(2,1)S(1)}, u32[]{:S(2)}, u32[]{:S(2)}) %collective-permute-start.1) | collective-permute-done | bytes 116768 | tf_op jit(solution)/shard_map/ppermute | solution.py:21
  18.9 1.6 %collective-permute-start.3 = (bf16[32,7296]{1,0:T(8,128)(2,1)S(1)}, bf16[32,7296]{1,0:T(8,128)(2,1)S(1)}, u32[]{:S(2)}, u32[]{:S(2)}) collective-permute-start(bf16[32,7296]{1,0:T(8,128)(2,1)S(1)} %pad_maximum_fusion), channel_id=1, source_target_pairs={{0,2},{1,3},{2,0},{3,1},{4,6},{5,7},{6,4},{7,5},{8,10},{9,11},{10,... | collective-permute-start | bytes 1400840 | tf_op jit(solution)/shard_map/ppermute | solution.py:21
  20.4 1.5 %collective-permute-start.4 = (bf16[32,7296]{1,0:T(8,128)(2,1)S(1)}, bf16[32,7296]{1,0:T(8,128)(2,1)S(1)}, u32[]{:S(2)}, u32[]{:S(2)}) collective-permute-start(bf16[32,7296]{1,0:T(8,128)(2,1)S(1)} %pad_maximum_fusion), channel_id=1, source_target_pairs={{0,4},{1,5},{2,6},{3,7},{4,0},{5,1},{6,2},{7,3},{8,12},{9,13},{10,... | collective-permute-start | bytes 1400840 | tf_op jit(solution)/shard_map/ppermute | solution.py:21
  22.8 6.3 %collective-permute-done.3 = bf16[32,7296]{1,0:T(8,128)(2,1)S(1)} collective-permute-done((bf16[32,7296]{1,0:T(8,128)(2,1)S(1)}, bf16[32,7296]{1,0:T(8,128)(2,1)S(1)}, u32[]{:S(2)}, u32[]{:S(2)}) %collective-permute-start.3) | collective-permute-done | bytes 466976 | tf_op jit(solution)/shard_map/ppermute | solution.py:21
  29.1 1.6 %collective-permute-start.5 = (bf16[16,7168]{1,0:T(8,128)(2,1)S(1)}, bf16[16,7168]{1,0:T(8,128)(2,1)S(1)}, u32[]{:S(2)}, u32[]{:S(2)}) collective-permute-start(bf16[16,7168]{1,0:T(8,128)(2,1)S(1)} %slice.102), channel_id=1, source_target_pairs={{0,4},{1,5},{2,6},{3,7},{4,0},{5,1},{6,2},{7,3},{8,12},{9,13},{10,... | collective-permute-start | bytes 688136 | tf_op jit(solution)/shard_map/ppermute | solution.py:21
  30.7 1.5 %collective-permute-done.4 = bf16[32,7296]{1,0:T(8,128)(2,1)S(1)} collective-permute-done((bf16[32,7296]{1,0:T(8,128)(2,1)S(1)}, bf16[32,7296]{1,0:T(8,128)(2,1)S(1)}, u32[]{:S(2)}, u32[]{:S(2)}) %collective-permute-start.4) | collective-permute-done | bytes 466976 | tf_op jit(solution)/shard_map/ppermute | solution.py:21
  35.9 2.3 %collective-permute-done.6 = bf16[16,7168]{1,0:T(8,128)(2,1)S(1)} collective-permute-done((bf16[16,7168]{1,0:T(8,128)(2,1)S(1)}, bf16[16,7168]{1,0:T(8,128)(2,1)S(1)}, u32[]{:S(2)}, u32[]{:S(2)}) %collective-permute-start.6) | collective-permute-done | bytes 229408 | tf_op jit(solution)/shard_map/ppermute | solution.py:21
  39.0 1.8 %copy-done.3 = bf16[256,7168]{1,0:T(8,128)(2,1)} copy-done((bf16[256,7168]{1,0:T(8,128)(2,1)}, bf16[256,7168]{1,0:T(8,128)(2,1)S(1)}, u32[]{:S(2)}) %copy-start.3) | copy-done | bytes 3670040
  40.8 4.0 %collective-permute-done.7 = bf16[128,7168]{1,0:T(8,128)(2,1)S(1)} collective-permute-done((bf16[128,7168]{1,0:T(8,128)(2,1)}, bf16[128,7168]{1,0:T(8,128)(2,1)S(1)}, u32[]{:S(2)}, u32[]{:S(2)}) %collective-permute-start.7) | collective-permute-done | bytes 1835040 | tf_op jit(solution)/shard_map/ppermute | solution.py:21
  46.1 3.4 %fusion.21 = f32[256,256]{1,0:T(8,128)S(1)} fusion(bf16[256,7168]{1,0:T(8,128)(2,1)} %constant_dynamic-update-slice_fusion.2, bf16[7168,256]{1,0:T(8,128)(2,1)S(1)} %copy-done.8), kind=kOutput, calls=%fused_computation.65 | convolution fusion | flops 939524096 | bytes 7602176 | tf_op jit(solution)/shard_map/dot_general | solution.py:25
  53.2 1.5 %reshape.190 = bf16[8,27648]{1,0:T(8,128)(2,1)S(1)} reshape(bf16[8,48,576]{2,1,0:T(8,128)(2,1)} %param.16) | data formatting | bytes 884736 | tf_op jit(solution)/shard_map/reshape | solution.py:77
  57.0 3.3 %add_convert_fusion = bf16[128,7168]{1,0:T(8,128)(2,1)S(1)} fusion(bf16[128,7168]{1,0:T(8,128)(2,1)} %collective-permute-done.8, bf16[256,7168]{1,0:T(8,128)(2,1)} %param.15, bf16[256,256]{1,0:T(8,128)(2,1)S(1)} %multiply_convert_fusion), kind=kOutput, calls=%fused_computation.3 | convolution fusion | flops 472514560 | bytes 7405568 | tf_op jit(solution)/shard_map/dot_general | solution.py:25
  64.4 5.4 %all-to-all-start = ((bf16[8,2,27648]{2,1,0:T(2,128)(2,1)}), bf16[8,2,27648]{2,1,0:T(2,128)(2,1)}, u32[]{:S(2)}, u32[]{:S(2)}) async-start(bf16[8,2,27648]{2,1,0:T(2,128)(2,1)} %all_to_all.8), calls=%async_computation | async-start | bytes 1769472 | tf_op jit(solution)/shard_map/all_to_all | solution.py:82
  73.7 1.7 %collective-permute-start.12 = (bf16[32,7168]{1,0:T(8,128)(2,1)}, bf16[32,7168]{1,0:T(8,128)(2,1)S(1)}, u32[]{:S(2)}, u32[]{:S(2)}) collective-permute-start(bf16[32,7168]{1,0:T(8,128)(2,1)} %pad_maximum_fusion.2), channel_id=1, source_target_pairs={{0,4},{1,5},{2,6},{3,7},{4,0},{5,1},{6,2},{7,3},{8,12},{9,13},{10,... | collective-permute-start | bytes 1376264 | tf_op jit(solution)/shard_map/ppermute | solution.py:21
  75.5 16.7 %all-to-all-done = bf16[8,2,27648]{2,1,0:T(2,128)(2,1)} async-done(((bf16[8,2,27648]{2,1,0:T(2,128)(2,1)}), bf16[8,2,27648]{2,1,0:T(2,128)(2,1)}, u32[]{:S(2)}, u32[]{:S(2)}) %all-to-all-start) | async-done | bytes 884768 | tf_op jit(solution)/shard_map/all_to_all | solution.py:82
  92.2 1.5 %all_to_all.10 = bf16[16,27648]{1,0:T(8,128)(2,1)S(1)} reshape(bf16[8,2,27648]{2,1,0:T(2,128)(2,1)} %all-to-all-done) | data formatting | bytes 1769472 | tf_op jit(solution)/shard_map/all_to_all | solution.py:82
  93.7 1.8 %dot_general.28 = bf16[48,576,16]{1,0,2:T(8,128)(2,1)} reshape(bf16[27648,16]{0,1:T(8,128)(2,1)S(1)} %bitcast.34) | data formatting | bytes 1769472 | tf_op jit(solution)/shard_map/dot_general | solution.py:25
  96.7 1.5 %collective-permute-start.14 = (bf16[8,7168]{1,0:T(8,128)(2,1)S(1)}, bf16[8,7168]{1,0:T(8,128)(2,1)S(1)}, u32[]{:S(2)}, u32[]{:S(2)}) collective-permute-start(bf16[8,7168]{1,0:T(8,128)(2,1)S(1)} %get-tuple-element.26), channel_id=1, source_target_pairs={{0,16},{1,17},{2,18},{3,19},{4,20},{5,21},{6,22},{7,23},{8,24},{9,... | collective-permute-start | bytes 344072 | tf_op jit(solution)/shard_map/ppermute | solution.py:21
  98.3 2.9 %collective-permute-start.15 = (bf16[8,7168]{1,0:T(8,128)(2,1)S(1)}, bf16[8,7168]{1,0:T(8,128)(2,1)S(1)}, u32[]{:S(2)}, u32[]{:S(2)}) collective-permute-start(bf16[8,7168]{1,0:T(8,128)(2,1)S(1)} %get-tuple-element.25), channel_id=1, source_target_pairs={{0,24},{1,25},{2,26},{3,27},{4,28},{5,29},{6,30},{7,31},{8,16},{9,... | collective-permute-start | bytes 344072 | tf_op jit(solution)/shard_map/ppermute | solution.py:21
  101.1 1.6 %fusion = bf16[8,48,576]{2,0,1:T(8,128)(2,1)S(1)} fusion(bf16[48,576,16]{1,0,2:T(8,128)(2,1)} %dot_general.28, bf16[8,576]{1,0:T(8,128)(2,1)S(1)} %copy-done.10, pred[8,48]{0,1:T(8,128)(4,1)S(1)} %get-tuple-element.34, pred[8,48]{0,1:T(8,128)(4,1)S(1)} %get-tuple-element.33, pred[16,8]{1,0:T(8,128)(4,1)S(1)} %and.40), kind=kOutput, calls=%fused_computation.5 | convolution fusion | flops 7520256 | bytes 1337216 | tf_op jit(solution)/shard_map/dot_general | solution.py:25
  103.5 3.8 %collective-permute-done.14 = bf16[8,7168]{1,0:T(8,128)(2,1)S(1)} collective-permute-done((bf16[8,7168]{1,0:T(8,128)(2,1)S(1)}, bf16[8,7168]{1,0:T(8,128)(2,1)S(1)}, u32[]{:S(2)}, u32[]{:S(2)}) %collective-permute-start.14) | collective-permute-done | bytes 114720 | tf_op jit(solution)/shard_map/ppermute | solution.py:21
  (88 shorter events, 26.9 us)
Async XLA Ops:
  3.0 37.8 %copy-start.7 = (s32[8,1]{0,1:T(1,128)S(1)}, s32[8,1]{0,1:T(1,128)}, u32[]{:S(2)}) copy-start(s32[8,1]{0,1:T(1,128)} %param.18) | copy-start | bytes 100
  3.0 7.5 %collective-permute-start = (bf16[8,7296]{1,0:T(8,128)(2,1)S(1)}, bf16[8,7296]{1,0:T(8,128)(2,1)S(1)}, u32[]{:S(2)}, u32[]{:S(2)}) collective-permute-start(bf16[8,7296]{1,0:T(8,128)(2,1)S(1)} %pad_maximum_fusion.3), channel_id=1, source_target_pairs={{0,8},{1,9},{2,10},{3,11},{4,12},{5,13},{6,14},{7,15},{8,0},{9,1},... | collective-permute-start | bytes 350216 | tf_op jit(solution)/shard_map/ppermute | solution.py:21
  6.1 11.9 %collective-permute-start.1 = (bf16[8,7296]{1,0:T(8,128)(2,1)S(1)}, bf16[8,7296]{1,0:T(8,128)(2,1)S(1)}, u32[]{:S(2)}, u32[]{:S(2)}) collective-permute-start(bf16[8,7296]{1,0:T(8,128)(2,1)S(1)} %pad_maximum_fusion.3), channel_id=1, source_target_pairs={{0,16},{1,17},{2,18},{3,19},{4,20},{5,21},{6,22},{7,23},{8,24},{9,... | collective-permute-start | bytes 350216 | tf_op jit(solution)/shard_map/ppermute | solution.py:21
  8.7 9.3 %collective-permute-start.2 = (bf16[8,7296]{1,0:T(8,128)(2,1)S(1)}, bf16[8,7296]{1,0:T(8,128)(2,1)S(1)}, u32[]{:S(2)}, u32[]{:S(2)}) collective-permute-start(bf16[8,7296]{1,0:T(8,128)(2,1)S(1)} %pad_maximum_fusion.3), channel_id=1, source_target_pairs={{0,24},{1,25},{2,26},{3,27},{4,28},{5,29},{6,30},{7,31},{8,16},{9,... | collective-permute-start | bytes 350216 | tf_op jit(solution)/shard_map/ppermute | solution.py:21
  18.9 10.2 %collective-permute-start.3 = (bf16[32,7296]{1,0:T(8,128)(2,1)S(1)}, bf16[32,7296]{1,0:T(8,128)(2,1)S(1)}, u32[]{:S(2)}, u32[]{:S(2)}) collective-permute-start(bf16[32,7296]{1,0:T(8,128)(2,1)S(1)} %pad_maximum_fusion), channel_id=1, source_target_pairs={{0,2},{1,3},{2,0},{3,1},{4,6},{5,7},{6,4},{7,5},{8,10},{9,11},{10,... | collective-permute-start | bytes 1400840 | tf_op jit(solution)/shard_map/ppermute | solution.py:21
  20.4 11.7 %collective-permute-start.4 = (bf16[32,7296]{1,0:T(8,128)(2,1)S(1)}, bf16[32,7296]{1,0:T(8,128)(2,1)S(1)}, u32[]{:S(2)}, u32[]{:S(2)}) collective-permute-start(bf16[32,7296]{1,0:T(8,128)(2,1)S(1)} %pad_maximum_fusion), channel_id=1, source_target_pairs={{0,4},{1,5},{2,6},{3,7},{4,0},{5,1},{6,2},{7,3},{8,12},{9,13},{10,... | collective-permute-start | bytes 1400840 | tf_op jit(solution)/shard_map/ppermute | solution.py:21
  29.1 6.1 %collective-permute-start.5 = (bf16[16,7168]{1,0:T(8,128)(2,1)S(1)}, bf16[16,7168]{1,0:T(8,128)(2,1)S(1)}, u32[]{:S(2)}, u32[]{:S(2)}) collective-permute-start(bf16[16,7168]{1,0:T(8,128)(2,1)S(1)} %slice.102), channel_id=1, source_target_pairs={{0,4},{1,5},{2,6},{3,7},{4,0},{5,1},{6,2},{7,3},{8,12},{9,13},{10,... | collective-permute-start | bytes 688136 | tf_op jit(solution)/shard_map/ppermute | solution.py:21
  32.1 6.8 %copy-start.1 = (bf16[32,7296]{1,0:T(8,128)(2,1)}, bf16[32,7296]{1,0:T(8,128)(2,1)S(1)}, u32[]{:S(2)}) copy-start(bf16[32,7296]{1,0:T(8,128)(2,1)S(1)} %collective-permute-done.4) | copy-start | bytes 1400836
  32.2 6.1 %collective-permute-start.6 = (bf16[16,7168]{1,0:T(8,128)(2,1)S(1)}, bf16[16,7168]{1,0:T(8,128)(2,1)S(1)}, u32[]{:S(2)}, u32[]{:S(2)}) collective-permute-start(bf16[16,7168]{1,0:T(8,128)(2,1)S(1)} %slice.103), channel_id=1, source_target_pairs={{0,2},{1,3},{2,0},{3,1},{4,6},{5,7},{6,4},{7,5},{8,10},{9,11},{10,... | collective-permute-start | bytes 688136 | tf_op jit(solution)/shard_map/ppermute | solution.py:21
  40.7 4.0 %collective-permute-start.7 = (bf16[128,7168]{1,0:T(8,128)(2,1)}, bf16[128,7168]{1,0:T(8,128)(2,1)S(1)}, u32[]{:S(2)}, u32[]{:S(2)}) collective-permute-start(bf16[128,7168]{1,0:T(8,128)(2,1)} %get-tuple-element.27), channel_id=1, source_target_pairs={{0,1},{1,0},{2,3},{3,2},{4,5},{5,4},{6,7},{7,6},{8,9},{9,8},{10,11... | collective-permute-start | bytes 5505032 | tf_op jit(solution)/shard_map/ppermute | solution.py:21
  40.7 5.3 %copy-start.8 = (bf16[7168,256]{1,0:T(8,128)(2,1)S(1)}, bf16[7168,256]{1,0:T(8,128)(2,1)}, u32[]{:S(2)}) copy-start(bf16[7168,256]{1,0:T(8,128)(2,1)} %param.13) | copy-start | bytes 11010052
  53.0 4.0 %collective-permute-start.8 = (bf16[128,7168]{1,0:T(8,128)(2,1)S(1)}, bf16[128,7168]{1,0:T(8,128)(2,1)}, u32[]{:S(2)}, u32[]{:S(2)}) collective-permute-start(bf16[128,7168]{1,0:T(8,128)(2,1)S(1)} %convolution_convert_fusion.1), channel_id=1, source_target_pairs={{0,1},{1,0},{2,3},{3,2},{4,5},{5,4},{6,7},{7,6},{8,9},{9,8},{10,11... | collective-permute-start | bytes 5505032 | tf_op jit(solution)/shard_map/ppermute | solution.py:21
  61.2 8.7 %collective-permute-start.11 = (bf16[16,7168]{1,0:T(8,128)(2,1)}, bf16[16,7168]{1,0:T(8,128)(2,1)}, u32[]{:S(2)}, u32[]{:S(2)}) collective-permute-start(bf16[16,7168]{1,0:T(8,128)(2,1)} %get-tuple-element.14), channel_id=1, source_target_pairs={{0,2},{1,3},{2,0},{3,1},{4,6},{5,7},{6,4},{7,5},{8,10},{9,11},{10,... | collective-permute-start | bytes 688136 | tf_op jit(solution)/shard_map/ppermute | solution.py:21
  61.5 8.3 %collective-permute-start.9 = (bf16[16,7168]{1,0:T(8,128)(2,1)}, bf16[16,7168]{1,0:T(8,128)(2,1)}, u32[]{:S(2)}, u32[]{:S(2)}) collective-permute-start(bf16[16,7168]{1,0:T(8,128)(2,1)} %get-tuple-element.15), channel_id=1, source_target_pairs={{0,4},{1,5},{2,6},{3,7},{4,0},{5,1},{6,2},{7,3},{8,12},{9,13},{10,... | collective-permute-start | bytes 688136 | tf_op jit(solution)/shard_map/ppermute | solution.py:21
  63.1 7.9 %copy-start.2 = (bf16[16,7168]{1,0:T(8,128)(2,1)S(1)}, bf16[16,7168]{1,0:T(8,128)(2,1)}, u32[]{:S(2)}) copy-start(bf16[16,7168]{1,0:T(8,128)(2,1)} %get-tuple-element.12) | copy-start | bytes 688132
  63.1 12.3 %copy-start.5 = (f32[8,2]{0,1:T(2,128)S(1)}, f32[8,2]{0,1:T(2,128)}, u32[]{:S(2)}) copy-start(f32[8,2]{0,1:T(2,128)} %param.12) | copy-start | bytes 196
  63.1 12.3 %copy-start.6 = (s32[8,2]{0,1:T(2,128)S(1)}, s32[8,2]{0,1:T(2,128)}, u32[]{:S(2)}) copy-start(s32[8,2]{0,1:T(2,128)} %param.11) | copy-start | bytes 196
  64.4 27.7 %all-to-all-start = ((bf16[8,2,27648]{2,1,0:T(2,128)(2,1)}), bf16[8,2,27648]{2,1,0:T(2,128)(2,1)}, u32[]{:S(2)}, u32[]{:S(2)}) async-start(bf16[8,2,27648]{2,1,0:T(2,128)(2,1)} %all_to_all.8), calls=%async_computation | async-start | bytes 1769472 | tf_op jit(solution)/shard_map/all_to_all | solution.py:82
  71.8 29.3 %copy-start.10 = (bf16[8,576]{1,0:T(8,128)(2,1)S(1)}, bf16[8,576]{1,0:T(8,128)(2,1)}, u32[]{:S(2)}) copy-start(bf16[8,576]{1,0:T(8,128)(2,1)} %param.17) | copy-start | bytes 27652
  71.8 23.6 %collective-permute-start.10 = (bf16[32,7168]{1,0:T(8,128)(2,1)}, bf16[32,7168]{1,0:T(8,128)(2,1)}, u32[]{:S(2)}, u32[]{:S(2)}) collective-permute-start(bf16[32,7168]{1,0:T(8,128)(2,1)} %pad_maximum_fusion.1), channel_id=1, source_target_pairs={{0,2},{1,3},{2,0},{3,1},{4,6},{5,7},{6,4},{7,5},{8,10},{9,11},{10,... | collective-permute-start | bytes 1376264 | tf_op jit(solution)/shard_map/ppermute | solution.py:21
  73.7 21.8 %collective-permute-start.12 = (bf16[32,7168]{1,0:T(8,128)(2,1)}, bf16[32,7168]{1,0:T(8,128)(2,1)S(1)}, u32[]{:S(2)}, u32[]{:S(2)}) collective-permute-start(bf16[32,7168]{1,0:T(8,128)(2,1)} %pad_maximum_fusion.2), channel_id=1, source_target_pairs={{0,4},{1,5},{2,6},{3,7},{4,0},{5,1},{6,2},{7,3},{8,12},{9,13},{10,... | collective-permute-start | bytes 1376264 | tf_op jit(solution)/shard_map/ppermute | solution.py:21
  96.7 6.9 %collective-permute-start.13 = (bf16[8,7168]{1,0:T(8,128)(2,1)S(1)}, bf16[8,7168]{1,0:T(8,128)(2,1)S(1)}, u32[]{:S(2)}, u32[]{:S(2)}) collective-permute-start(bf16[8,7168]{1,0:T(8,128)(2,1)S(1)} %get-tuple-element.24), channel_id=1, source_target_pairs={{0,8},{1,9},{2,10},{3,11},{4,12},{5,13},{6,14},{7,15},{8,0},{9,1},... | collective-permute-start | bytes 344072 | tf_op jit(solution)/shard_map/ppermute | solution.py:21
  96.7 10.6 %collective-permute-start.14 = (bf16[8,7168]{1,0:T(8,128)(2,1)S(1)}, bf16[8,7168]{1,0:T(8,128)(2,1)S(1)}, u32[]{:S(2)}, u32[]{:S(2)}) collective-permute-start(bf16[8,7168]{1,0:T(8,128)(2,1)S(1)} %get-tuple-element.26), channel_id=1, source_target_pairs={{0,16},{1,17},{2,18},{3,19},{4,20},{5,21},{6,22},{7,23},{8,24},{9,... | collective-permute-start | bytes 344072 | tf_op jit(solution)/shard_map/ppermute | solution.py:21
  98.3 9.0 %collective-permute-start.15 = (bf16[8,7168]{1,0:T(8,128)(2,1)S(1)}, bf16[8,7168]{1,0:T(8,128)(2,1)S(1)}, u32[]{:S(2)}, u32[]{:S(2)}) collective-permute-start(bf16[8,7168]{1,0:T(8,128)(2,1)S(1)} %get-tuple-element.25), channel_id=1, source_target_pairs={{0,24},{1,25},{2,26},{3,27},{4,28},{5,29},{6,30},{7,31},{8,16},{9,... | collective-permute-start | bytes 344072 | tf_op jit(solution)/shard_map/ppermute | solution.py:21
  (4 other events, 11.5 us)

commit v2 on v0

--- a/solution.py
+++ b/solution.py
@@ -1,6 +1,8 @@
 import jax
 import jax.numpy as jnp
 from jax import lax
+from jax.experimental import pallas as pl
+from jax.experimental.pallas import tpu as pltpu
 from jax.sharding import PartitionSpec as P
 
 D = 7168
@@ -8,11 +10,361 @@
 BEAMS = 8
 SPLIT = 8
 CAP = 2
+CORE, X, Y = 1, 2, 4
+LANES = 128
+STEPS = 4
+MIB = 1024 * 1024
 
 
 def passed_along(value, axis, by):
     peers = lax.axis_size(axis)
     return lax.ppermute(value, axis, [(i, (i + by) % peers) for i in range(peers)])
+
+
+def swapped(value, mask):
+    peers = lax.axis_size("ep")
+    return lax.ppermute(value, "ep", [(i, i ^ mask) for i in range(peers)])
+
+
+def dot32(a, b):
+    return jnp.dot(a, b, preferred_element_type=jnp.float32)
+
+
+def in_vmem(value):
+    return pltpu.with_memory_space_constraint(value, pltpu.VMEM)
+
+
+def in_hbm(value):
+    return pltpu.with_memory_space_constraint(value, pltpu.HBM)
+
+
+def whole_call(body, ins, outs, limit=4, scratch=(), flops=0):
+    whole = pl.BlockSpec(memory_space=pltpu.VMEM)
+    far = pl.BlockSpec(memory_space=pltpu.HBM)
+    arrays = [a[0] if isinstance(a, tuple) else a for a in ins]
+    moved = sum(a.size * a.dtype.itemsize for a in arrays)
+    return pl.pallas_call(
+        body,
+        in_specs=[far if isinstance(a, tuple) else whole for a in ins],
+        out_specs=[whole] * len(outs),
+        out_shape=[pltpu.VMEM(shape, dtype) for shape, dtype in outs],
+        scratch_shapes=list(scratch),
+        compiler_params=pltpu.CompilerParams(vmem_limit_bytes=limit * MIB),
+        cost_estimate=pl.CostEstimate(flops=flops, bytes_accessed=moved, transcendentals=0),
+    )(*[in_hbm(a[0]) if isinstance(a, tuple) else in_vmem(a) for a in ins])
+
+
+def tailed_kernel(parents, lengths, rows, out):
+    d = rows.shape[1]
+    shape = (rows.shape[0], LANES)
+    row = lax.broadcasted_iota(jnp.int32, shape, 0)
+    lane = lax.broadcasted_iota(jnp.int32, shape, 1)
+    tail = jnp.zeros(shape, jnp.int32)
+    for i in range(shape[0]):
+        tail = jnp.where((row == i) & (lane == 0), parents[i], tail)
+        tail = jnp.where((row == i) & (lane == 1), lengths[i], tail)
+    out[:, :d] = rows[...]
+    out[:, d:] = tail.astype(jnp.float32).astype(out.dtype)
+
+
+def tailed(rows, parents, lengths):
+    count, d = rows.shape
+    scalars = pl.BlockSpec(memory_space=pltpu.SMEM)
+    whole = pl.BlockSpec(memory_space=pltpu.VMEM)
+    return pl.pallas_call(
+        tailed_kernel,
+        in_specs=[scalars, scalars, whole],
+        out_specs=whole,
+        out_shape=pltpu.VMEM((count, d + LANES), rows.dtype),
+        compiler_params=pltpu.CompilerParams(vmem_limit_bytes=2 * MIB),
+        cost_estimate=pl.CostEstimate(flops=0, bytes_accessed=4 * count * d, transcendentals=0),
+    )(parents, lengths, rows)
+
+
+def stack_kernel(*refs):
+    ins, out = refs[:-1], refs[-1]
+    out[...] = jnp.concatenate([r[...].astype(jnp.float32) for r in ins], axis=0).astype(out.dtype)
+
+
+def stacked(pieces):
+    rows = sum(p.shape[0] for p in pieces)
+    return whole_call(stack_kernel, pieces, [((rows, pieces[0].shape[1]), pieces[0].dtype)])[0]
+
+
+def expert_math(rows, weights, near, far, gate_sum, up_sum, act):
+    own, from_x, from_y, left, right = rows
+    d = near.shape[1]
+    chunk = d // STEPS
+    half = left.shape[1]
+    cuts = [slice(step * chunk, (step + 1) * chunk) for step in range(STEPS)]
+    hid = gate_sum.shape[1] // len(weights)
+    for core, (w_gate, w_up, _, ready) in enumerate(weights):
+        units = slice(core * hid, (core + 1) * hid)
+        for step, cut in enumerate(cuts):
+            ready(step)
+            corner = left[:, cut] if cut.stop <= half else right[:, cut.start - half : cut.stop - half]
+            block = jnp.concatenate([own[:, cut], from_x[:, cut], from_y[:, cut], corner], axis=0)
+            gate, up = dot32(block, w_gate[cut, :]), dot32(block, w_up[cut, :])
+            if step:
+                gate, up = gate_sum[:, units] + gate, up_sum[:, units] + up
+            if step < STEPS - 1:
+                gate_sum[:, units] = gate
+                up_sum[:, units] = up
+            else:
+                act[:, units] = (gate / (1.0 + jnp.exp(-gate)) * up).astype(act.dtype)
+    for _, _, _, ready in weights:
+        ready(STEPS)
+    rest = near.shape[0]
+    for cut in cuts:
+        part = sum(
+            dot32(act[:, core * hid : (core + 1) * hid], w_down[:, cut])
+            for core, (_, _, w_down, _) in enumerate(weights)
+        ).astype(near.dtype)
+        near[:, cut] = part[:rest]
+        far[:, cut] = part[rest:]
+
+
+def first_kernel(*refs):
+    rows, sources, other = refs[:5], refs[5:8], refs[8:11]
+    near, far = refs[11:13]
+    held = refs[13:16]
+    gate_sum, up_sum, act, sems = refs[16:]
+    d = held[0].shape[0]
+    chunk = d // STEPS
+    steps = []
+    for step in range(STEPS):
+        cut = slice(step * chunk, (step + 1) * chunk)
+        steps.append(
+            [
+                pltpu.make_async_copy(sources[i].at[cut, :], held[i].at[cut, :], sems.at[i, step])
+                for i in range(2)
+            ]
+        )
+    steps.append([pltpu.make_async_copy(sources[2], held[2], sems.at[2, 0])])
+    for copies in steps:
+        for copy in copies:
+            copy.start()
+
+    def ready(step):
+        for copy in steps[step]:
+            copy.wait()
+
+    weights = [tuple(other) + (lambda step: None,), tuple(held) + (ready,)]
+    expert_math(rows, weights, near, far, gate_sum, up_sum, act)
+
+
+def second_kernel(*refs):
+    rows, held, other = refs[:5], refs[5:8], refs[8:11]
+    near, far, gate_sum, up_sum, act = refs[11:]
+    weights = [tuple(w) + (lambda step: None,) for w in (other, held)]
+    expert_math(rows, weights, near, far, gate_sum, up_sum, act)
+
+
+def expert_outputs(rows, weights, other, first):
+    quad = rows[0].shape[0]
+    d, hid = weights[0].shape
+    bf16, f32 = jnp.bfloat16, jnp.float32
+    outs = [((3 * quad, d), bf16), ((quad, d), bf16)]
+    scratch = [
+        pltpu.VMEM((4 * quad, 2 * hid), f32),
+        pltpu.VMEM((4 * quad, 2 * hid), f32),
+        pltpu.VMEM((4 * quad, 2 * hid), bf16),
+    ]
+    flops = 2 * 4 * quad * d * 2 * hid * 3
+    if first:
+        outs = outs + [(w.shape, w.dtype) for w in weights]
+        scratch.append(pltpu.SemaphoreType.DMA((3, STEPS)))
+        ins = rows + [(w,) for w in weights] + other
+        near, far, *held = whole_call(first_kernel, ins, outs, 8, scratch, flops)
+        return near, far, held
+    near, far = whole_call(second_kernel, rows + weights + other, outs, 8, scratch, flops)
+    return near, far, weights
+
+
+def join_kernel(near, got_a, got_b, mine, for_x, for_y):
+    f32 = jnp.float32
+    q = mine.shape[0]
+    half = got_a.shape[1]
+    mine[...] = near[:q, :]
+    for_x[:, :half] = near[q : 2 * q, :half]
+    for_x[:, half:] = (near[q : 2 * q, half:].astype(f32) + got_b[...].astype(f32)).astype(for_x.dtype)
+    for_y[:, :half] = (near[2 * q :, :half].astype(f32) + got_a[...].astype(f32)).astype(for_y.dtype)
+    for_y[:, half:] = near[2 * q :, half:]
+
+
+def total_kernel(mine, back_x, back_y, *outs):
+    f32 = jnp.float32
+    total = mine[...].astype(f32) + back_x[...].astype(f32) + back_y[...].astype(f32)
+    rows = outs[0].shape[0]
+    for i, out in enumerate(outs):
+        out[...] = total[i * rows : (i + 1) * rows].astype(out.dtype)
+
+
+def read_facts(pieces, facts, scalars, sem):
+    quad = pieces[0].shape[0]
+    d = pieces[0].shape[1] - LANES
+    for i, piece in enumerate(pieces):
+        facts[i * quad : (i + 1) * quad, :] = piece[:, d:].astype(jnp.float32).astype(jnp.int32)
+    copy = pltpu.make_async_copy(facts, scalars, sem)
+    copy.start()
+    copy.wait()
+
+
+def fact_row(place, quad, rows):
+    planes = quad // rows
+    plane, side = place // 2, place % 2
+    return ((plane // planes) * 2 + side) * quad + (plane % planes) * rows
+
+
+def packing_kernel(who, own_a, y_a, own_b, y_b, cache, out, facts, scalars, sem):
+    read_facts([own_a, y_a, own_b, y_b], facts, scalars, sem)
+    rows = cache.shape[0]
+    for place in range(BEAMS):
+        at = fact_row(place, own_a.shape[0], rows)
+        first = second = count = jnp.int32(0)
+        for row in range(rows):
+            hit = scalars[at + row, 0] == who[0]
+            first = jnp.where(hit & (count == 0), row, first)
+            second = jnp.where(hit & (count == 1), row, second)
+            count = count + hit.astype(jnp.int32)
+        for rank, pick in enumerate((first, second)):
+            out[who[0] ^ place, rank] = cache[pick]
+
+
+def unpacking_kernel(quad, who, facts, newest, arrived, out, scalars, sem):
+    copy = pltpu.make_async_copy(facts, scalars, sem)
+    copy.start()
+    copy.wait()
+    rows, tokens, width = out.shape
+    planes = quad // rows
+    for row in range(rows):
+        parent = scalars[row, 0]
+        rank = sum([(scalars[other, 0] == parent).astype(jnp.int32) for other in range(row)], jnp.int32(0))
+        place = parent ^ who[0]
+        plane, side = place // 2, place % 2
+        at = ((plane // planes) * 2 + side) * quad + (plane % planes) * rows + row
+        bound = scalars[at, 1]
+        token = lax.broadcasted_iota(jnp.int32, (tokens, width), 0)
+        old = arrived[parent, jnp.minimum(rank, CAP - 1)].astype(jnp.float32)
+        value = jnp.where(token < bound, old, jnp.where(token == bound, newest[row], 0.0))
+        out[row] = value.astype(out.dtype)
+
+
+def packing_call(who, blocks, cache):
+    whole = pl.BlockSpec(memory_space=pltpu.VMEM)
+    table = (len(blocks) * blocks[0].shape[0], LANES)
+    return pl.pallas_call(
+        packing_kernel,
+        in_specs=[pl.BlockSpec(memory_space=pltpu.SMEM)] + [whole] * (len(blocks) + 1),
+        out_specs=[whole] * 2,
+        out_shape=[
+            jax.ShapeDtypeStruct((BEAMS, CAP) + cache.shape[1:], cache.dtype),
+            pltpu.VMEM(table, jnp.int32),
+        ],
+        scratch_shapes=[pltpu.SMEM(table, jnp.int32), pltpu.SemaphoreType.DMA],
+        compiler_params=pltpu.CompilerParams(vmem_limit_bytes=4 * MIB),
+        cost_estimate=pl.CostEstimate(flops=0, bytes_accessed=4 * cache.size, transcendentals=0),
+    )(who, *[in_vmem(b) for b in blocks], in_vmem(cache))
+
+
+def unpacking_call(who, facts, quad, newest, arrived, shape):
+    whole = pl.BlockSpec(memory_space=pltpu.VMEM)
+    return pl.pallas_call(
+        lambda *refs: unpacking_kernel(quad, *refs),
+        in_specs=[pl.BlockSpec(memory_space=pltpu.SMEM)] + [whole] * 3,
+        out_specs=whole,
+        out_shape=shape,
+        scratch_shapes=[pltpu.SMEM(facts.shape, jnp.int32), pltpu.SemaphoreType.DMA],
+        compiler_params=pltpu.CompilerParams(vmem_limit_bytes=6 * MIB),
+        cost_estimate=pl.CostEstimate(
+            flops=0, bytes_accessed=4 * newest.size * shape.shape[1], transcendentals=0
+        ),
+    )(who, facts, newest, arrived)
+
+
+def tied(*values):
+    return lax.optimization_barrier(values)
+
+
+def dense_local(
+    hidden_rows,
+    expert_ids,
+    gate_weights,
+    w_gate,
+    w_up,
+    w_down,
+    latent_cache,
+    new_latent,
+    parents,
+    lengths,
+):
+    device_count = lax.axis_size("ep")
+    device_index = lax.axis_index("ep")
+    experts = device_count // SPLIT
+    rows, d = hidden_rows.shape
+    half = d // 2
+    beam_stride = device_count // BEAMS
+    own_beam = device_index // beam_stride
+    own_expert = device_index // SPLIT
+    bf16 = jnp.bfloat16
+    f32 = jnp.float32
+    middle = experts // 2
+    who = own_beam.reshape(1)
+
+    other = [swapped(w_gate, CORE), swapped(w_up, CORE)]
+    carried = tailed(hidden_rows, parents.reshape(rows), lengths)
+    planes = [carried] + [swapped(carried, SPLIT * k) for k in range(1, experts)]
+    own_a = stacked(planes[:middle])
+    x_a, y_a = swapped(own_a, X), swapped(own_a, Y)
+    x_a, y_a, planes[2], planes[3], w_down_out, *other[:2] = tied(x_a, y_a, planes[2], planes[3], w_down, *other[:2])
+    other.append(swapped(w_down_out, CORE))
+    rows_a = [own_a, x_a, y_a, swapped(x_a[:, :half], Y), swapped(y_a[:, half:d], X)]
+    own_b = stacked(planes[middle:])
+    x_b, y_b = swapped(own_b, X), swapped(own_b, Y)
+    packets, facts = packing_call(who, [own_a, y_a, own_b, y_b], latent_cache)
+    rows_b = [own_b, x_b, y_b, swapped(x_b[:, :half], Y), swapped(y_b[:, half:d], X)]
+    groups = [[b * beam_stride + r for b in range(BEAMS)] for r in range(beam_stride)]
+    arrived = lax.all_to_all(
+        packets, "ep", split_axis=0, concat_axis=0, axis_index_groups=groups, tiled=True
+    )
+
+    near_a, far_a, held = expert_outputs(rows_a, [w_gate, w_up, w_down], other, True)
+    near_b, far_b, _ = expert_outputs(rows_b, held, other, False)
+
+
+    def joined(near, far):
+        quad = far.shape[0]
+        got_a, got_b = swapped(far[:, :half], X), swapped(far[:, half:], Y)
+        return whole_call(join_kernel, [near, got_a, got_b], [((quad, d), bf16)] * 3)
+
+    def totals(mine, for_x, for_y, count):
+        return whole_call(
+            total_kernel, [mine, swapped(for_x, X), swapped(for_y, Y)], [((rows, d), bf16)] * count
+        )
+    mine_b, to_x_b, to_y_b = joined(near_b, far_b)
+    far_a, to_x_b, to_y_b = tied(far_a, to_x_b, to_y_b)
+    sums_b = totals(mine_b, to_x_b, to_y_b, experts - middle)
+    mine_a, to_x_a, to_y_a = joined(near_a, far_a)
+    sums_a = totals(mine_a, to_x_a, to_y_a, middle)
+    moe = None
+    for k, piece in enumerate(list(sums_a) + list(sums_b)):
+        if k:
+            piece = swapped(piece, SPLIT * k)
+        weight = jnp.sum(
+            jnp.where(expert_ids == (own_expert ^ k), gate_weights, 0.0), axis=1, keepdims=True
+        )
+        term = weight * piece.astype(f32)
+        moe = term if moe is None else moe + term
+    moe_out = moe.astype(bf16)
+    new_cache = unpacking_call(
+        who,
+        facts,
+        own_a.shape[0],
+        new_latent.astype(f32)[:, None, :],
+        arrived,
+        jax.ShapeDtypeStruct(latent_cache.shape, bf16),
+    )
+    return (moe_out, new_cache)
 
 
 def local(
@@ -35,6 +387,19 @@
     local_rows = hidden_rows.shape[0]
     experts = device_count // SPLIT
     capacity = max(2, min(local_rows, (2 * local_rows * TOP + experts - 1) // experts))
+    if capacity == local_rows and experts & (experts - 1) == 0 and beam_stride * 2 == SPLIT:
+        return dense_local(
+            hidden_rows,
+            expert_ids,
+            gate_weights,
+            w_gate,
+            w_up,
+            w_down,
+            latent_cache,
+            new_latent,
+            parents,
+            lengths,
+        )
     expert_range = jnp.arange(experts, dtype=jnp.int32)
     chosen = expert_ids[:, :, None] == expert_range[None, None, :]
     hit_count = jnp.sum(chosen.astype(jnp.int32), axis=1)

time: 245 us -> 92.4 us (0.38)
  blocking collectives: 102 us -> 0 us
  waiting for transfers between devices: 81.6 us -> 20.5 us
  Pallas kernels: 0 us -> 20.1 us
  matrix products: 17 us -> 0 us
  starting transfers between devices: 27.4 us -> 38.6 us
  other arithmetic: 9.43 us -> 0.83 us
  local copies, waits for them, and re-layouts: 5.64 us -> 11 us
    unnamed x1 -> x0, blocking collectives: 102 us -> none
    all_to_all x2 -> x1, waiting for transfers between devices: 80.6 us -> 0.01 us  [dense_local(): lax.all_to_all(packets, 'ep', split_axis=0, concat_axis=0, axis_index_gro...]
    ppermute x7 -> x25, starting transfers between devices: 10.9 us -> 34.9 us  [swapped(): return lax.ppermute(value, 'ep', [(i, i ^ mask) for i in range(peers)])]
    pallas_call x0 -> x11, Pallas kernels: none -> 20.1 us  [the longest x8 15.3 us: whole_call(): pl.pallas_call(body, in_specs=[far if isinstance(a, tuple) else whole for...]
    ppermute x7 -> x25, waiting for transfers between devices: 0.99 us -> 20.5 us  [swapped(): return lax.ppermute(value, 'ep', [(i, i ^ mask) for i in range(peers)])]
    dot_general x12 -> x0, matrix products: 17 us -> none  [the longest x1 10 us: local(): jnp.dot(activated, w_down, preferred_element_type=jnp.float32)]
    all_to_all x2 -> x1, starting transfers between devices: 16.5 us -> 3.76 us  [dense_local(): lax.all_to_all(packets, 'ep', split_axis=0, concat_axis=0, axis_index_gro...]
    unnamed x25 -> x26, local copies, waits for them, and re-layouts: 1.05 us -> 10.9 us
  transfers between devices with their start and end apart: 9 -> 26, of which waited for: 2 -> 10; matrix products, arithmetic and copies ran while one was open for 10% -> 0% of each run, Pallas kernels for 0% -> 22%
where the time goes in v2:
time: 92.4 us; the launch traced here: 92 us
  starting transfers between devices  38.6 us (42%)
  waiting for transfers between devices  20.5 us (22%)
  Pallas kernels  20.1 us (22%)
  local copies, waits for them, and re-layouts  11 us (12%)
    ppermute x25, starting transfers between devices, swapped(): return lax.ppermute(value, 'ep', [(i, i ^ mask) for i in range(peers)])  34.9 us
    ppermute x25, waiting for transfers between devices, swapped(): return lax.ppermute(value, 'ep', [(i, i ^ mask) for i in range(peers)])  20.5 us
    pallas_call x8, Pallas kernels, whole_call(): pl.pallas_call(body, in_specs=[far if isinstance(a, tuple) else whole for...  15.3 us
    unnamed x26, local copies, waits for them, and re-layouts  10.9 us
    all_to_all x1, starting transfers between devices, dense_local(): lax.all_to_all(packets, 'ep', split_axis=0, concat_axis=0, axis_index_gro...  3.76 us
    pallas_call x1, Pallas kernels, packing_call(): pl.pallas_call(packing_kernel, in_specs=[pl.BlockSpec(memory_space=pltpu....  2.26 us
    pallas_call x1, Pallas kernels, unpacking_call(): pl.pallas_call(lambda *refs: unpacking_kernel(quad, *refs), in_specs=[pl....  2.03 us
  transfers between devices with their start and end apart: 26, of which 10 were waited for; matrix products, arithmetic and copies ran while one was open for 0% of the time, Pallas kernels for 22%

profile of v2, /device:TPU:0, one launch (start us, length us, event | category | flops | bytes accessed | tf_op | source)
XLA Modules:
  0.0 92.0 jit_solution(2533949189365309620)
XLA Ops:
  4.0 3.1 %collective-permute-start = (bf16[8,7296]{1,0:T(8,128)(2,1)S(1)}, bf16[8,7296]{1,0:T(8,128)(2,1)S(1)}, u32[]{:S(2)}, u32[]{:S(2)}) collective-permute-start(bf16[8,7296]{1,0:T(8,128)(2,1)S(1)} %shard_map.113.refs_0_), channel_id=1, source_target_pairs={{0,8},{1,9},{2,10},{3,11},{4,12},{5,13},{6,14},{7,15},{8,0},{9,1},... | collective-permute-start | bytes 350216 | tf_op jit(solution)/shard_map/ppermute | solution.py:26
  7.1 2.6 %collective-permute-start.3 = (bf16[8,7296]{1,0:T(8,128)(2,1)S(1)}, bf16[8,7296]{1,0:T(8,128)(2,1)S(1)}, u32[]{:S(2)}, u32[]{:S(2)}) collective-permute-start(bf16[8,7296]{1,0:T(8,128)(2,1)S(1)} %shard_map.113.refs_0_), channel_id=1, source_target_pairs={{0,16},{1,17},{2,18},{3,19},{4,20},{5,21},{6,22},{7,23},{8,24},{9,... | collective-permute-start | bytes 350216 | tf_op jit(solution)/shard_map/ppermute | solution.py:26
  9.7 2.3 %collective-permute-done.refs_1_ = bf16[8,7296]{1,0:T(8,128)(2,1)S(1)} collective-permute-done((bf16[8,7296]{1,0:T(8,128)(2,1)S(1)}, bf16[8,7296]{1,0:T(8,128)(2,1)S(1)}, u32[]{:S(2)}, u32[]{:S(2)}) %collective-permute-start) | collective-permute-done | bytes 116768 | tf_op jit(solution)/shard_map/ppermute | solution.py:26
  12.0 1.9 %collective-permute-start.1 = (bf16[16,7296]{1,0:T(8,128)(2,1)S(1)}, bf16[16,7296]{1,0:T(8,128)(2,1)S(1)}, u32[]{:S(2)}, u32[]{:S(2)}) collective-permute-start(bf16[16,7296]{1,0:T(8,128)(2,1)S(1)} %shard_map.114.refs_0_.own_a), channel_id=1, source_target_pairs={{0,2},{1,3},{2,0},{3,1},{4,6},{5,7},{6,4},{7,5},{8,10},{9,11},{10,... | collective-permute-start | bytes 700424 | tf_op jit(solution)/shard_map/ppermute | solution.py:26
  15.4 3.2 %collective-permute-start.4 = (bf16[8,7296]{1,0:T(8,128)(2,1)S(1)}, bf16[8,7296]{1,0:T(8,128)(2,1)S(1)}, u32[]{:S(2)}, u32[]{:S(2)}) collective-permute-start(bf16[8,7296]{1,0:T(8,128)(2,1)S(1)} %shard_map.113.refs_0_), channel_id=1, source_target_pairs={{0,24},{1,25},{2,26},{3,27},{4,28},{5,29},{6,30},{7,31},{8,16},{9,... | collective-permute-start | bytes 350216 | tf_op jit(solution)/shard_map/ppermute | solution.py:26
  18.6 3.4 %collective-permute-done.4.refs_1_ = bf16[8,7296]{1,0:T(8,128)(2,1)S(1)} collective-permute-done((bf16[8,7296]{1,0:T(8,128)(2,1)S(1)}, bf16[8,7296]{1,0:T(8,128)(2,1)S(1)}, u32[]{:S(2)}, u32[]{:S(2)}) %collective-permute-start.4) | collective-permute-done | bytes 116768 | tf_op jit(solution)/shard_map/ppermute | solution.py:26
  22.1 1.8 %copy-done = bf16[7168,256]{1,0:T(8,128)(2,1)} copy-done((bf16[7168,256]{1,0:T(8,128)(2,1)}, bf16[7168,256]{1,0:T(8,128)(2,1)S(1)}, u32[]{:S(2)}) %copy-start) | copy-done | bytes 3670040
  23.9 1.8 %copy-done.3 = bf16[7168,256]{1,0:T(8,128)(2,1)} copy-done((bf16[7168,256]{1,0:T(8,128)(2,1)}, bf16[7168,256]{1,0:T(8,128)(2,1)S(1)}, u32[]{:S(2)}) %copy-start.3) | copy-done | bytes 3670040
  30.0 4.3 %collective-permute-done.10.refs_1_ = bf16[16,7296]{1,0:T(8,128)(2,1)S(1)} collective-permute-done((bf16[16,7296]{1,0:T(8,128)(2,1)S(1)}, bf16[16,7296]{1,0:T(8,128)(2,1)S(1)}, u32[]{:S(2)}, u32[]{:S(2)}) %collective-permute-start.10) | collective-permute-done | bytes 233504 | tf_op jit(solution)/shard_map/ppermute | solution.py:26
  34.3 1.6 %collective-permute-start.12 = (bf16[16,3584]{1,0:T(8,128)(2,1)S(1)}, bf16[16,3584]{1,0:T(8,128)(2,1)S(1)}, u32[]{:S(2)}, u32[]{:S(2)}) collective-permute-start(bf16[16,3584]{1,0:T(8,128)(2,1)S(1)} %slice.32), channel_id=1, source_target_pairs={{0,4},{1,5},{2,6},{3,7},{4,0},{5,1},{6,2},{7,3},{8,12},{9,13},{10,... | collective-permute-start | bytes 344072 | tf_op jit(solution)/shard_map/ppermute | solution.py:26
  38.4 2.3 %shard_map.122 = (bf16[8,2,48,576]{3,2,1,0:T(8,128)(2,1)}, s32[64,128]{1,0:T(8,128)S(1)}) custom-call(s32[1]{0:T(128)} %bitcast.1.who.refs_0_, bf16[16,7296]{1,0:T(8,128)(2,1)S(1)} %shard_map.114.refs_0_.own_a, bf16[16,7296]{1,0:T(8,128)(2,1)S(1)} %collective-permute-done.2.refs_2_.y_a, bf16[16,7296]{1,0:T(8,128)(2,1)S(1)} %shard_map.116.refs_0_.own_b, ...), custom_call_target="tpu_custom_call" | custom-call | bytes 884736 | tf_op jit(solution)/shard_map/pallas_call | solution.py:256
  40.7 3.8 %all-to-all-start = ((bf16[8,2,48,576]{3,2,1,0:T(8,128)(2,1)}), bf16[8,2,48,576]{3,2,1,0:T(8,128)(2,1)S(1)}, u32[]{:S(2)}, u32[]{:S(2)}) async-start(bf16[8,2,48,576]{3,2,1,0:T(8,128)(2,1)} %get-tuple-element.59), calls=%async_computation | async-start | bytes 1966080 | tf_op jit(solution)/shard_map/all_to_all | solution.py:327
  44.5 2.0 %copy-done.1 = bf16[7168,256]{1,0:T(8,128)(2,1)S(1)} copy-done((bf16[7168,256]{1,0:T(8,128)(2,1)S(1)}, bf16[7168,256]{1,0:T(8,128)(2,1)}, u32[]{:S(2)}) %copy-start.1) | copy-done | bytes 3670040
  46.5 2.0 %copy-done.4 = bf16[7168,256]{1,0:T(8,128)(2,1)S(1)} copy-done((bf16[7168,256]{1,0:T(8,128)(2,1)S(1)}, bf16[7168,256]{1,0:T(8,128)(2,1)}, u32[]{:S(2)}) %copy-start.4) | copy-done | bytes 3670040
  48.6 8.8 %shard_map.115 = (bf16[48,7168]{1,0:T(8,128)(2,1)S(1)}, bf16[16,7168]{1,0:T(8,128)(2,1)S(1)}, bf16[7168,256]{1,0:T(8,128)(2,1)S(1)}, bf16[7168,256]{1,0:T(8,128)(2,1)S(1)}, bf16[256,7168]{1,0:T(8,128)(2,1)S(1)}) custom-call(bf16[16,7296]{1,0:T(8,128)(2,1)S(1)} %shard_map.114.refs_0_.own_a, bf16[16,7296]{1,0:T(8,128)(2,1)S(1)} %collective-permute-done.1.refs_1_, ...), custom_call_target="tpu_custom_call" | custom-call | flops 1409286144 | bytes 22949888 | tf_op jit(solution)/shard_map/pallas_call | solution.py:46
  57.4 6.1 %shard_map.117 = (bf16[48,7168]{1,0:T(8,128)(2,1)S(1)}, bf16[16,7168]{1,0:T(8,128)(2,1)S(1)}) custom-call(bf16[16,7296]{1,0:T(8,128)(2,1)S(1)} %shard_map.116.refs_0_.own_b, bf16[16,7296]{1,0:T(8,128)(2,1)S(1)} %collective-permute-done.10.refs_1_, bf16[16,7296]{1,0:T(8,128)(2,1)S(1)} %collective-permute-done.11.refs_2_.y_b, ...), custom_call_target="tpu_custom_call" | custom-call | flops 1409286144 | bytes 22949888 | tf_op jit(solution)/shard_map/pallas_call | solution.py:46
  65.1 2.0 %collective-permute-start.15 = (bf16[16,3584]{1,0:T(8,128)(2,1)S(1)}, bf16[16,3584]{1,0:T(8,128)(2,1)S(1)}, u32[]{:S(2)}, u32[]{:S(2)}) collective-permute-start(bf16[16,3584]{1,0:T(8,128)(2,1)S(1)} %get-tuple-element.66), channel_id=1, source_target_pairs={{0,4},{1,5},{2,6},{3,7},{4,0},{5,1},{6,2},{7,3},{8,12},{9,13},{10,... | collective-permute-start | bytes 344072 | tf_op jit(solution)/shard_map/ppermute | solution.py:26
  70.7 2.0 %collective-permute-start.17 = (bf16[16,3584]{1,0:T(8,128)(2,1)S(1)}, bf16[16,3584]{1,0:T(8,128)(2,1)S(1)}, u32[]{:S(2)}, u32[]{:S(2)}) collective-permute-start(bf16[16,3584]{1,0:T(8,128)(2,1)S(1)} %get-tuple-element.64), channel_id=1, source_target_pairs={{0,4},{1,5},{2,6},{3,7},{4,0},{5,1},{6,2},{7,3},{8,12},{9,13},{10,... | collective-permute-start | bytes 344072 | tf_op jit(solution)/shard_map/ppermute | solution.py:26
  74.1 1.9 %collective-permute-done.16.got_a = bf16[16,3584]{1,0:T(8,128)(2,1)S(1)} collective-permute-done((bf16[16,3584]{1,0:T(8,128)(2,1)S(1)}, bf16[16,3584]{1,0:T(8,128)(2,1)S(1)}, u32[]{:S(2)}, u32[]{:S(2)}) %collective-permute-start.16) | collective-permute-done | bytes 114720 | tf_op jit(solution)/shard_map/ppermute | solution.py:26
  79.3 1.9 %collective-permute-done.21.back_x = bf16[16,7168]{1,0:T(8,128)(2,1)S(1)} collective-permute-done((bf16[16,7168]{1,0:T(8,128)(2,1)S(1)}, bf16[16,7168]{1,0:T(8,128)(2,1)S(1)}, u32[]{:S(2)}, u32[]{:S(2)}) %collective-permute-start.21) | collective-permute-done | bytes 229408 | tf_op jit(solution)/shard_map/ppermute | solution.py:26
  82.1 2.5 %collective-permute-start.24 = (bf16[8,7168]{1,0:T(8,128)(2,1)S(1)}, bf16[8,7168]{1,0:T(8,128)(2,1)S(1)}, u32[]{:S(2)}, u32[]{:S(2)}) collective-permute-start(bf16[8,7168]{1,0:T(8,128)(2,1)S(1)} %get-tuple-element.57), channel_id=1, source_target_pairs={{0,24},{1,25},{2,26},{3,27},{4,28},{5,29},{6,30},{7,31},{8,16},{9,... | collective-permute-start | bytes 344072 | tf_op jit(solution)/shard_map/ppermute | solution.py:26
  84.7 2.0 %collective-permute-start.20 = (bf16[8,7168]{1,0:T(8,128)(2,1)S(1)}, bf16[8,7168]{1,0:T(8,128)(2,1)S(1)}, u32[]{:S(2)}, u32[]{:S(2)}) collective-permute-start(bf16[8,7168]{1,0:T(8,128)(2,1)S(1)} %get-tuple-element.52), channel_id=1, source_target_pairs={{0,8},{1,9},{2,10},{3,11},{4,12},{5,13},{6,14},{7,15},{8,0},{9,1},... | collective-permute-start | bytes 344072 | tf_op jit(solution)/shard_map/ppermute | solution.py:26
  86.8 2.0 %shard_map.123 = bf16[8,48,576]{2,1,0:T(8,128)(2,1)} custom-call(s32[1]{0:T(128)} %bitcast.1.who.refs_0_, s32[64,128]{1,0:T(8,128)S(1)} %get-tuple-element.58.refs_1_, f32[8,1,576]{2,1,0:T(1,128)S(1)} %reshape.16.refs_2_, bf16[8,2,48,576]{3,2,1,0:T(8,128)(2,1)S(1)} %all-to-all-done.refs_3_), custom_call_target="tpu_custom_call" | custom-call | bytes 884736 | tf_op jit(solution)/shard_map/pallas_call | solution.py:272
  88.8 2.4 %collective-permute-done.23 = bf16[8,7168]{1,0:T(8,128)(2,1)S(1)} collective-permute-done((bf16[8,7168]{1,0:T(8,128)(2,1)S(1)}, bf16[8,7168]{1,0:T(8,128)(2,1)S(1)}, u32[]{:S(2)}, u32[]{:S(2)}) %collective-permute-start.23) | collective-permute-done | bytes 114720 | tf_op jit(solution)/shard_map/ppermute | solution.py:26
  (74 shorter events, 23.4 us)
Async XLA Ops:
  0.6 21.4 %collective-permute-start.5 = (bf16[7168,256]{1,0:T(8,128)(2,1)}, bf16[7168,256]{1,0:T(8,128)(2,1)S(1)}, u32[]{:S(2)}, u32[]{:S(2)}) collective-permute-start(bf16[7168,256]{1,0:T(8,128)(2,1)} %refs_5_.1), channel_id=1, source_target_pairs={{0,1},{1,0},{2,3},{3,2},{4,5},{5,4},{6,7},{7,6},{8,9},{9,8},{10,11... | collective-permute-start | bytes 11010056 | tf_op jit(solution)/shard_map/ppermute | solution.py:26
  1.1 22.7 %collective-permute-start.6 = (bf16[7168,256]{1,0:T(8,128)(2,1)}, bf16[7168,256]{1,0:T(8,128)(2,1)S(1)}, u32[]{:S(2)}, u32[]{:S(2)}) collective-permute-start(bf16[7168,256]{1,0:T(8,128)(2,1)} %refs_6_.1), channel_id=1, source_target_pairs={{0,1},{1,0},{2,3},{3,2},{4,5},{5,4},{6,7},{7,6},{8,9},{9,8},{10,11... | collective-permute-start | bytes 11010056 | tf_op jit(solution)/shard_map/ppermute | solution.py:26
  4.0 8.0 %collective-permute-start = (bf16[8,7296]{1,0:T(8,128)(2,1)S(1)}, bf16[8,7296]{1,0:T(8,128)(2,1)S(1)}, u32[]{:S(2)}, u32[]{:S(2)}) collective-permute-start(bf16[8,7296]{1,0:T(8,128)(2,1)S(1)} %shard_map.113.refs_0_), channel_id=1, source_target_pairs={{0,8},{1,9},{2,10},{3,11},{4,12},{5,13},{6,14},{7,15},{8,0},{9,1},... | collective-permute-start | bytes 350216 | tf_op jit(solution)/shard_map/ppermute | solution.py:26
  7.1 8.4 %collective-permute-start.3 = (bf16[8,7296]{1,0:T(8,128)(2,1)S(1)}, bf16[8,7296]{1,0:T(8,128)(2,1)S(1)}, u32[]{:S(2)}, u32[]{:S(2)}) collective-permute-start(bf16[8,7296]{1,0:T(8,128)(2,1)S(1)} %shard_map.113.refs_0_), channel_id=1, source_target_pairs={{0,16},{1,17},{2,18},{3,19},{4,20},{5,21},{6,22},{7,23},{8,24},{9,... | collective-permute-start | bytes 350216 | tf_op jit(solution)/shard_map/ppermute | solution.py:26
  12.0 10.0 %collective-permute-start.1 = (bf16[16,7296]{1,0:T(8,128)(2,1)S(1)}, bf16[16,7296]{1,0:T(8,128)(2,1)S(1)}, u32[]{:S(2)}, u32[]{:S(2)}) collective-permute-start(bf16[16,7296]{1,0:T(8,128)(2,1)S(1)} %shard_map.114.refs_0_.own_a), channel_id=1, source_target_pairs={{0,2},{1,3},{2,0},{3,1},{4,6},{5,7},{6,4},{7,5},{8,10},{9,11},{10,... | collective-permute-start | bytes 700424 | tf_op jit(solution)/shard_map/ppermute | solution.py:26
  13.9 8.1 %collective-permute-start.2 = (bf16[16,7296]{1,0:T(8,128)(2,1)S(1)}, bf16[16,7296]{1,0:T(8,128)(2,1)S(1)}, u32[]{:S(2)}, u32[]{:S(2)}) collective-permute-start(bf16[16,7296]{1,0:T(8,128)(2,1)S(1)} %shard_map.114.refs_0_.own_a), channel_id=1, source_target_pairs={{0,4},{1,5},{2,6},{3,7},{4,0},{5,1},{6,2},{7,3},{8,12},{9,13},{10,... | collective-permute-start | bytes 700424 | tf_op jit(solution)/shard_map/ppermute | solution.py:26
  15.4 6.6 %collective-permute-start.4 = (bf16[8,7296]{1,0:T(8,128)(2,1)S(1)}, bf16[8,7296]{1,0:T(8,128)(2,1)S(1)}, u32[]{:S(2)}, u32[]{:S(2)}) collective-permute-start(bf16[8,7296]{1,0:T(8,128)(2,1)S(1)} %shard_map.113.refs_0_), channel_id=1, source_target_pairs={{0,24},{1,25},{2,26},{3,27},{4,28},{5,29},{6,30},{7,31},{8,16},{9,... | collective-permute-start | bytes 350216 | tf_op jit(solution)/shard_map/ppermute | solution.py:26
  25.7 18.8 %collective-permute-start.9 = (bf16[256,7168]{1,0:T(8,128)(2,1)}, bf16[256,7168]{1,0:T(8,128)(2,1)}, u32[]{:S(2)}, u32[]{:S(2)}) collective-permute-start(bf16[256,7168]{1,0:T(8,128)(2,1)} %refs_7_.1), channel_id=1, source_target_pairs={{0,1},{1,0},{2,3},{3,2},{4,5},{5,4},{6,7},{7,6},{8,9},{9,8},{10,11... | collective-permute-start | bytes 11010056 | tf_op jit(solution)/shard_map/ppermute | solution.py:26
  25.7 8.6 %collective-permute-start.10 = (bf16[16,7296]{1,0:T(8,128)(2,1)S(1)}, bf16[16,7296]{1,0:T(8,128)(2,1)S(1)}, u32[]{:S(2)}, u32[]{:S(2)}) collective-permute-start(bf16[16,7296]{1,0:T(8,128)(2,1)S(1)} %shard_map.116.refs_0_.own_b), channel_id=1, source_target_pairs={{0,2},{1,3},{2,0},{3,1},{4,6},{5,7},{6,4},{7,5},{8,10},{9,11},{10,... | collective-permute-start | bytes 700424 | tf_op jit(solution)/shard_map/ppermute | solution.py:26
  27.2 8.6 %collective-permute-start.11 = (bf16[16,7296]{1,0:T(8,128)(2,1)S(1)}, bf16[16,7296]{1,0:T(8,128)(2,1)S(1)}, u32[]{:S(2)}, u32[]{:S(2)}) collective-permute-start(bf16[16,7296]{1,0:T(8,128)(2,1)S(1)} %shard_map.116.refs_0_.own_b), channel_id=1, source_target_pairs={{0,4},{1,5},{2,6},{3,7},{4,0},{5,1},{6,2},{7,3},{8,12},{9,13},{10,... | collective-permute-start | bytes 700424 | tf_op jit(solution)/shard_map/ppermute | solution.py:26
  28.8 15.7 %collective-permute-start.7 = (bf16[16,3584]{1,0:T(8,128)(2,1)S(1)}, bf16[16,3584]{1,0:T(8,128)(2,1)S(1)}, u32[]{:S(2)}, u32[]{:S(2)}) collective-permute-start(bf16[16,3584]{1,0:T(8,128)(2,1)S(1)} %slice.24), channel_id=1, source_target_pairs={{0,4},{1,5},{2,6},{3,7},{4,0},{5,1},{6,2},{7,3},{8,12},{9,13},{10,... | collective-permute-start | bytes 344072 | tf_op jit(solution)/shard_map/ppermute | solution.py:26
  29.3 15.1 %collective-permute-start.8 = (bf16[16,3584]{1,0:T(8,128)(2,1)S(1)}, bf16[16,3584]{1,0:T(8,128)(2,1)S(1)}, u32[]{:S(2)}, u32[]{:S(2)}) collective-permute-start(bf16[16,3584]{1,0:T(8,128)(2,1)S(1)} %slice.25), channel_id=1, source_target_pairs={{0,2},{1,3},{2,0},{3,1},{4,6},{5,7},{6,4},{7,5},{8,10},{9,11},{10,... | collective-permute-start | bytes 344072 | tf_op jit(solution)/shard_map/ppermute | solution.py:26
  34.3 23.1 %collective-permute-start.12 = (bf16[16,3584]{1,0:T(8,128)(2,1)S(1)}, bf16[16,3584]{1,0:T(8,128)(2,1)S(1)}, u32[]{:S(2)}, u32[]{:S(2)}) collective-permute-start(bf16[16,3584]{1,0:T(8,128)(2,1)S(1)} %slice.32), channel_id=1, source_target_pairs={{0,4},{1,5},{2,6},{3,7},{4,0},{5,1},{6,2},{7,3},{8,12},{9,13},{10,... | collective-permute-start | bytes 344072 | tf_op jit(solution)/shard_map/ppermute | solution.py:26
  35.8 21.5 %collective-permute-start.13 = (bf16[16,3584]{1,0:T(8,128)(2,1)S(1)}, bf16[16,3584]{1,0:T(8,128)(2,1)S(1)}, u32[]{:S(2)}, u32[]{:S(2)}) collective-permute-start(bf16[16,3584]{1,0:T(8,128)(2,1)S(1)} %slice.33), channel_id=1, source_target_pairs={{0,2},{1,3},{2,0},{3,1},{4,6},{5,7},{6,4},{7,5},{8,10},{9,11},{10,... | collective-permute-start | bytes 344072 | tf_op jit(solution)/shard_map/ppermute | solution.py:26
  40.7 46.1 %all-to-all-start = ((bf16[8,2,48,576]{3,2,1,0:T(8,128)(2,1)}), bf16[8,2,48,576]{3,2,1,0:T(8,128)(2,1)S(1)}, u32[]{:S(2)}, u32[]{:S(2)}) async-start(bf16[8,2,48,576]{3,2,1,0:T(8,128)(2,1)} %get-tuple-element.59), calls=%async_computation | async-start | bytes 1966080 | tf_op jit(solution)/shard_map/all_to_all | solution.py:327
  70.0 6.1 %collective-permute-start.16 = (bf16[16,3584]{1,0:T(8,128)(2,1)S(1)}, bf16[16,3584]{1,0:T(8,128)(2,1)S(1)}, u32[]{:S(2)}, u32[]{:S(2)}) collective-permute-start(bf16[16,3584]{1,0:T(8,128)(2,1)S(1)} %get-tuple-element.65), channel_id=1, source_target_pairs={{0,2},{1,3},{2,0},{3,1},{4,6},{5,7},{6,4},{7,5},{8,10},{9,11},{10,... | collective-permute-start | bytes 344072 | tf_op jit(solution)/shard_map/ppermute | solution.py:26
  70.7 6.0 %collective-permute-start.17 = (bf16[16,3584]{1,0:T(8,128)(2,1)S(1)}, bf16[16,3584]{1,0:T(8,128)(2,1)S(1)}, u32[]{:S(2)}, u32[]{:S(2)}) collective-permute-start(bf16[16,3584]{1,0:T(8,128)(2,1)S(1)} %get-tuple-element.64), channel_id=1, source_target_pairs={{0,4},{1,5},{2,6},{3,7},{4,0},{5,1},{6,2},{7,3},{8,12},{9,13},{10,... | collective-permute-start | bytes 344072 | tf_op jit(solution)/shard_map/ppermute | solution.py:26
  72.7 8.5 %collective-permute-start.21 = (bf16[16,7168]{1,0:T(8,128)(2,1)S(1)}, bf16[16,7168]{1,0:T(8,128)(2,1)S(1)}, u32[]{:S(2)}, u32[]{:S(2)}) collective-permute-start(bf16[16,7168]{1,0:T(8,128)(2,1)S(1)} %get-tuple-element.54), channel_id=1, source_target_pairs={{0,2},{1,3},{2,0},{3,1},{4,6},{5,7},{6,4},{7,5},{8,10},{9,11},{10,... | collective-permute-start | bytes 688136 | tf_op jit(solution)/shard_map/ppermute | solution.py:26
  74.1 7.9 %collective-permute-start.22 = (bf16[16,7168]{1,0:T(8,128)(2,1)S(1)}, bf16[16,7168]{1,0:T(8,128)(2,1)S(1)}, u32[]{:S(2)}, u32[]{:S(2)}) collective-permute-start(bf16[16,7168]{1,0:T(8,128)(2,1)S(1)} %get-tuple-element.55), channel_id=1, source_target_pairs={{0,4},{1,5},{2,6},{3,7},{4,0},{5,1},{6,2},{7,3},{8,12},{9,13},{10,... | collective-permute-start | bytes 688136 | tf_op jit(solution)/shard_map/ppermute | solution.py:26
  76.7 7.8 %collective-permute-start.18 = (bf16[16,7168]{1,0:T(8,128)(2,1)S(1)}, bf16[16,7168]{1,0:T(8,128)(2,1)S(1)}, u32[]{:S(2)}, u32[]{:S(2)}) collective-permute-start(bf16[16,7168]{1,0:T(8,128)(2,1)S(1)} %get-tuple-element.49), channel_id=1, source_target_pairs={{0,2},{1,3},{2,0},{3,1},{4,6},{5,7},{6,4},{7,5},{8,10},{9,11},{10,... | collective-permute-start | bytes 688136 | tf_op jit(solution)/shard_map/ppermute | solution.py:26
  78.3 6.3 %collective-permute-start.19 = (bf16[16,7168]{1,0:T(8,128)(2,1)S(1)}, bf16[16,7168]{1,0:T(8,128)(2,1)S(1)}, u32[]{:S(2)}, u32[]{:S(2)}) collective-permute-start(bf16[16,7168]{1,0:T(8,128)(2,1)S(1)} %get-tuple-element.50), channel_id=1, source_target_pairs={{0,4},{1,5},{2,6},{3,7},{4,0},{5,1},{6,2},{7,3},{8,12},{9,13},{10,... | collective-permute-start | bytes 688136 | tf_op jit(solution)/shard_map/ppermute | solution.py:26
  82.1 6.7 %collective-permute-start.24 = (bf16[8,7168]{1,0:T(8,128)(2,1)S(1)}, bf16[8,7168]{1,0:T(8,128)(2,1)S(1)}, u32[]{:S(2)}, u32[]{:S(2)}) collective-permute-start(bf16[8,7168]{1,0:T(8,128)(2,1)S(1)} %get-tuple-element.57), channel_id=1, source_target_pairs={{0,24},{1,25},{2,26},{3,27},{4,28},{5,29},{6,30},{7,31},{8,16},{9,... | collective-permute-start | bytes 344072 | tf_op jit(solution)/shard_map/ppermute | solution.py:26
  84.6 6.7 %collective-permute-start.23 = (bf16[8,7168]{1,0:T(8,128)(2,1)S(1)}, bf16[8,7168]{1,0:T(8,128)(2,1)S(1)}, u32[]{:S(2)}, u32[]{:S(2)}) collective-permute-start(bf16[8,7168]{1,0:T(8,128)(2,1)S(1)} %get-tuple-element.56), channel_id=1, source_target_pairs={{0,16},{1,17},{2,18},{3,19},{4,20},{5,21},{6,22},{7,23},{8,24},{9,... | collective-permute-start | bytes 344072 | tf_op jit(solution)/shard_map/ppermute | solution.py:26
  84.7 6.5 %collective-permute-start.20 = (bf16[8,7168]{1,0:T(8,128)(2,1)S(1)}, bf16[8,7168]{1,0:T(8,128)(2,1)S(1)}, u32[]{:S(2)}, u32[]{:S(2)}) collective-permute-start(bf16[8,7168]{1,0:T(8,128)(2,1)S(1)} %get-tuple-element.52), channel_id=1, source_target_pairs={{0,8},{1,9},{2,10},{3,11},{4,12},{5,13},{6,14},{7,15},{8,0},{9,1},... | collective-permute-start | bytes 344072 | tf_op jit(solution)/shard_map/ppermute | solution.py:26
  (15 other events, 107.8 us)

commit v3 on v2

--- a/solution.py
+++ b/solution.py
@@ -91,94 +91,69 @@
     return whole_call(stack_kernel, pieces, [((rows, pieces[0].shape[1]), pieces[0].dtype)])[0]
 
 
-def expert_math(rows, weights, near, far, gate_sum, up_sum, act):
-    own, from_x, from_y, left, right = rows
-    d = near.shape[1]
+def expert_kernel(*refs):
+    groups, sources, outs = (refs[:5], refs[5:10]), refs[10:16], refs[16:20]
+    held, (gate_sum, up_sum, act, sems) = refs[20:26], refs[26:]
+    d, hid = held[0].shape
     chunk = d // STEPS
-    half = left.shape[1]
+    half = d // 2
+    quad = groups[0][0].shape[0]
     cuts = [slice(step * chunk, (step + 1) * chunk) for step in range(STEPS)]
-    hid = gate_sum.shape[1] // len(weights)
-    for core, (w_gate, w_up, _, ready) in enumerate(weights):
+    copies = {}
+    for core in range(2):
+        for step, cut in enumerate(cuts):
+            for i in range(2):
+                at = 3 * core + i
+                copies[at, step] = pltpu.make_async_copy(
+                    sources[at].at[cut, :], held[at].at[cut, :], sems.at[at, step]
+                )
+    for core in range(2):
+        at = 3 * core + 2
+        copies[at, 0] = pltpu.make_async_copy(sources[at], held[at], sems.at[at, 0])
+    for copy in copies.values():
+        copy.start()
+    for core in range(2):
         units = slice(core * hid, (core + 1) * hid)
         for step, cut in enumerate(cuts):
-            ready(step)
-            corner = left[:, cut] if cut.stop <= half else right[:, cut.start - half : cut.stop - half]
-            block = jnp.concatenate([own[:, cut], from_x[:, cut], from_y[:, cut], corner], axis=0)
-            gate, up = dot32(block, w_gate[cut, :]), dot32(block, w_up[cut, :])
+            blocks = []
+            for own, from_x, from_y, left, right in groups:
+                corner = left[:, cut] if cut.stop <= half else right[:, cut.start - half : cut.stop - half]
+                blocks += [own[:, cut], from_x[:, cut], from_y[:, cut], corner]
+            block = jnp.concatenate(blocks, axis=0)
+            copies[3 * core, step].wait()
+            gate = dot32(block, held[3 * core][cut, :])
+            copies[3 * core + 1, step].wait()
+            up = dot32(block, held[3 * core + 1][cut, :])
             if step:
-                gate, up = gate_sum[:, units] + gate, up_sum[:, units] + up
+                gate, up = gate_sum[...] + gate, up_sum[...] + up
             if step < STEPS - 1:
-                gate_sum[:, units] = gate
-                up_sum[:, units] = up
+                gate_sum[...] = gate
+                up_sum[...] = up
             else:
                 act[:, units] = (gate / (1.0 + jnp.exp(-gate)) * up).astype(act.dtype)
-    for _, _, _, ready in weights:
-        ready(STEPS)
-    rest = near.shape[0]
+    for core in range(2):
+        copies[3 * core + 2, 0].wait()
     for cut in cuts:
-        part = sum(
-            dot32(act[:, core * hid : (core + 1) * hid], w_down[:, cut])
-            for core, (_, _, w_down, _) in enumerate(weights)
-        ).astype(near.dtype)
-        near[:, cut] = part[:rest]
-        far[:, cut] = part[rest:]
-
-
-def first_kernel(*refs):
-    rows, sources, other = refs[:5], refs[5:8], refs[8:11]
-    near, far = refs[11:13]
-    held = refs[13:16]
-    gate_sum, up_sum, act, sems = refs[16:]
-    d = held[0].shape[0]
-    chunk = d // STEPS
-    steps = []
-    for step in range(STEPS):
-        cut = slice(step * chunk, (step + 1) * chunk)
-        steps.append(
-            [
-                pltpu.make_async_copy(sources[i].at[cut, :], held[i].at[cut, :], sems.at[i, step])
-                for i in range(2)
-            ]
-        )
-    steps.append([pltpu.make_async_copy(sources[2], held[2], sems.at[2, 0])])
-    for copies in steps:
-        for copy in copies:
-            copy.start()
-
-    def ready(step):
-        for copy in steps[step]:
-            copy.wait()
-
-    weights = [tuple(other) + (lambda step: None,), tuple(held) + (ready,)]
-    expert_math(rows, weights, near, far, gate_sum, up_sum, act)
-
-
-def second_kernel(*refs):
-    rows, held, other = refs[:5], refs[5:8], refs[8:11]
-    near, far, gate_sum, up_sum, act = refs[11:]
-    weights = [tuple(w) + (lambda step: None,) for w in (other, held)]
-    expert_math(rows, weights, near, far, gate_sum, up_sum, act)
-
-
-def expert_outputs(rows, weights, other, first):
-    quad = rows[0].shape[0]
+        part = (dot32(act[:, :hid], held[2][:, cut]) + dot32(act[:, hid:], held[5][:, cut])).astype(outs[0].dtype)
+        for i in range(2):
+            start = 4 * quad * i
+            outs[2 * i][:, cut] = part[start : start + 3 * quad]
+            outs[2 * i + 1][:, cut] = part[start + 3 * quad : start + 4 * quad]
+
+
+def expert_outputs(rows_a, rows_b, weights):
+    quad = rows_a[0].shape[0]
     d, hid = weights[0].shape
     bf16, f32 = jnp.bfloat16, jnp.float32
-    outs = [((3 * quad, d), bf16), ((quad, d), bf16)]
-    scratch = [
-        pltpu.VMEM((4 * quad, 2 * hid), f32),
-        pltpu.VMEM((4 * quad, 2 * hid), f32),
-        pltpu.VMEM((4 * quad, 2 * hid), bf16),
+    outs = [((3 * quad, d), bf16), ((quad, d), bf16)] * 2
+    scratch = [pltpu.VMEM(w.shape, w.dtype) for w in weights] + [
+        pltpu.VMEM((8 * quad, hid), f32),
+        pltpu.VMEM((8 * quad, hid), f32),
+        pltpu.VMEM((8 * quad, 2 * hid), bf16),
+        pltpu.SemaphoreType.DMA((6, STEPS)),
     ]
-    flops = 2 * 4 * quad * d * 2 * hid * 3
-    if first:
-        outs = outs + [(w.shape, w.dtype) for w in weights]
-        scratch.append(pltpu.SemaphoreType.DMA((3, STEPS)))
-        ins = rows + [(w,) for w in weights] + other
-        near, far, *held = whole_call(first_kernel, ins, outs, 8, scratch, flops)
-        return near, far, held
-    near, far = whole_call(second_kernel, rows + weights + other, outs, 8, scratch, flops)
-    return near, far, weights
+    flops = 2 * 8 * quad * d * 2 * hid * 3
+    return whole_call(expert_kernel, rows_a + rows_b + [(w,) for w in weights], outs, 32, scratch, flops)
 
 
 def join_kernel(near, got_a, got_b, mine, for_x, for_y):
@@ -216,31 +191,37 @@
     return ((plane // planes) * 2 + side) * quad + (plane % planes) * rows
 
 
-def packing_kernel(who, own_a, y_a, own_b, y_b, cache, out, facts, scalars, sem):
+def own_beam():
+    return lax.div(lax.axis_index("ep"), lax.axis_size("ep") // BEAMS)
+
+
+def packing_kernel(own_a, y_a, own_b, y_b, cache, out, facts, scalars, sem):
     read_facts([own_a, y_a, own_b, y_b], facts, scalars, sem)
     rows = cache.shape[0]
+    beam = own_beam()
     for place in range(BEAMS):
         at = fact_row(place, own_a.shape[0], rows)
         first = second = count = jnp.int32(0)
         for row in range(rows):
-            hit = scalars[at + row, 0] == who[0]
+            hit = scalars[at + row, 0] == beam
             first = jnp.where(hit & (count == 0), row, first)
             second = jnp.where(hit & (count == 1), row, second)
             count = count + hit.astype(jnp.int32)
         for rank, pick in enumerate((first, second)):
-            out[who[0] ^ place, rank] = cache[pick]
-
-
-def unpacking_kernel(quad, who, facts, newest, arrived, out, scalars, sem):
+            out[beam ^ place, rank] = cache[pick]
+
+
+def unpacking_kernel(quad, facts, newest, arrived, out, scalars, sem):
     copy = pltpu.make_async_copy(facts, scalars, sem)
     copy.start()
     copy.wait()
     rows, tokens, width = out.shape
     planes = quad // rows
+    beam = own_beam()
     for row in range(rows):
         parent = scalars[row, 0]
         rank = sum([(scalars[other, 0] == parent).astype(jnp.int32) for other in range(row)], jnp.int32(0))
-        place = parent ^ who[0]
+        place = parent ^ beam
         plane, side = place // 2, place % 2
         at = ((plane // planes) * 2 + side) * quad + (plane % planes) * rows + row
         bound = scalars[at, 1]
@@ -250,12 +231,12 @@
         out[row] = value.astype(out.dtype)
 
 
-def packing_call(who, blocks, cache):
+def packing_call(blocks, cache):
     whole = pl.BlockSpec(memory_space=pltpu.VMEM)
     table = (len(blocks) * blocks[0].shape[0], LANES)
     return pl.pallas_call(
         packing_kernel,
-        in_specs=[pl.BlockSpec(memory_space=pltpu.SMEM)] + [whole] * (len(blocks) + 1),
+        in_specs=[whole] * (len(blocks) + 1),
         out_specs=[whole] * 2,
         out_shape=[
             jax.ShapeDtypeStruct((BEAMS, CAP) + cache.shape[1:], cache.dtype),
@@ -264,14 +245,14 @@
         scratch_shapes=[pltpu.SMEM(table, jnp.int32), pltpu.SemaphoreType.DMA],
         compiler_params=pltpu.CompilerParams(vmem_limit_bytes=4 * MIB),
         cost_estimate=pl.CostEstimate(flops=0, bytes_accessed=4 * cache.size, transcendentals=0),
-    )(who, *[in_vmem(b) for b in blocks], in_vmem(cache))
-
-
-def unpacking_call(who, facts, quad, newest, arrived, shape):
+    )(*[in_vmem(b) for b in blocks], in_vmem(cache))
+
+
+def unpacking_call(facts, quad, newest, arrived, shape):
     whole = pl.BlockSpec(memory_space=pltpu.VMEM)
     return pl.pallas_call(
         lambda *refs: unpacking_kernel(quad, *refs),
-        in_specs=[pl.BlockSpec(memory_space=pltpu.SMEM)] + [whole] * 3,
+        in_specs=[whole] * 3,
         out_specs=whole,
         out_shape=shape,
         scratch_shapes=[pltpu.SMEM(facts.shape, jnp.int32), pltpu.SemaphoreType.DMA],
@@ -279,7 +260,7 @@
         cost_estimate=pl.CostEstimate(
             flops=0, bytes_accessed=4 * newest.size * shape.shape[1], transcendentals=0
         ),
-    )(who, facts, newest, arrived)
+    )(facts, newest, arrived)
 
 
 def tied(*values):
@@ -304,12 +285,10 @@
     rows, d = hidden_rows.shape
     half = d // 2
     beam_stride = device_count // BEAMS
-    own_beam = device_index // beam_stride
     own_expert = device_index // SPLIT
     bf16 = jnp.bfloat16
     f32 = jnp.float32
     middle = experts // 2
-    who = own_beam.reshape(1)
 
     other = [swapped(w_gate, CORE), swapped(w_up, CORE)]
     carried = tailed(hidden_rows, parents.reshape(rows), lengths)
@@ -321,15 +300,14 @@
     rows_a = [own_a, x_a, y_a, swapped(x_a[:, :half], Y), swapped(y_a[:, half:d], X)]
     own_b = stacked(planes[middle:])
     x_b, y_b = swapped(own_b, X), swapped(own_b, Y)
-    packets, facts = packing_call(who, [own_a, y_a, own_b, y_b], latent_cache)
+    packets, facts = packing_call([own_a, y_a, own_b, y_b], latent_cache)
     rows_b = [own_b, x_b, y_b, swapped(x_b[:, :half], Y), swapped(y_b[:, half:d], X)]
     groups = [[b * beam_stride + r for b in range(BEAMS)] for r in range(beam_stride)]
     arrived = lax.all_to_all(
         packets, "ep", split_axis=0, concat_axis=0, axis_index_groups=groups, tiled=True
     )
 
-    near_a, far_a, held = expert_outputs(rows_a, [w_gate, w_up, w_down], other, True)
-    near_b, far_b, _ = expert_outputs(rows_b, held, other, False)
+    near_a, far_a, near_b, far_b = expert_outputs(rows_a, rows_b, [w_gate, w_up, w_down] + other)
 
 
     def joined(near, far):
@@ -357,7 +335,6 @@
         moe = term if moe is None else moe + term
     moe_out = moe.astype(bf16)
     new_cache = unpacking_call(
-        who,
         facts,
         own_a.shape[0],
         new_latent.astype(f32)[:, None, :],

time: 92.4 us -> 81.2 us (0.88)
  Pallas kernels: 20.1 us -> 14 us
  local copies, waits for them, and re-layouts: 11 us -> 4.98 us
  waiting for transfers between devices: 20.5 us -> 22.4 us
    pallas_call x8 -> x7, Pallas kernels: 15.3 us -> 9.11 us  [whole_call(): pl.pallas_call(body, in_specs=[far if isinstance(a, tuple) else whole for...]
    unnamed x26 -> x18, local copies, waits for them, and re-layouts: 10.9 us -> 4.9 us
    ppermute x25, waiting for transfers between devices: 20.5 us -> 22.4 us  [swapped(): return lax.ppermute(value, 'ep', [(i, i ^ mask) for i in range(peers)])]
    ppermute x25, starting transfers between devices: 34.9 us -> 33.6 us  [swapped(): return lax.ppermute(value, 'ep', [(i, i ^ mask) for i in range(peers)])]
  transfers between devices with their start and end apart: 26 -> 26, of which waited for: 10 -> 13; matrix products, arithmetic and copies ran while one was open for 0% -> 0% of each run, Pallas kernels for 22% -> 17%
where the time goes in v3:
time: 81.2 us; the launch traced here: 80.9 us
  starting transfers between devices  37.8 us (47%)
  waiting for transfers between devices  22.4 us (28%)
  Pallas kernels  14 us (17%)
  local copies, waits for them, and re-layouts  4.98 us (6%)
  between operations  0.9 us (1%)
  other arithmetic  0.83 us (1%)
    ppermute x25, starting transfers between devices, swapped(): return lax.ppermute(value, 'ep', [(i, i ^ mask) for i in range(peers)])  33.6 us
    ppermute x25, waiting for transfers between devices, swapped(): return lax.ppermute(value, 'ep', [(i, i ^ mask) for i in range(peers)])  22.4 us
    pallas_call x7, Pallas kernels, whole_call(): pl.pallas_call(body, in_specs=[far if isinstance(a, tuple) else whole for...  9.11 us
    unnamed x18, local copies, waits for them, and re-layouts  4.9 us
    all_to_all x1, starting transfers between devices, dense_local(): lax.all_to_all(packets, 'ep', split_axis=0, concat_axis=0, axis_index_gro...  4.25 us
    pallas_call x1, Pallas kernels, packing_call(): pl.pallas_call(packing_kernel, in_specs=[whole] * (len(blocks) + 1), out_...  2.28 us
    pallas_call x1, Pallas kernels, unpacking_call(): pl.pallas_call(lambda *refs: unpacking_kernel(quad, *refs), in_specs=[who...  2.03 us
  transfers between devices with their start and end apart: 26, of which 13 were waited for; matrix products, arithmetic and copies ran while one was open for 0% of the time, Pallas kernels for 17%

profile of v3, /device:TPU:0, one launch (start us, length us, event | category | flops | bytes accessed | tf_op | source)
XLA Modules:
  0.0 80.9 jit_solution(1887250853030494563)
XLA Ops:
  4.0 3.1 %collective-permute-start = (bf16[8,7296]{1,0:T(8,128)(2,1)S(1)}, bf16[8,7296]{1,0:T(8,128)(2,1)S(1)}, u32[]{:S(2)}, u32[]{:S(2)}) collective-permute-start(bf16[8,7296]{1,0:T(8,128)(2,1)S(1)} %shard_map.113.refs_0_), channel_id=1, source_target_pairs={{0,8},{1,9},{2,10},{3,11},{4,12},{5,13},{6,14},{7,15},{8,0},{9,1},... | collective-permute-start | bytes 350216 | tf_op jit(solution)/shard_map/ppermute | solution.py:26
  7.1 2.6 %collective-permute-start.3 = (bf16[8,7296]{1,0:T(8,128)(2,1)S(1)}, bf16[8,7296]{1,0:T(8,128)(2,1)S(1)}, u32[]{:S(2)}, u32[]{:S(2)}) collective-permute-start(bf16[8,7296]{1,0:T(8,128)(2,1)S(1)} %shard_map.113.refs_0_), channel_id=1, source_target_pairs={{0,16},{1,17},{2,18},{3,19},{4,20},{5,21},{6,22},{7,23},{8,24},{9,... | collective-permute-start | bytes 350216 | tf_op jit(solution)/shard_map/ppermute | solution.py:26
  9.7 2.3 %collective-permute-done.refs_1_ = bf16[8,7296]{1,0:T(8,128)(2,1)S(1)} collective-permute-done((bf16[8,7296]{1,0:T(8,128)(2,1)S(1)}, bf16[8,7296]{1,0:T(8,128)(2,1)S(1)}, u32[]{:S(2)}, u32[]{:S(2)}) %collective-permute-start) | collective-permute-done | bytes 116768 | tf_op jit(solution)/shard_map/ppermute | solution.py:26
  12.0 1.9 %collective-permute-start.1 = (bf16[16,7296]{1,0:T(8,128)(2,1)S(1)}, bf16[16,7296]{1,0:T(8,128)(2,1)S(1)}, u32[]{:S(2)}, u32[]{:S(2)}) collective-permute-start(bf16[16,7296]{1,0:T(8,128)(2,1)S(1)} %shard_map.114.refs_0_.own_a), channel_id=1, source_target_pairs={{0,2},{1,3},{2,0},{3,1},{4,6},{5,7},{6,4},{7,5},{8,10},{9,11},{10,... | collective-permute-start | bytes 700424 | tf_op jit(solution)/shard_map/ppermute | solution.py:26
  13.9 1.5 %collective-permute-start.2 = (bf16[16,7296]{1,0:T(8,128)(2,1)S(1)}, bf16[16,7296]{1,0:T(8,128)(2,1)S(1)}, u32[]{:S(2)}, u32[]{:S(2)}) collective-permute-start(bf16[16,7296]{1,0:T(8,128)(2,1)S(1)} %shard_map.114.refs_0_.own_a), channel_id=1, source_target_pairs={{0,4},{1,5},{2,6},{3,7},{4,0},{5,1},{6,2},{7,3},{8,12},{9,13},{10,... | collective-permute-start | bytes 700424 | tf_op jit(solution)/shard_map/ppermute | solution.py:26
  15.4 3.2 %collective-permute-start.4 = (bf16[8,7296]{1,0:T(8,128)(2,1)S(1)}, bf16[8,7296]{1,0:T(8,128)(2,1)S(1)}, u32[]{:S(2)}, u32[]{:S(2)}) collective-permute-start(bf16[8,7296]{1,0:T(8,128)(2,1)S(1)} %shard_map.113.refs_0_), channel_id=1, source_target_pairs={{0,24},{1,25},{2,26},{3,27},{4,28},{5,29},{6,30},{7,31},{8,16},{9,... | collective-permute-start | bytes 350216 | tf_op jit(solution)/shard_map/ppermute | solution.py:26
  18.6 3.4 %collective-permute-done.4.refs_1_ = bf16[8,7296]{1,0:T(8,128)(2,1)S(1)} collective-permute-done((bf16[8,7296]{1,0:T(8,128)(2,1)S(1)}, bf16[8,7296]{1,0:T(8,128)(2,1)S(1)}, u32[]{:S(2)}, u32[]{:S(2)}) %collective-permute-start.4) | collective-permute-done | bytes 116768 | tf_op jit(solution)/shard_map/ppermute | solution.py:26
  22.2 1.6 %copy-done.4 = bf16[7168,256]{1,0:T(8,128)(2,1)} copy-done((bf16[7168,256]{1,0:T(8,128)(2,1)}, bf16[7168,256]{1,0:T(8,128)(2,1)S(1)}, u32[]{:S(2)}) %copy-start.4) | copy-done | bytes 3670040
  23.9 1.5 %collective-permute-start.9 = (bf16[16,7296]{1,0:T(8,128)(2,1)S(1)}, bf16[16,7296]{1,0:T(8,128)(2,1)S(1)}, u32[]{:S(2)}, u32[]{:S(2)}) collective-permute-start(bf16[16,7296]{1,0:T(8,128)(2,1)S(1)} %shard_map.115.refs_5_.own_b), channel_id=1, source_target_pairs={{0,2},{1,3},{2,0},{3,1},{4,6},{5,7},{6,4},{7,5},{8,10},{9,11},{10,... | collective-permute-start | bytes 700424 | tf_op jit(solution)/shard_map/ppermute | solution.py:26
  25.3 1.5 %collective-permute-start.10 = (bf16[16,7296]{1,0:T(8,128)(2,1)S(1)}, bf16[16,7296]{1,0:T(8,128)(2,1)S(1)}, u32[]{:S(2)}, u32[]{:S(2)}) collective-permute-start(bf16[16,7296]{1,0:T(8,128)(2,1)S(1)} %shard_map.115.refs_5_.own_b), channel_id=1, source_target_pairs={{0,4},{1,5},{2,6},{3,7},{4,0},{5,1},{6,2},{7,3},{8,12},{9,13},{10,... | collective-permute-start | bytes 700424 | tf_op jit(solution)/shard_map/ppermute | solution.py:26
  28.7 2.9 %collective-permute-done.9.refs_6_ = bf16[16,7296]{1,0:T(8,128)(2,1)S(1)} collective-permute-done((bf16[16,7296]{1,0:T(8,128)(2,1)S(1)}, bf16[16,7296]{1,0:T(8,128)(2,1)S(1)}, u32[]{:S(2)}, u32[]{:S(2)}) %collective-permute-start.9) | collective-permute-done | bytes 233504 | tf_op jit(solution)/shard_map/ppermute | solution.py:26
  31.6 1.6 %collective-permute-start.11 = (bf16[16,3584]{1,0:T(8,128)(2,1)S(1)}, bf16[16,3584]{1,0:T(8,128)(2,1)S(1)}, u32[]{:S(2)}, u32[]{:S(2)}) collective-permute-start(bf16[16,3584]{1,0:T(8,128)(2,1)S(1)} %slice.32), channel_id=1, source_target_pairs={{0,4},{1,5},{2,6},{3,7},{4,0},{5,1},{6,2},{7,3},{8,12},{9,13},{10,... | collective-permute-start | bytes 344072 | tf_op jit(solution)/shard_map/ppermute | solution.py:26
  36.0 2.3 %shard_map.121 = (bf16[8,2,48,576]{3,2,1,0:T(8,128)(2,1)}, s32[64,128]{1,0:T(8,128)S(1)}) custom-call(bf16[16,7296]{1,0:T(8,128)(2,1)S(1)} %shard_map.114.refs_0_.own_a, bf16[16,7296]{1,0:T(8,128)(2,1)S(1)} %collective-permute-done.2.refs_2_.y_a, bf16[16,7296]{1,0:T(8,128)(2,1)S(1)} %shard_map.115.refs_5_.own_b, ...), custom_call_target="tpu_custom_call" | custom-call | bytes 884736 | tf_op jit(solution)/shard_map/pallas_call | solution.py:237
  38.2 4.2 %all-to-all-start = ((bf16[8,2,48,576]{3,2,1,0:T(8,128)(2,1)}), bf16[8,2,48,576]{3,2,1,0:T(8,128)(2,1)S(1)}, u32[]{:S(2)}, u32[]{:S(2)}) async-start(bf16[8,2,48,576]{3,2,1,0:T(8,128)(2,1)} %get-tuple-element.53), calls=%async_computation | async-start | bytes 1966080 | tf_op jit(solution)/shard_map/all_to_all | solution.py:306
  42.5 8.7 %shard_map.116 = (bf16[48,7168]{1,0:T(8,128)(2,1)S(1)}, bf16[16,7168]{1,0:T(8,128)(2,1)S(1)}, bf16[48,7168]{1,0:T(8,128)(2,1)S(1)}, bf16[16,7168]{1,0:T(8,128)(2,1)S(1)}) custom-call(bf16[16,7296]{1,0:T(8,128)(2,1)S(1)} %shard_map.114.refs_0_.own_a, bf16[16,7296]{1,0:T(8,128)(2,1)S(1)} %collective-permute-done.1.refs_1_, ...), custom_call_target="tpu_custom_call" | custom-call | flops 2818572288 | bytes 23879680 | tf_op jit(solution)/shard_map/pallas_call | solution.py:46
  51.3 1.6 %collective-permute-start.14 = (bf16[16,3584]{1,0:T(8,128)(2,1)S(1)}, bf16[16,3584]{1,0:T(8,128)(2,1)S(1)}, u32[]{:S(2)}, u32[]{:S(2)}) collective-permute-start(bf16[16,3584]{1,0:T(8,128)(2,1)S(1)} %get-tuple-element.61), channel_id=1, source_target_pairs={{0,2},{1,3},{2,0},{3,1},{4,6},{5,7},{6,4},{7,5},{8,10},{9,11},{10,... | collective-permute-start | bytes 344072 | tf_op jit(solution)/shard_map/ppermute | solution.py:26
  53.0 2.0 %collective-permute-start.15 = (bf16[16,3584]{1,0:T(8,128)(2,1)S(1)}, bf16[16,3584]{1,0:T(8,128)(2,1)S(1)}, u32[]{:S(2)}, u32[]{:S(2)}) collective-permute-start(bf16[16,3584]{1,0:T(8,128)(2,1)S(1)} %get-tuple-element.60), channel_id=1, source_target_pairs={{0,4},{1,5},{2,6},{3,7},{4,0},{5,1},{6,2},{7,3},{8,12},{9,13},{10,... | collective-permute-start | bytes 344072 | tf_op jit(solution)/shard_map/ppermute | solution.py:26
  56.3 3.9 %collective-permute-done.15.got_b = bf16[16,3584]{1,0:T(8,128)(2,1)S(1)} collective-permute-done((bf16[16,3584]{1,0:T(8,128)(2,1)S(1)}, bf16[16,3584]{1,0:T(8,128)(2,1)S(1)}, u32[]{:S(2)}, u32[]{:S(2)}) %collective-permute-start.15) | collective-permute-done | bytes 114720 | tf_op jit(solution)/shard_map/ppermute | solution.py:26
  62.5 1.9 %collective-permute-start.22 = (bf16[16,7168]{1,0:T(8,128)(2,1)S(1)}, bf16[16,7168]{1,0:T(8,128)(2,1)S(1)}, u32[]{:S(2)}, u32[]{:S(2)}) collective-permute-start(bf16[16,7168]{1,0:T(8,128)(2,1)S(1)} %get-tuple-element.49), channel_id=1, source_target_pairs={{0,4},{1,5},{2,6},{3,7},{4,0},{5,1},{6,2},{7,3},{8,12},{9,13},{10,... | collective-permute-start | bytes 688136 | tf_op jit(solution)/shard_map/ppermute | solution.py:26
  64.4 1.9 %collective-permute-done.16.got_a = bf16[16,3584]{1,0:T(8,128)(2,1)S(1)} collective-permute-done((bf16[16,3584]{1,0:T(8,128)(2,1)S(1)}, bf16[16,3584]{1,0:T(8,128)(2,1)S(1)}, u32[]{:S(2)}, u32[]{:S(2)}) %collective-permute-start.16) | collective-permute-done | bytes 114720 | tf_op jit(solution)/shard_map/ppermute | solution.py:26
  66.9 1.7 %collective-permute-start.18 = (bf16[16,7168]{1,0:T(8,128)(2,1)S(1)}, bf16[16,7168]{1,0:T(8,128)(2,1)S(1)}, u32[]{:S(2)}, u32[]{:S(2)}) collective-permute-start(bf16[16,7168]{1,0:T(8,128)(2,1)S(1)} %get-tuple-element.43), channel_id=1, source_target_pairs={{0,2},{1,3},{2,0},{3,1},{4,6},{5,7},{6,4},{7,5},{8,10},{9,11},{10,... | collective-permute-start | bytes 688136 | tf_op jit(solution)/shard_map/ppermute | solution.py:26
  69.6 3.6 %collective-permute-start.24 = (bf16[8,7168]{1,0:T(8,128)(2,1)S(1)}, bf16[8,7168]{1,0:T(8,128)(2,1)S(1)}, u32[]{:S(2)}, u32[]{:S(2)}) collective-permute-start(bf16[8,7168]{1,0:T(8,128)(2,1)S(1)} %get-tuple-element.51), channel_id=1, source_target_pairs={{0,24},{1,25},{2,26},{3,27},{4,28},{5,29},{6,30},{7,31},{8,16},{9,... | collective-permute-start | bytes 344072 | tf_op jit(solution)/shard_map/ppermute | solution.py:26
  74.9 2.0 %shard_map.122 = bf16[8,48,576]{2,1,0:T(8,128)(2,1)} custom-call(s32[64,128]{1,0:T(8,128)S(1)} %get-tuple-element.52.refs_0_, f32[8,1,576]{2,1,0:T(1,128)S(1)} %reshape.12.refs_1_, bf16[8,2,48,576]{3,2,1,0:T(8,128)(2,1)S(1)} %all-to-all-done.refs_2_), custom_call_target="tpu_custom_call" | custom-call | bytes 884736 | tf_op jit(solution)/shard_map/pallas_call | solution.py:253
  76.9 2.0 %collective-permute-done.23 = bf16[8,7168]{1,0:T(8,128)(2,1)S(1)} collective-permute-done((bf16[8,7168]{1,0:T(8,128)(2,1)S(1)}, bf16[8,7168]{1,0:T(8,128)(2,1)S(1)}, u32[]{:S(2)}, u32[]{:S(2)}) %collective-permute-start.23) | collective-permute-done | bytes 114720 | tf_op jit(solution)/shard_map/ppermute | solution.py:26
  (65 shorter events, 16.9 us)
Async XLA Ops:
  0.6 21.4 %collective-permute-start.5 = (bf16[7168,256]{1,0:T(8,128)(2,1)}, bf16[7168,256]{1,0:T(8,128)(2,1)S(1)}, u32[]{:S(2)}, u32[]{:S(2)}) collective-permute-start(bf16[7168,256]{1,0:T(8,128)(2,1)} %refs_10_.1), channel_id=1, source_target_pairs={{0,1},{1,0},{2,3},{3,2},{4,5},{5,4},{6,7},{7,6},{8,9},{9,8},{10,11... | collective-permute-start | bytes 11010056 | tf_op jit(solution)/shard_map/ppermute | solution.py:26
  1.1 20.9 %collective-permute-start.6 = (bf16[7168,256]{1,0:T(8,128)(2,1)}, bf16[7168,256]{1,0:T(8,128)(2,1)S(1)}, u32[]{:S(2)}, u32[]{:S(2)}) collective-permute-start(bf16[7168,256]{1,0:T(8,128)(2,1)} %refs_11_.1), channel_id=1, source_target_pairs={{0,1},{1,0},{2,3},{3,2},{4,5},{5,4},{6,7},{7,6},{8,9},{9,8},{10,11... | collective-permute-start | bytes 11010056 | tf_op jit(solution)/shard_map/ppermute | solution.py:26
  4.0 8.0 %collective-permute-start = (bf16[8,7296]{1,0:T(8,128)(2,1)S(1)}, bf16[8,7296]{1,0:T(8,128)(2,1)S(1)}, u32[]{:S(2)}, u32[]{:S(2)}) collective-permute-start(bf16[8,7296]{1,0:T(8,128)(2,1)S(1)} %shard_map.113.refs_0_), channel_id=1, source_target_pairs={{0,8},{1,9},{2,10},{3,11},{4,12},{5,13},{6,14},{7,15},{8,0},{9,1},... | collective-permute-start | bytes 350216 | tf_op jit(solution)/shard_map/ppermute | solution.py:26
  7.1 8.4 %collective-permute-start.3 = (bf16[8,7296]{1,0:T(8,128)(2,1)S(1)}, bf16[8,7296]{1,0:T(8,128)(2,1)S(1)}, u32[]{:S(2)}, u32[]{:S(2)}) collective-permute-start(bf16[8,7296]{1,0:T(8,128)(2,1)S(1)} %shard_map.113.refs_0_), channel_id=1, source_target_pairs={{0,16},{1,17},{2,18},{3,19},{4,20},{5,21},{6,22},{7,23},{8,24},{9,... | collective-permute-start | bytes 350216 | tf_op jit(solution)/shard_map/ppermute | solution.py:26
  12.0 10.0 %collective-permute-start.1 = (bf16[16,7296]{1,0:T(8,128)(2,1)S(1)}, bf16[16,7296]{1,0:T(8,128)(2,1)S(1)}, u32[]{:S(2)}, u32[]{:S(2)}) collective-permute-start(bf16[16,7296]{1,0:T(8,128)(2,1)S(1)} %shard_map.114.refs_0_.own_a), channel_id=1, source_target_pairs={{0,2},{1,3},{2,0},{3,1},{4,6},{5,7},{6,4},{7,5},{8,10},{9,11},{10,... | collective-permute-start | bytes 700424 | tf_op jit(solution)/shard_map/ppermute | solution.py:26
  13.9 8.1 %collective-permute-start.2 = (bf16[16,7296]{1,0:T(8,128)(2,1)S(1)}, bf16[16,7296]{1,0:T(8,128)(2,1)S(1)}, u32[]{:S(2)}, u32[]{:S(2)}) collective-permute-start(bf16[16,7296]{1,0:T(8,128)(2,1)S(1)} %shard_map.114.refs_0_.own_a), channel_id=1, source_target_pairs={{0,4},{1,5},{2,6},{3,7},{4,0},{5,1},{6,2},{7,3},{8,12},{9,13},{10,... | collective-permute-start | bytes 700424 | tf_op jit(solution)/shard_map/ppermute | solution.py:26
  15.4 6.6 %collective-permute-start.4 = (bf16[8,7296]{1,0:T(8,128)(2,1)S(1)}, bf16[8,7296]{1,0:T(8,128)(2,1)S(1)}, u32[]{:S(2)}, u32[]{:S(2)}) collective-permute-start(bf16[8,7296]{1,0:T(8,128)(2,1)S(1)} %shard_map.113.refs_0_), channel_id=1, source_target_pairs={{0,24},{1,25},{2,26},{3,27},{4,28},{5,29},{6,30},{7,31},{8,16},{9,... | collective-permute-start | bytes 350216 | tf_op jit(solution)/shard_map/ppermute | solution.py:26
  22.1 20.4 %collective-permute-start.13 = (bf16[256,7168]{1,0:T(8,128)(2,1)}, bf16[256,7168]{1,0:T(8,128)(2,1)}, u32[]{:S(2)}, u32[]{:S(2)}) collective-permute-start(bf16[256,7168]{1,0:T(8,128)(2,1)} %refs_12_.1), channel_id=1, source_target_pairs={{0,1},{1,0},{2,3},{3,2},{4,5},{5,4},{6,7},{7,6},{8,9},{9,8},{10,11... | collective-permute-start | bytes 11010056 | tf_op jit(solution)/shard_map/ppermute | solution.py:26
  23.9 7.7 %collective-permute-start.9 = (bf16[16,7296]{1,0:T(8,128)(2,1)S(1)}, bf16[16,7296]{1,0:T(8,128)(2,1)S(1)}, u32[]{:S(2)}, u32[]{:S(2)}) collective-permute-start(bf16[16,7296]{1,0:T(8,128)(2,1)S(1)} %shard_map.115.refs_5_.own_b), channel_id=1, source_target_pairs={{0,2},{1,3},{2,0},{3,1},{4,6},{5,7},{6,4},{7,5},{8,10},{9,11},{10,... | collective-permute-start | bytes 700424 | tf_op jit(solution)/shard_map/ppermute | solution.py:26
  25.3 8.6 %collective-permute-start.10 = (bf16[16,7296]{1,0:T(8,128)(2,1)S(1)}, bf16[16,7296]{1,0:T(8,128)(2,1)S(1)}, u32[]{:S(2)}, u32[]{:S(2)}) collective-permute-start(bf16[16,7296]{1,0:T(8,128)(2,1)S(1)} %shard_map.115.refs_5_.own_b), channel_id=1, source_target_pairs={{0,4},{1,5},{2,6},{3,7},{4,0},{5,1},{6,2},{7,3},{8,12},{9,13},{10,... | collective-permute-start | bytes 700424 | tf_op jit(solution)/shard_map/ppermute | solution.py:26
  26.9 15.6 %collective-permute-start.7 = (bf16[16,3584]{1,0:T(8,128)(2,1)S(1)}, bf16[16,3584]{1,0:T(8,128)(2,1)S(1)}, u32[]{:S(2)}, u32[]{:S(2)}) collective-permute-start(bf16[16,3584]{1,0:T(8,128)(2,1)S(1)} %slice.24), channel_id=1, source_target_pairs={{0,4},{1,5},{2,6},{3,7},{4,0},{5,1},{6,2},{7,3},{8,12},{9,13},{10,... | collective-permute-start | bytes 344072 | tf_op jit(solution)/shard_map/ppermute | solution.py:26
  27.4 15.1 %collective-permute-start.8 = (bf16[16,3584]{1,0:T(8,128)(2,1)S(1)}, bf16[16,3584]{1,0:T(8,128)(2,1)S(1)}, u32[]{:S(2)}, u32[]{:S(2)}) collective-permute-start(bf16[16,3584]{1,0:T(8,128)(2,1)S(1)} %slice.25), channel_id=1, source_target_pairs={{0,2},{1,3},{2,0},{3,1},{4,6},{5,7},{6,4},{7,5},{8,10},{9,11},{10,... | collective-permute-start | bytes 344072 | tf_op jit(solution)/shard_map/ppermute | solution.py:26
  31.6 10.9 %collective-permute-start.11 = (bf16[16,3584]{1,0:T(8,128)(2,1)S(1)}, bf16[16,3584]{1,0:T(8,128)(2,1)S(1)}, u32[]{:S(2)}, u32[]{:S(2)}) collective-permute-start(bf16[16,3584]{1,0:T(8,128)(2,1)S(1)} %slice.32), channel_id=1, source_target_pairs={{0,4},{1,5},{2,6},{3,7},{4,0},{5,1},{6,2},{7,3},{8,12},{9,13},{10,... | collective-permute-start | bytes 344072 | tf_op jit(solution)/shard_map/ppermute | solution.py:26
  34.0 8.6 %collective-permute-start.12 = (bf16[16,3584]{1,0:T(8,128)(2,1)S(1)}, bf16[16,3584]{1,0:T(8,128)(2,1)S(1)}, u32[]{:S(2)}, u32[]{:S(2)}) collective-permute-start(bf16[16,3584]{1,0:T(8,128)(2,1)S(1)} %slice.33), channel_id=1, source_target_pairs={{0,2},{1,3},{2,0},{3,1},{4,6},{5,7},{6,4},{7,5},{8,10},{9,11},{10,... | collective-permute-start | bytes 344072 | tf_op jit(solution)/shard_map/ppermute | solution.py:26
  38.2 36.6 %all-to-all-start = ((bf16[8,2,48,576]{3,2,1,0:T(8,128)(2,1)}), bf16[8,2,48,576]{3,2,1,0:T(8,128)(2,1)S(1)}, u32[]{:S(2)}, u32[]{:S(2)}) async-start(bf16[8,2,48,576]{3,2,1,0:T(8,128)(2,1)} %get-tuple-element.53), calls=%async_computation | async-start | bytes 1966080 | tf_op jit(solution)/shard_map/all_to_all | solution.py:306
  53.0 7.2 %collective-permute-start.15 = (bf16[16,3584]{1,0:T(8,128)(2,1)S(1)}, bf16[16,3584]{1,0:T(8,128)(2,1)S(1)}, u32[]{:S(2)}, u32[]{:S(2)}) collective-permute-start(bf16[16,3584]{1,0:T(8,128)(2,1)S(1)} %get-tuple-element.60), channel_id=1, source_target_pairs={{0,4},{1,5},{2,6},{3,7},{4,0},{5,1},{6,2},{7,3},{8,12},{9,13},{10,... | collective-permute-start | bytes 344072 | tf_op jit(solution)/shard_map/ppermute | solution.py:26
  60.3 6.1 %collective-permute-start.16 = (bf16[16,3584]{1,0:T(8,128)(2,1)S(1)}, bf16[16,3584]{1,0:T(8,128)(2,1)S(1)}, u32[]{:S(2)}, u32[]{:S(2)}) collective-permute-start(bf16[16,3584]{1,0:T(8,128)(2,1)S(1)} %get-tuple-element.59), channel_id=1, source_target_pairs={{0,2},{1,3},{2,0},{3,1},{4,6},{5,7},{6,4},{7,5},{8,10},{9,11},{10,... | collective-permute-start | bytes 344072 | tf_op jit(solution)/shard_map/ppermute | solution.py:26
  60.8 6.0 %collective-permute-start.17 = (bf16[16,3584]{1,0:T(8,128)(2,1)S(1)}, bf16[16,3584]{1,0:T(8,128)(2,1)S(1)}, u32[]{:S(2)}, u32[]{:S(2)}) collective-permute-start(bf16[16,3584]{1,0:T(8,128)(2,1)S(1)} %get-tuple-element.58), channel_id=1, source_target_pairs={{0,4},{1,5},{2,6},{3,7},{4,0},{5,1},{6,2},{7,3},{8,12},{9,13},{10,... | collective-permute-start | bytes 344072 | tf_op jit(solution)/shard_map/ppermute | solution.py:26
  61.6 7.5 %collective-permute-start.21 = (bf16[16,7168]{1,0:T(8,128)(2,1)S(1)}, bf16[16,7168]{1,0:T(8,128)(2,1)S(1)}, u32[]{:S(2)}, u32[]{:S(2)}) collective-permute-start(bf16[16,7168]{1,0:T(8,128)(2,1)S(1)} %get-tuple-element.48), channel_id=1, source_target_pairs={{0,2},{1,3},{2,0},{3,1},{4,6},{5,7},{6,4},{7,5},{8,10},{9,11},{10,... | collective-permute-start | bytes 688136 | tf_op jit(solution)/shard_map/ppermute | solution.py:26
  62.5 7.0 %collective-permute-start.22 = (bf16[16,7168]{1,0:T(8,128)(2,1)S(1)}, bf16[16,7168]{1,0:T(8,128)(2,1)S(1)}, u32[]{:S(2)}, u32[]{:S(2)}) collective-permute-start(bf16[16,7168]{1,0:T(8,128)(2,1)S(1)} %get-tuple-element.49), channel_id=1, source_target_pairs={{0,4},{1,5},{2,6},{3,7},{4,0},{5,1},{6,2},{7,3},{8,12},{9,13},{10,... | collective-permute-start | bytes 688136 | tf_op jit(solution)/shard_map/ppermute | solution.py:26
  66.9 6.3 %collective-permute-start.18 = (bf16[16,7168]{1,0:T(8,128)(2,1)S(1)}, bf16[16,7168]{1,0:T(8,128)(2,1)S(1)}, u32[]{:S(2)}, u32[]{:S(2)}) collective-permute-start(bf16[16,7168]{1,0:T(8,128)(2,1)S(1)} %get-tuple-element.43), channel_id=1, source_target_pairs={{0,2},{1,3},{2,0},{3,1},{4,6},{5,7},{6,4},{7,5},{8,10},{9,11},{10,... | collective-permute-start | bytes 688136 | tf_op jit(solution)/shard_map/ppermute | solution.py:26
  68.6 6.0 %collective-permute-start.19 = (bf16[16,7168]{1,0:T(8,128)(2,1)S(1)}, bf16[16,7168]{1,0:T(8,128)(2,1)S(1)}, u32[]{:S(2)}, u32[]{:S(2)}) collective-permute-start(bf16[16,7168]{1,0:T(8,128)(2,1)S(1)} %get-tuple-element.44), channel_id=1, source_target_pairs={{0,4},{1,5},{2,6},{3,7},{4,0},{5,1},{6,2},{7,3},{8,12},{9,13},{10,... | collective-permute-start | bytes 688136 | tf_op jit(solution)/shard_map/ppermute | solution.py:26
  69.6 7.3 %collective-permute-start.24 = (bf16[8,7168]{1,0:T(8,128)(2,1)S(1)}, bf16[8,7168]{1,0:T(8,128)(2,1)S(1)}, u32[]{:S(2)}, u32[]{:S(2)}) collective-permute-start(bf16[8,7168]{1,0:T(8,128)(2,1)S(1)} %get-tuple-element.51), channel_id=1, source_target_pairs={{0,24},{1,25},{2,26},{3,27},{4,28},{5,29},{6,30},{7,31},{8,16},{9,... | collective-permute-start | bytes 344072 | tf_op jit(solution)/shard_map/ppermute | solution.py:26
  73.2 5.7 %collective-permute-start.23 = (bf16[8,7168]{1,0:T(8,128)(2,1)S(1)}, bf16[8,7168]{1,0:T(8,128)(2,1)S(1)}, u32[]{:S(2)}, u32[]{:S(2)}) collective-permute-start(bf16[8,7168]{1,0:T(8,128)(2,1)S(1)} %get-tuple-element.50), channel_id=1, source_target_pairs={{0,16},{1,17},{2,18},{3,19},{4,20},{5,21},{6,22},{7,23},{8,24},{9,... | collective-permute-start | bytes 344072 | tf_op jit(solution)/shard_map/ppermute | solution.py:26
  (11 other events, 89.2 us)

commit v4 on v3

--- a/solution.py
+++ b/solution.py
@@ -54,31 +54,43 @@
     )(*[in_hbm(a[0]) if isinstance(a, tuple) else in_vmem(a) for a in ins])
 
 
-def tailed_kernel(parents, lengths, rows, out):
+def tailed_kernel(parents, lengths, rows, out, parent, length, sems):
     d = rows.shape[1]
+    copies = [
+        pltpu.make_async_copy(parents, parent, sems.at[0]),
+        pltpu.make_async_copy(lengths, length, sems.at[1]),
+        pltpu.make_async_copy(rows, out.at[:, pl.ds(0, d)], sems.at[2]),
+    ]
+    for copy in copies:
+        copy.start()
     shape = (rows.shape[0], LANES)
     row = lax.broadcasted_iota(jnp.int32, shape, 0)
     lane = lax.broadcasted_iota(jnp.int32, shape, 1)
     tail = jnp.zeros(shape, jnp.int32)
+    copies[0].wait()
+    copies[1].wait()
     for i in range(shape[0]):
-        tail = jnp.where((row == i) & (lane == 0), parents[i], tail)
-        tail = jnp.where((row == i) & (lane == 1), lengths[i], tail)
-    out[:, :d] = rows[...]
+        tail = jnp.where((row == i) & (lane == 0), parent[i], tail)
+        tail = jnp.where((row == i) & (lane == 1), length[i], tail)
     out[:, d:] = tail.astype(jnp.float32).astype(out.dtype)
+    copies[2].wait()
 
 
 def tailed(rows, parents, lengths):
     count, d = rows.shape
-    scalars = pl.BlockSpec(memory_space=pltpu.SMEM)
-    whole = pl.BlockSpec(memory_space=pltpu.VMEM)
     return pl.pallas_call(
         tailed_kernel,
-        in_specs=[scalars, scalars, whole],
-        out_specs=whole,
+        in_specs=[pl.BlockSpec(memory_space=pltpu.HBM)] * 3,
+        out_specs=pl.BlockSpec(memory_space=pltpu.VMEM),
         out_shape=pltpu.VMEM((count, d + LANES), rows.dtype),
+        scratch_shapes=[
+            pltpu.SMEM((count,), jnp.int32),
+            pltpu.SMEM((count,), jnp.int32),
+            pltpu.SemaphoreType.DMA((3,)),
+        ],
         compiler_params=pltpu.CompilerParams(vmem_limit_bytes=2 * MIB),
         cost_estimate=pl.CostEstimate(flops=0, bytes_accessed=4 * count * d, transcendentals=0),
-    )(parents, lengths, rows)
+    )(in_hbm(parents), in_hbm(lengths), in_hbm(rows))
 
 
 def stack_kernel(*refs):
@@ -107,9 +119,11 @@
                 copies[at, step] = pltpu.make_async_copy(
                     sources[at].at[cut, :], held[at].at[cut, :], sems.at[at, step]
                 )
-    for core in range(2):
-        at = 3 * core + 2
-        copies[at, 0] = pltpu.make_async_copy(sources[at], held[at], sems.at[at, 0])
+    for step, cut in enumerate(cuts):
+        for at in (2, 5):
+            copies[at, step] = pltpu.make_async_copy(
+                sources[at].at[:, cut], held[at].at[:, cut], sems.at[at, step]
+            )
     for copy in copies.values():
         copy.start()
     for core in range(2):
@@ -131,9 +145,9 @@
                 up_sum[...] = up
             else:
                 act[:, units] = (gate / (1.0 + jnp.exp(-gate)) * up).astype(act.dtype)
-    for core in range(2):
-        copies[3 * core + 2, 0].wait()
-    for cut in cuts:
+    for step, cut in enumerate(cuts):
+        for at in (2, 5):
+            copies[at, step].wait()
         part = (dot32(act[:, :hid], held[2][:, cut]) + dot32(act[:, hid:], held[5][:, cut])).astype(outs[0].dtype)
         for i in range(2):
             start = 4 * quad * i
@@ -320,7 +334,6 @@
             total_kernel, [mine, swapped(for_x, X), swapped(for_y, Y)], [((rows, d), bf16)] * count
         )
     mine_b, to_x_b, to_y_b = joined(near_b, far_b)
-    far_a, to_x_b, to_y_b = tied(far_a, to_x_b, to_y_b)
     sums_b = totals(mine_b, to_x_b, to_y_b, experts - middle)
     mine_a, to_x_a, to_y_a = joined(near_a, far_a)
     sums_a = totals(mine_a, to_x_a, to_y_a, middle)

time: 81.2 us -> 76.1 us (0.937)
  waiting for transfers between devices: 22.4 us -> 19.8 us
  local copies, waits for them, and re-layouts: 4.98 us -> 2.77 us
    ppermute x25, waiting for transfers between devices: 22.4 us -> 19.7 us  [swapped(): return lax.ppermute(value, 'ep', [(i, i ^ mask) for i in range(peers)])]
    unnamed x18 -> x12, local copies, waits for them, and re-layouts: 4.9 us -> 2.69 us
  transfers between devices with their start and end apart: 26 -> 26, of which waited for: 13 -> 10; matrix products, arithmetic and copies ran while one was open for 0% -> 0% of each run, Pallas kernels for 17% -> 18%
where the time goes in v4:
time: 76.1 us; the launch traced here: 75.8 us
  starting transfers between devices  37.8 us (50%)
  waiting for transfers between devices  19.8 us (26%)
  Pallas kernels  13.8 us (18%)
  local copies, waits for them, and re-layouts  2.77 us (4%)
  between operations  0.86 us (1%)
  other arithmetic  0.83 us (1%)
    ppermute x25, starting transfers between devices, swapped(): return lax.ppermute(value, 'ep', [(i, i ^ mask) for i in range(peers)])  33.5 us
    ppermute x25, waiting for transfers between devices, swapped(): return lax.ppermute(value, 'ep', [(i, i ^ mask) for i in range(peers)])  19.7 us
    pallas_call x7, Pallas kernels, whole_call(): pl.pallas_call(body, in_specs=[far if isinstance(a, tuple) else whole for...  8.62 us
    all_to_all x1, starting transfers between devices, dense_local(): lax.all_to_all(packets, 'ep', split_axis=0, concat_axis=0, axis_index_gro...  4.25 us
    unnamed x12, local copies, waits for them, and re-layouts  2.69 us
    pallas_call x1, Pallas kernels, packing_call(): pl.pallas_call(packing_kernel, in_specs=[whole] * (len(blocks) + 1), out_...  2.25 us
    pallas_call x1, Pallas kernels, unpacking_call(): pl.pallas_call(lambda *refs: unpacking_kernel(quad, *refs), in_specs=[who...  2.03 us
  transfers between devices with their start and end apart: 26, of which 10 were waited for; matrix products, arithmetic and copies ran while one was open for 0% of the time, Pallas kernels for 18%

profile of v4, /device:TPU:0, one launch (start us, length us, event | category | flops | bytes accessed | tf_op | source)
XLA Modules:
  0.0 75.8 jit_solution(7250485930931176350)
XLA Ops:
  2.2 3.1 %collective-permute-start = (bf16[8,7296]{1,0:T(8,128)(2,1)S(1)}, bf16[8,7296]{1,0:T(8,128)(2,1)S(1)}, u32[]{:S(2)}, u32[]{:S(2)}) collective-permute-start(bf16[8,7296]{1,0:T(8,128)(2,1)S(1)} %shard_map.113.refs_0_), channel_id=1, source_target_pairs={{0,8},{1,9},{2,10},{3,11},{4,12},{5,13},{6,14},{7,15},{8,0},{9,1},... | collective-permute-start | bytes 350216 | tf_op jit(solution)/shard_map/ppermute | solution.py:26
  5.2 2.6 %collective-permute-start.3 = (bf16[8,7296]{1,0:T(8,128)(2,1)S(1)}, bf16[8,7296]{1,0:T(8,128)(2,1)S(1)}, u32[]{:S(2)}, u32[]{:S(2)}) collective-permute-start(bf16[8,7296]{1,0:T(8,128)(2,1)S(1)} %shard_map.113.refs_0_), channel_id=1, source_target_pairs={{0,16},{1,17},{2,18},{3,19},{4,20},{5,21},{6,22},{7,23},{8,24},{9,... | collective-permute-start | bytes 350216 | tf_op jit(solution)/shard_map/ppermute | solution.py:26
  7.8 2.3 %collective-permute-done.refs_1_ = bf16[8,7296]{1,0:T(8,128)(2,1)S(1)} collective-permute-done((bf16[8,7296]{1,0:T(8,128)(2,1)S(1)}, bf16[8,7296]{1,0:T(8,128)(2,1)S(1)}, u32[]{:S(2)}, u32[]{:S(2)}) %collective-permute-start) | collective-permute-done | bytes 116768 | tf_op jit(solution)/shard_map/ppermute | solution.py:26
  10.2 1.9 %collective-permute-start.1 = (bf16[16,7296]{1,0:T(8,128)(2,1)S(1)}, bf16[16,7296]{1,0:T(8,128)(2,1)S(1)}, u32[]{:S(2)}, u32[]{:S(2)}) collective-permute-start(bf16[16,7296]{1,0:T(8,128)(2,1)S(1)} %shard_map.114.refs_0_.own_a), channel_id=1, source_target_pairs={{0,2},{1,3},{2,0},{3,1},{4,6},{5,7},{6,4},{7,5},{8,10},{9,11},{10,... | collective-permute-start | bytes 700424 | tf_op jit(solution)/shard_map/ppermute | solution.py:26
  12.1 1.5 %collective-permute-start.2 = (bf16[16,7296]{1,0:T(8,128)(2,1)S(1)}, bf16[16,7296]{1,0:T(8,128)(2,1)S(1)}, u32[]{:S(2)}, u32[]{:S(2)}) collective-permute-start(bf16[16,7296]{1,0:T(8,128)(2,1)S(1)} %shard_map.114.refs_0_.own_a), channel_id=1, source_target_pairs={{0,4},{1,5},{2,6},{3,7},{4,0},{5,1},{6,2},{7,3},{8,12},{9,13},{10,... | collective-permute-start | bytes 700424 | tf_op jit(solution)/shard_map/ppermute | solution.py:26
  13.6 3.2 %collective-permute-start.4 = (bf16[8,7296]{1,0:T(8,128)(2,1)S(1)}, bf16[8,7296]{1,0:T(8,128)(2,1)S(1)}, u32[]{:S(2)}, u32[]{:S(2)}) collective-permute-start(bf16[8,7296]{1,0:T(8,128)(2,1)S(1)} %shard_map.113.refs_0_), channel_id=1, source_target_pairs={{0,24},{1,25},{2,26},{3,27},{4,28},{5,29},{6,30},{7,31},{8,16},{9,... | collective-permute-start | bytes 350216 | tf_op jit(solution)/shard_map/ppermute | solution.py:26
  16.8 3.4 %collective-permute-done.4.refs_1_ = bf16[8,7296]{1,0:T(8,128)(2,1)S(1)} collective-permute-done((bf16[8,7296]{1,0:T(8,128)(2,1)S(1)}, bf16[8,7296]{1,0:T(8,128)(2,1)S(1)}, u32[]{:S(2)}, u32[]{:S(2)}) %collective-permute-start.4) | collective-permute-done | bytes 116768 | tf_op jit(solution)/shard_map/ppermute | solution.py:26
  20.4 1.6 %copy-done.1 = bf16[7168,256]{1,0:T(8,128)(2,1)} copy-done((bf16[7168,256]{1,0:T(8,128)(2,1)}, bf16[7168,256]{1,0:T(8,128)(2,1)S(1)}, u32[]{:S(2)}) %copy-start.1) | copy-done | bytes 3670040
  22.0 1.5 %collective-permute-start.9 = (bf16[16,7296]{1,0:T(8,128)(2,1)S(1)}, bf16[16,7296]{1,0:T(8,128)(2,1)S(1)}, u32[]{:S(2)}, u32[]{:S(2)}) collective-permute-start(bf16[16,7296]{1,0:T(8,128)(2,1)S(1)} %shard_map.115.refs_5_.own_b), channel_id=1, source_target_pairs={{0,2},{1,3},{2,0},{3,1},{4,6},{5,7},{6,4},{7,5},{8,10},{9,11},{10,... | collective-permute-start | bytes 700424 | tf_op jit(solution)/shard_map/ppermute | solution.py:26
  23.5 1.5 %collective-permute-start.10 = (bf16[16,7296]{1,0:T(8,128)(2,1)S(1)}, bf16[16,7296]{1,0:T(8,128)(2,1)S(1)}, u32[]{:S(2)}, u32[]{:S(2)}) collective-permute-start(bf16[16,7296]{1,0:T(8,128)(2,1)S(1)} %shard_map.115.refs_5_.own_b), channel_id=1, source_target_pairs={{0,4},{1,5},{2,6},{3,7},{4,0},{5,1},{6,2},{7,3},{8,12},{9,13},{10,... | collective-permute-start | bytes 700424 | tf_op jit(solution)/shard_map/ppermute | solution.py:26
  26.8 2.9 %collective-permute-done.9.refs_6_ = bf16[16,7296]{1,0:T(8,128)(2,1)S(1)} collective-permute-done((bf16[16,7296]{1,0:T(8,128)(2,1)S(1)}, bf16[16,7296]{1,0:T(8,128)(2,1)S(1)}, u32[]{:S(2)}, u32[]{:S(2)}) %collective-permute-start.9) | collective-permute-done | bytes 233504 | tf_op jit(solution)/shard_map/ppermute | solution.py:26
  29.8 1.6 %collective-permute-start.11 = (bf16[16,3584]{1,0:T(8,128)(2,1)S(1)}, bf16[16,3584]{1,0:T(8,128)(2,1)S(1)}, u32[]{:S(2)}, u32[]{:S(2)}) collective-permute-start(bf16[16,3584]{1,0:T(8,128)(2,1)S(1)} %slice.32), channel_id=1, source_target_pairs={{0,4},{1,5},{2,6},{3,7},{4,0},{5,1},{6,2},{7,3},{8,12},{9,13},{10,... | collective-permute-start | bytes 344072 | tf_op jit(solution)/shard_map/ppermute | solution.py:26
  34.1 2.3 %shard_map.121 = (bf16[8,2,48,576]{3,2,1,0:T(8,128)(2,1)}, s32[64,128]{1,0:T(8,128)S(1)}) custom-call(bf16[16,7296]{1,0:T(8,128)(2,1)S(1)} %shard_map.114.refs_0_.own_a, bf16[16,7296]{1,0:T(8,128)(2,1)S(1)} %collective-permute-done.2.refs_2_.y_a, bf16[16,7296]{1,0:T(8,128)(2,1)S(1)} %shard_map.115.refs_5_.own_b, ...), custom_call_target="tpu_custom_call" | custom-call | bytes 884736 | tf_op jit(solution)/shard_map/pallas_call | solution.py:251
  36.4 4.2 %all-to-all-start = ((bf16[8,2,48,576]{3,2,1,0:T(8,128)(2,1)}), bf16[8,2,48,576]{3,2,1,0:T(8,128)(2,1)S(1)}, u32[]{:S(2)}, u32[]{:S(2)}) async-start(bf16[8,2,48,576]{3,2,1,0:T(8,128)(2,1)} %get-tuple-element.47), calls=%async_computation | async-start | bytes 1966080 | tf_op jit(solution)/shard_map/all_to_all | solution.py:320
  40.7 8.2 %shard_map.116 = (bf16[48,7168]{1,0:T(8,128)(2,1)S(1)}, bf16[16,7168]{1,0:T(8,128)(2,1)S(1)}, bf16[48,7168]{1,0:T(8,128)(2,1)S(1)}, bf16[16,7168]{1,0:T(8,128)(2,1)S(1)}) custom-call(bf16[16,7296]{1,0:T(8,128)(2,1)S(1)} %shard_map.114.refs_0_.own_a, bf16[16,7296]{1,0:T(8,128)(2,1)S(1)} %collective-permute-done.1.refs_1_, ...), custom_call_target="tpu_custom_call" | custom-call | flops 2818572288 | bytes 23879680 | tf_op jit(solution)/shard_map/pallas_call | solution.py:46
  49.0 1.6 %collective-permute-start.19 = (bf16[16,3584]{1,0:T(8,128)(2,1)S(1)}, bf16[16,3584]{1,0:T(8,128)(2,1)S(1)}, u32[]{:S(2)}, u32[]{:S(2)}) collective-permute-start(bf16[16,3584]{1,0:T(8,128)(2,1)S(1)} %get-tuple-element.55), channel_id=1, source_target_pairs={{0,2},{1,3},{2,0},{3,1},{4,6},{5,7},{6,4},{7,5},{8,10},{9,11},{10,... | collective-permute-start | bytes 344072 | tf_op jit(solution)/shard_map/ppermute | solution.py:26
  50.6 2.0 %collective-permute-start.20 = (bf16[16,3584]{1,0:T(8,128)(2,1)S(1)}, bf16[16,3584]{1,0:T(8,128)(2,1)S(1)}, u32[]{:S(2)}, u32[]{:S(2)}) collective-permute-start(bf16[16,3584]{1,0:T(8,128)(2,1)S(1)} %get-tuple-element.54), channel_id=1, source_target_pairs={{0,4},{1,5},{2,6},{3,7},{4,0},{5,1},{6,2},{7,3},{8,12},{9,13},{10,... | collective-permute-start | bytes 344072 | tf_op jit(solution)/shard_map/ppermute | solution.py:26
  53.8 3.5 %collective-permute-done.20.got_b = bf16[16,3584]{1,0:T(8,128)(2,1)S(1)} collective-permute-done((bf16[16,3584]{1,0:T(8,128)(2,1)S(1)}, bf16[16,3584]{1,0:T(8,128)(2,1)S(1)}, u32[]{:S(2)}, u32[]{:S(2)}) %collective-permute-start.20) | collective-permute-done | bytes 114720 | tf_op jit(solution)/shard_map/ppermute | solution.py:26
  61.0 1.9 %collective-permute-start.17 = (bf16[16,7168]{1,0:T(8,128)(2,1)S(1)}, bf16[16,7168]{1,0:T(8,128)(2,1)S(1)}, u32[]{:S(2)}, u32[]{:S(2)}) collective-permute-start(bf16[16,7168]{1,0:T(8,128)(2,1)S(1)} %get-tuple-element.36), channel_id=1, source_target_pairs={{0,4},{1,5},{2,6},{3,7},{4,0},{5,1},{6,2},{7,3},{8,12},{9,13},{10,... | collective-permute-start | bytes 688136 | tf_op jit(solution)/shard_map/ppermute | solution.py:26
  63.6 1.8 %collective-permute-done.22.back_y = bf16[16,7168]{1,0:T(8,128)(2,1)S(1)} collective-permute-done((bf16[16,7168]{1,0:T(8,128)(2,1)S(1)}, bf16[16,7168]{1,0:T(8,128)(2,1)S(1)}, u32[]{:S(2)}, u32[]{:S(2)}) %collective-permute-start.22) | collective-permute-done | bytes 229408 | tf_op jit(solution)/shard_map/ppermute | solution.py:26
  65.4 2.6 %collective-permute-start.24 = (bf16[8,7168]{1,0:T(8,128)(2,1)S(1)}, bf16[8,7168]{1,0:T(8,128)(2,1)S(1)}, u32[]{:S(2)}, u32[]{:S(2)}) collective-permute-start(bf16[8,7168]{1,0:T(8,128)(2,1)S(1)} %get-tuple-element.45), channel_id=1, source_target_pairs={{0,24},{1,25},{2,26},{3,27},{4,28},{5,29},{6,30},{7,31},{8,16},{9,... | collective-permute-start | bytes 344072 | tf_op jit(solution)/shard_map/ppermute | solution.py:26
  68.7 1.4 %collective-permute-start.18 = (bf16[8,7168]{1,0:T(8,128)(2,1)S(1)}, bf16[8,7168]{1,0:T(8,128)(2,1)S(1)}, u32[]{:S(2)}, u32[]{:S(2)}) collective-permute-start(bf16[8,7168]{1,0:T(8,128)(2,1)S(1)} %get-tuple-element.38), channel_id=1, source_target_pairs={{0,8},{1,9},{2,10},{3,11},{4,12},{5,13},{6,14},{7,15},{8,0},{9,1},... | collective-permute-start | bytes 344072 | tf_op jit(solution)/shard_map/ppermute | solution.py:26
  70.1 2.0 %shard_map.122 = bf16[8,48,576]{2,1,0:T(8,128)(2,1)} custom-call(s32[64,128]{1,0:T(8,128)S(1)} %get-tuple-element.46.refs_0_, f32[8,1,576]{2,1,0:T(1,128)S(1)} %reshape.12.refs_1_, bf16[8,2,48,576]{3,2,1,0:T(8,128)(2,1)S(1)} %all-to-all-done.refs_2_), custom_call_target="tpu_custom_call" | custom-call | bytes 884736 | tf_op jit(solution)/shard_map/pallas_call | solution.py:267
  72.2 2.8 %collective-permute-done.23 = bf16[8,7168]{1,0:T(8,128)(2,1)S(1)} collective-permute-done((bf16[8,7168]{1,0:T(8,128)(2,1)S(1)}, bf16[8,7168]{1,0:T(8,128)(2,1)S(1)}, u32[]{:S(2)}, u32[]{:S(2)}) %collective-permute-start.23) | collective-permute-done | bytes 114720 | tf_op jit(solution)/shard_map/ppermute | solution.py:26
  (59 shorter events, 13.3 us)
Async XLA Ops:
  0.6 19.6 %collective-permute-start.5 = (bf16[7168,256]{1,0:T(8,128)(2,1)}, bf16[7168,256]{1,0:T(8,128)(2,1)S(1)}, u32[]{:S(2)}, u32[]{:S(2)}) collective-permute-start(bf16[7168,256]{1,0:T(8,128)(2,1)} %refs_10_.1), channel_id=1, source_target_pairs={{0,1},{1,0},{2,3},{3,2},{4,5},{5,4},{6,7},{7,6},{8,9},{9,8},{10,11... | collective-permute-start | bytes 11010056 | tf_op jit(solution)/shard_map/ppermute | solution.py:26
  1.1 19.1 %collective-permute-start.6 = (bf16[7168,256]{1,0:T(8,128)(2,1)}, bf16[7168,256]{1,0:T(8,128)(2,1)S(1)}, u32[]{:S(2)}, u32[]{:S(2)}) collective-permute-start(bf16[7168,256]{1,0:T(8,128)(2,1)} %refs_11_.1), channel_id=1, source_target_pairs={{0,1},{1,0},{2,3},{3,2},{4,5},{5,4},{6,7},{7,6},{8,9},{9,8},{10,11... | collective-permute-start | bytes 11010056 | tf_op jit(solution)/shard_map/ppermute | solution.py:26
  2.2 8.0 %collective-permute-start = (bf16[8,7296]{1,0:T(8,128)(2,1)S(1)}, bf16[8,7296]{1,0:T(8,128)(2,1)S(1)}, u32[]{:S(2)}, u32[]{:S(2)}) collective-permute-start(bf16[8,7296]{1,0:T(8,128)(2,1)S(1)} %shard_map.113.refs_0_), channel_id=1, source_target_pairs={{0,8},{1,9},{2,10},{3,11},{4,12},{5,13},{6,14},{7,15},{8,0},{9,1},... | collective-permute-start | bytes 350216 | tf_op jit(solution)/shard_map/ppermute | solution.py:26
  5.2 8.4 %collective-permute-start.3 = (bf16[8,7296]{1,0:T(8,128)(2,1)S(1)}, bf16[8,7296]{1,0:T(8,128)(2,1)S(1)}, u32[]{:S(2)}, u32[]{:S(2)}) collective-permute-start(bf16[8,7296]{1,0:T(8,128)(2,1)S(1)} %shard_map.113.refs_0_), channel_id=1, source_target_pairs={{0,16},{1,17},{2,18},{3,19},{4,20},{5,21},{6,22},{7,23},{8,24},{9,... | collective-permute-start | bytes 350216 | tf_op jit(solution)/shard_map/ppermute | solution.py:26
  10.2 10.0 %collective-permute-start.1 = (bf16[16,7296]{1,0:T(8,128)(2,1)S(1)}, bf16[16,7296]{1,0:T(8,128)(2,1)S(1)}, u32[]{:S(2)}, u32[]{:S(2)}) collective-permute-start(bf16[16,7296]{1,0:T(8,128)(2,1)S(1)} %shard_map.114.refs_0_.own_a), channel_id=1, source_target_pairs={{0,2},{1,3},{2,0},{3,1},{4,6},{5,7},{6,4},{7,5},{8,10},{9,11},{10,... | collective-permute-start | bytes 700424 | tf_op jit(solution)/shard_map/ppermute | solution.py:26
  12.1 8.1 %collective-permute-start.2 = (bf16[16,7296]{1,0:T(8,128)(2,1)S(1)}, bf16[16,7296]{1,0:T(8,128)(2,1)S(1)}, u32[]{:S(2)}, u32[]{:S(2)}) collective-permute-start(bf16[16,7296]{1,0:T(8,128)(2,1)S(1)} %shard_map.114.refs_0_.own_a), channel_id=1, source_target_pairs={{0,4},{1,5},{2,6},{3,7},{4,0},{5,1},{6,2},{7,3},{8,12},{9,13},{10,... | collective-permute-start | bytes 700424 | tf_op jit(solution)/shard_map/ppermute | solution.py:26
  13.6 6.6 %collective-permute-start.4 = (bf16[8,7296]{1,0:T(8,128)(2,1)S(1)}, bf16[8,7296]{1,0:T(8,128)(2,1)S(1)}, u32[]{:S(2)}, u32[]{:S(2)}) collective-permute-start(bf16[8,7296]{1,0:T(8,128)(2,1)S(1)} %shard_map.113.refs_0_), channel_id=1, source_target_pairs={{0,24},{1,25},{2,26},{3,27},{4,28},{5,29},{6,30},{7,31},{8,16},{9,... | collective-permute-start | bytes 350216 | tf_op jit(solution)/shard_map/ppermute | solution.py:26
  20.3 20.4 %collective-permute-start.13 = (bf16[256,7168]{1,0:T(8,128)(2,1)}, bf16[256,7168]{1,0:T(8,128)(2,1)}, u32[]{:S(2)}, u32[]{:S(2)}) collective-permute-start(bf16[256,7168]{1,0:T(8,128)(2,1)} %refs_12_.1), channel_id=1, source_target_pairs={{0,1},{1,0},{2,3},{3,2},{4,5},{5,4},{6,7},{7,6},{8,9},{9,8},{10,11... | collective-permute-start | bytes 11010056 | tf_op jit(solution)/shard_map/ppermute | solution.py:26
  22.0 7.8 %collective-permute-start.9 = (bf16[16,7296]{1,0:T(8,128)(2,1)S(1)}, bf16[16,7296]{1,0:T(8,128)(2,1)S(1)}, u32[]{:S(2)}, u32[]{:S(2)}) collective-permute-start(bf16[16,7296]{1,0:T(8,128)(2,1)S(1)} %shard_map.115.refs_5_.own_b), channel_id=1, source_target_pairs={{0,2},{1,3},{2,0},{3,1},{4,6},{5,7},{6,4},{7,5},{8,10},{9,11},{10,... | collective-permute-start | bytes 700424 | tf_op jit(solution)/shard_map/ppermute | solution.py:26
  23.5 8.6 %collective-permute-start.10 = (bf16[16,7296]{1,0:T(8,128)(2,1)S(1)}, bf16[16,7296]{1,0:T(8,128)(2,1)S(1)}, u32[]{:S(2)}, u32[]{:S(2)}) collective-permute-start(bf16[16,7296]{1,0:T(8,128)(2,1)S(1)} %shard_map.115.refs_5_.own_b), channel_id=1, source_target_pairs={{0,4},{1,5},{2,6},{3,7},{4,0},{5,1},{6,2},{7,3},{8,12},{9,13},{10,... | collective-permute-start | bytes 700424 | tf_op jit(solution)/shard_map/ppermute | solution.py:26
  25.0 15.6 %collective-permute-start.7 = (bf16[16,3584]{1,0:T(8,128)(2,1)S(1)}, bf16[16,3584]{1,0:T(8,128)(2,1)S(1)}, u32[]{:S(2)}, u32[]{:S(2)}) collective-permute-start(bf16[16,3584]{1,0:T(8,128)(2,1)S(1)} %slice.24), channel_id=1, source_target_pairs={{0,4},{1,5},{2,6},{3,7},{4,0},{5,1},{6,2},{7,3},{8,12},{9,13},{10,... | collective-permute-start | bytes 344072 | tf_op jit(solution)/shard_map/ppermute | solution.py:26
  25.6 15.0 %collective-permute-start.8 = (bf16[16,3584]{1,0:T(8,128)(2,1)S(1)}, bf16[16,3584]{1,0:T(8,128)(2,1)S(1)}, u32[]{:S(2)}, u32[]{:S(2)}) collective-permute-start(bf16[16,3584]{1,0:T(8,128)(2,1)S(1)} %slice.25), channel_id=1, source_target_pairs={{0,2},{1,3},{2,0},{3,1},{4,6},{5,7},{6,4},{7,5},{8,10},{9,11},{10,... | collective-permute-start | bytes 344072 | tf_op jit(solution)/shard_map/ppermute | solution.py:26
  29.8 10.9 %collective-permute-start.11 = (bf16[16,3584]{1,0:T(8,128)(2,1)S(1)}, bf16[16,3584]{1,0:T(8,128)(2,1)S(1)}, u32[]{:S(2)}, u32[]{:S(2)}) collective-permute-start(bf16[16,3584]{1,0:T(8,128)(2,1)S(1)} %slice.32), channel_id=1, source_target_pairs={{0,4},{1,5},{2,6},{3,7},{4,0},{5,1},{6,2},{7,3},{8,12},{9,13},{10,... | collective-permute-start | bytes 344072 | tf_op jit(solution)/shard_map/ppermute | solution.py:26
  32.1 8.5 %collective-permute-start.12 = (bf16[16,3584]{1,0:T(8,128)(2,1)S(1)}, bf16[16,3584]{1,0:T(8,128)(2,1)S(1)}, u32[]{:S(2)}, u32[]{:S(2)}) collective-permute-start(bf16[16,3584]{1,0:T(8,128)(2,1)S(1)} %slice.33), channel_id=1, source_target_pairs={{0,2},{1,3},{2,0},{3,1},{4,6},{5,7},{6,4},{7,5},{8,10},{9,11},{10,... | collective-permute-start | bytes 344072 | tf_op jit(solution)/shard_map/ppermute | solution.py:26
  36.4 33.7 %all-to-all-start = ((bf16[8,2,48,576]{3,2,1,0:T(8,128)(2,1)}), bf16[8,2,48,576]{3,2,1,0:T(8,128)(2,1)S(1)}, u32[]{:S(2)}, u32[]{:S(2)}) async-start(bf16[8,2,48,576]{3,2,1,0:T(8,128)(2,1)} %get-tuple-element.47), calls=%async_computation | async-start | bytes 1966080 | tf_op jit(solution)/shard_map/all_to_all | solution.py:320
  50.6 6.8 %collective-permute-start.20 = (bf16[16,3584]{1,0:T(8,128)(2,1)S(1)}, bf16[16,3584]{1,0:T(8,128)(2,1)S(1)}, u32[]{:S(2)}, u32[]{:S(2)}) collective-permute-start(bf16[16,3584]{1,0:T(8,128)(2,1)S(1)} %get-tuple-element.54), channel_id=1, source_target_pairs={{0,4},{1,5},{2,6},{3,7},{4,0},{5,1},{6,2},{7,3},{8,12},{9,13},{10,... | collective-permute-start | bytes 344072 | tf_op jit(solution)/shard_map/ppermute | solution.py:26
  52.7 6.5 %collective-permute-start.14 = (bf16[16,3584]{1,0:T(8,128)(2,1)S(1)}, bf16[16,3584]{1,0:T(8,128)(2,1)S(1)}, u32[]{:S(2)}, u32[]{:S(2)}) collective-permute-start(bf16[16,3584]{1,0:T(8,128)(2,1)S(1)} %get-tuple-element.53), channel_id=1, source_target_pairs={{0,2},{1,3},{2,0},{3,1},{4,6},{5,7},{6,4},{7,5},{8,10},{9,11},{10,... | collective-permute-start | bytes 344072 | tf_op jit(solution)/shard_map/ppermute | solution.py:26
  53.2 6.8 %collective-permute-start.15 = (bf16[16,3584]{1,0:T(8,128)(2,1)S(1)}, bf16[16,3584]{1,0:T(8,128)(2,1)S(1)}, u32[]{:S(2)}, u32[]{:S(2)}) collective-permute-start(bf16[16,3584]{1,0:T(8,128)(2,1)S(1)} %get-tuple-element.52), channel_id=1, source_target_pairs={{0,4},{1,5},{2,6},{3,7},{4,0},{5,1},{6,2},{7,3},{8,12},{9,13},{10,... | collective-permute-start | bytes 344072 | tf_op jit(solution)/shard_map/ppermute | solution.py:26
  58.1 7.2 %collective-permute-start.22 = (bf16[16,7168]{1,0:T(8,128)(2,1)S(1)}, bf16[16,7168]{1,0:T(8,128)(2,1)S(1)}, u32[]{:S(2)}, u32[]{:S(2)}) collective-permute-start(bf16[16,7168]{1,0:T(8,128)(2,1)S(1)} %get-tuple-element.43), channel_id=1, source_target_pairs={{0,4},{1,5},{2,6},{3,7},{4,0},{5,1},{6,2},{7,3},{8,12},{9,13},{10,... | collective-permute-start | bytes 688136 | tf_op jit(solution)/shard_map/ppermute | solution.py:26
  60.1 8.5 %collective-permute-start.16 = (bf16[16,7168]{1,0:T(8,128)(2,1)S(1)}, bf16[16,7168]{1,0:T(8,128)(2,1)S(1)}, u32[]{:S(2)}, u32[]{:S(2)}) collective-permute-start(bf16[16,7168]{1,0:T(8,128)(2,1)S(1)} %get-tuple-element.35), channel_id=1, source_target_pairs={{0,2},{1,3},{2,0},{3,1},{4,6},{5,7},{6,4},{7,5},{8,10},{9,11},{10,... | collective-permute-start | bytes 688136 | tf_op jit(solution)/shard_map/ppermute | solution.py:26
  61.0 7.5 %collective-permute-start.17 = (bf16[16,7168]{1,0:T(8,128)(2,1)S(1)}, bf16[16,7168]{1,0:T(8,128)(2,1)S(1)}, u32[]{:S(2)}, u32[]{:S(2)}) collective-permute-start(bf16[16,7168]{1,0:T(8,128)(2,1)S(1)} %get-tuple-element.36), channel_id=1, source_target_pairs={{0,4},{1,5},{2,6},{3,7},{4,0},{5,1},{6,2},{7,3},{8,12},{9,13},{10,... | collective-permute-start | bytes 688136 | tf_op jit(solution)/shard_map/ppermute | solution.py:26
  65.4 6.8 %collective-permute-start.24 = (bf16[8,7168]{1,0:T(8,128)(2,1)S(1)}, bf16[8,7168]{1,0:T(8,128)(2,1)S(1)}, u32[]{:S(2)}, u32[]{:S(2)}) collective-permute-start(bf16[8,7168]{1,0:T(8,128)(2,1)S(1)} %get-tuple-element.45), channel_id=1, source_target_pairs={{0,24},{1,25},{2,26},{3,27},{4,28},{5,29},{6,30},{7,31},{8,16},{9,... | collective-permute-start | bytes 344072 | tf_op jit(solution)/shard_map/ppermute | solution.py:26
  68.0 7.0 %collective-permute-start.23 = (bf16[8,7168]{1,0:T(8,128)(2,1)S(1)}, bf16[8,7168]{1,0:T(8,128)(2,1)S(1)}, u32[]{:S(2)}, u32[]{:S(2)}) collective-permute-start(bf16[8,7168]{1,0:T(8,128)(2,1)S(1)} %get-tuple-element.44), channel_id=1, source_target_pairs={{0,16},{1,17},{2,18},{3,19},{4,20},{5,21},{6,22},{7,23},{8,24},{9,... | collective-permute-start | bytes 344072 | tf_op jit(solution)/shard_map/ppermute | solution.py:26
  68.7 6.4 %collective-permute-start.18 = (bf16[8,7168]{1,0:T(8,128)(2,1)S(1)}, bf16[8,7168]{1,0:T(8,128)(2,1)S(1)}, u32[]{:S(2)}, u32[]{:S(2)}) collective-permute-start(bf16[8,7168]{1,0:T(8,128)(2,1)S(1)} %get-tuple-element.38), channel_id=1, source_target_pairs={{0,8},{1,9},{2,10},{3,11},{4,12},{5,13},{6,14},{7,15},{8,0},{9,1},... | collective-permute-start | bytes 344072 | tf_op jit(solution)/shard_map/ppermute | solution.py:26
  (8 other events, 80.4 us)

commit v5 on v4

--- a/solution.py
+++ b/solution.py
@@ -209,10 +209,13 @@
     return lax.div(lax.axis_index("ep"), lax.axis_size("ep") // BEAMS)
 
 
-def packing_kernel(own_a, y_a, own_b, y_b, cache, out, facts, scalars, sem):
+def packing_kernel(own_a, y_a, own_b, y_b, cache, out, facts, scalars, held, sem, cache_sem):
+    fetch = pltpu.make_async_copy(cache, held, cache_sem)
+    fetch.start()
     read_facts([own_a, y_a, own_b, y_b], facts, scalars, sem)
     rows = cache.shape[0]
     beam = own_beam()
+    fetch.wait()
     for place in range(BEAMS):
         at = fact_row(place, own_a.shape[0], rows)
         first = second = count = jnp.int32(0)
@@ -222,7 +225,7 @@
             second = jnp.where(hit & (count == 1), row, second)
             count = count + hit.astype(jnp.int32)
         for rank, pick in enumerate((first, second)):
-            out[beam ^ place, rank] = cache[pick]
+            out[beam ^ place, rank] = held[pick]
 
 
 def unpacking_kernel(quad, facts, newest, arrived, out, scalars, sem):
@@ -250,16 +253,21 @@
     table = (len(blocks) * blocks[0].shape[0], LANES)
     return pl.pallas_call(
         packing_kernel,
-        in_specs=[whole] * (len(blocks) + 1),
+        in_specs=[whole] * len(blocks) + [pl.BlockSpec(memory_space=pltpu.HBM)],
         out_specs=[whole] * 2,
         out_shape=[
             jax.ShapeDtypeStruct((BEAMS, CAP) + cache.shape[1:], cache.dtype),
             pltpu.VMEM(table, jnp.int32),
         ],
-        scratch_shapes=[pltpu.SMEM(table, jnp.int32), pltpu.SemaphoreType.DMA],
+        scratch_shapes=[
+            pltpu.SMEM(table, jnp.int32),
+            pltpu.VMEM(cache.shape, cache.dtype),
+            pltpu.SemaphoreType.DMA,
+            pltpu.SemaphoreType.DMA,
+        ],
         compiler_params=pltpu.CompilerParams(vmem_limit_bytes=4 * MIB),
         cost_estimate=pl.CostEstimate(flops=0, bytes_accessed=4 * cache.size, transcendentals=0),
-    )(*[in_vmem(b) for b in blocks], in_vmem(cache))
+    )(*[in_vmem(b) for b in blocks], in_hbm(cache))
 
 
 def unpacking_call(facts, quad, newest, arrived, shape):

time: 76.1 us -> 75 us (0.986)
  local copies, waits for them, and re-layouts: 2.77 us -> 1.75 us
    unnamed x12 -> x10, local copies, waits for them, and re-layouts: 2.69 us -> 1.67 us
  transfers between devices with their start and end apart: 26 -> 26, of which waited for: 10 -> 10; matrix products, arithmetic and copies ran while one was open for 0% -> 0% of each run, Pallas kernels for 18% -> 19%
where the time goes in v5:
time: 75 us; the launch traced here: 74.8 us
  starting transfers between devices  37.7 us (50%)
  waiting for transfers between devices  19.8 us (26%)
  Pallas kernels  13.8 us (18%)
  local copies, waits for them, and re-layouts  1.75 us (2%)
  between operations  0.86 us (1%)
  other arithmetic  0.83 us (1%)
    ppermute x25, starting transfers between devices, swapped(): return lax.ppermute(value, 'ep', [(i, i ^ mask) for i in range(peers)])  33.5 us
    ppermute x25, waiting for transfers between devices, swapped(): return lax.ppermute(value, 'ep', [(i, i ^ mask) for i in range(peers)])  19.8 us
    pallas_call x7, Pallas kernels, whole_call(): pl.pallas_call(body, in_specs=[far if isinstance(a, tuple) else whole for...  8.61 us
    all_to_all x1, starting transfers between devices, dense_local(): lax.all_to_all(packets, 'ep', split_axis=0, concat_axis=0, axis_index_gro...  4.25 us
    pallas_call x1, Pallas kernels, packing_call(): pl.pallas_call(packing_kernel, in_specs=[whole] * len(blocks) + [pl.Block...  2.27 us
    pallas_call x1, Pallas kernels, unpacking_call(): pl.pallas_call(lambda *refs: unpacking_kernel(quad, *refs), in_specs=[who...  2.03 us
    unnamed x10, local copies, waits for them, and re-layouts  1.67 us
  transfers between devices with their start and end apart: 26, of which 10 were waited for; matrix products, arithmetic and copies ran while one was open for 0% of the time, Pallas kernels for 19%

profile of v5, /device:TPU:0, one launch (start us, length us, event | category | flops | bytes accessed | tf_op | source)
XLA Modules:
  0.0 74.8 jit_solution(7191347180574880240)
XLA Ops:
  2.2 3.1 %collective-permute-start = (bf16[8,7296]{1,0:T(8,128)(2,1)S(1)}, bf16[8,7296]{1,0:T(8,128)(2,1)S(1)}, u32[]{:S(2)}, u32[]{:S(2)}) collective-permute-start(bf16[8,7296]{1,0:T(8,128)(2,1)S(1)} %shard_map.113.refs_0_), channel_id=1, source_target_pairs={{0,8},{1,9},{2,10},{3,11},{4,12},{5,13},{6,14},{7,15},{8,0},{9,1},... | collective-permute-start | bytes 350216 | tf_op jit(solution)/shard_map/ppermute | solution.py:26
  5.2 2.6 %collective-permute-start.3 = (bf16[8,7296]{1,0:T(8,128)(2,1)S(1)}, bf16[8,7296]{1,0:T(8,128)(2,1)S(1)}, u32[]{:S(2)}, u32[]{:S(2)}) collective-permute-start(bf16[8,7296]{1,0:T(8,128)(2,1)S(1)} %shard_map.113.refs_0_), channel_id=1, source_target_pairs={{0,16},{1,17},{2,18},{3,19},{4,20},{5,21},{6,22},{7,23},{8,24},{9,... | collective-permute-start | bytes 350216 | tf_op jit(solution)/shard_map/ppermute | solution.py:26
  7.8 2.3 %collective-permute-done.refs_1_ = bf16[8,7296]{1,0:T(8,128)(2,1)S(1)} collective-permute-done((bf16[8,7296]{1,0:T(8,128)(2,1)S(1)}, bf16[8,7296]{1,0:T(8,128)(2,1)S(1)}, u32[]{:S(2)}, u32[]{:S(2)}) %collective-permute-start) | collective-permute-done | bytes 116768 | tf_op jit(solution)/shard_map/ppermute | solution.py:26
  10.2 1.9 %collective-permute-start.1 = (bf16[16,7296]{1,0:T(8,128)(2,1)S(1)}, bf16[16,7296]{1,0:T(8,128)(2,1)S(1)}, u32[]{:S(2)}, u32[]{:S(2)}) collective-permute-start(bf16[16,7296]{1,0:T(8,128)(2,1)S(1)} %shard_map.114.refs_0_.own_a), channel_id=1, source_target_pairs={{0,2},{1,3},{2,0},{3,1},{4,6},{5,7},{6,4},{7,5},{8,10},{9,11},{10,... | collective-permute-start | bytes 700424 | tf_op jit(solution)/shard_map/ppermute | solution.py:26
  12.1 1.5 %collective-permute-start.2 = (bf16[16,7296]{1,0:T(8,128)(2,1)S(1)}, bf16[16,7296]{1,0:T(8,128)(2,1)S(1)}, u32[]{:S(2)}, u32[]{:S(2)}) collective-permute-start(bf16[16,7296]{1,0:T(8,128)(2,1)S(1)} %shard_map.114.refs_0_.own_a), channel_id=1, source_target_pairs={{0,4},{1,5},{2,6},{3,7},{4,0},{5,1},{6,2},{7,3},{8,12},{9,13},{10,... | collective-permute-start | bytes 700424 | tf_op jit(solution)/shard_map/ppermute | solution.py:26
  13.6 3.2 %collective-permute-start.4 = (bf16[8,7296]{1,0:T(8,128)(2,1)S(1)}, bf16[8,7296]{1,0:T(8,128)(2,1)S(1)}, u32[]{:S(2)}, u32[]{:S(2)}) collective-permute-start(bf16[8,7296]{1,0:T(8,128)(2,1)S(1)} %shard_map.113.refs_0_), channel_id=1, source_target_pairs={{0,24},{1,25},{2,26},{3,27},{4,28},{5,29},{6,30},{7,31},{8,16},{9,... | collective-permute-start | bytes 350216 | tf_op jit(solution)/shard_map/ppermute | solution.py:26
  16.8 3.4 %collective-permute-done.4.refs_1_ = bf16[8,7296]{1,0:T(8,128)(2,1)S(1)} collective-permute-done((bf16[8,7296]{1,0:T(8,128)(2,1)S(1)}, bf16[8,7296]{1,0:T(8,128)(2,1)S(1)}, u32[]{:S(2)}, u32[]{:S(2)}) %collective-permute-start.4) | collective-permute-done | bytes 116768 | tf_op jit(solution)/shard_map/ppermute | solution.py:26
  20.4 1.6 %copy-done = bf16[7168,256]{1,0:T(8,128)(2,1)} copy-done((bf16[7168,256]{1,0:T(8,128)(2,1)}, bf16[7168,256]{1,0:T(8,128)(2,1)S(1)}, u32[]{:S(2)}) %copy-start) | copy-done | bytes 3670040
  22.0 1.5 %collective-permute-start.9 = (bf16[16,7296]{1,0:T(8,128)(2,1)S(1)}, bf16[16,7296]{1,0:T(8,128)(2,1)S(1)}, u32[]{:S(2)}, u32[]{:S(2)}) collective-permute-start(bf16[16,7296]{1,0:T(8,128)(2,1)S(1)} %shard_map.115.refs_5_.own_b), channel_id=1, source_target_pairs={{0,2},{1,3},{2,0},{3,1},{4,6},{5,7},{6,4},{7,5},{8,10},{9,11},{10,... | collective-permute-start | bytes 700424 | tf_op jit(solution)/shard_map/ppermute | solution.py:26
  23.5 1.5 %collective-permute-start.10 = (bf16[16,7296]{1,0:T(8,128)(2,1)S(1)}, bf16[16,7296]{1,0:T(8,128)(2,1)S(1)}, u32[]{:S(2)}, u32[]{:S(2)}) collective-permute-start(bf16[16,7296]{1,0:T(8,128)(2,1)S(1)} %shard_map.115.refs_5_.own_b), channel_id=1, source_target_pairs={{0,4},{1,5},{2,6},{3,7},{4,0},{5,1},{6,2},{7,3},{8,12},{9,13},{10,... | collective-permute-start | bytes 700424 | tf_op jit(solution)/shard_map/ppermute | solution.py:26
  26.8 2.9 %collective-permute-done.9.refs_6_ = bf16[16,7296]{1,0:T(8,128)(2,1)S(1)} collective-permute-done((bf16[16,7296]{1,0:T(8,128)(2,1)S(1)}, bf16[16,7296]{1,0:T(8,128)(2,1)S(1)}, u32[]{:S(2)}, u32[]{:S(2)}) %collective-permute-start.9) | collective-permute-done | bytes 233504 | tf_op jit(solution)/shard_map/ppermute | solution.py:26
  29.8 1.6 %collective-permute-start.11 = (bf16[16,3584]{1,0:T(8,128)(2,1)S(1)}, bf16[16,3584]{1,0:T(8,128)(2,1)S(1)}, u32[]{:S(2)}, u32[]{:S(2)}) collective-permute-start(bf16[16,3584]{1,0:T(8,128)(2,1)S(1)} %slice.32), channel_id=1, source_target_pairs={{0,4},{1,5},{2,6},{3,7},{4,0},{5,1},{6,2},{7,3},{8,12},{9,13},{10,... | collective-permute-start | bytes 344072 | tf_op jit(solution)/shard_map/ppermute | solution.py:26
  33.1 2.3 %shard_map.121 = (bf16[8,2,48,576]{3,2,1,0:T(8,128)(2,1)}, s32[64,128]{1,0:T(8,128)S(1)}) custom-call(bf16[16,7296]{1,0:T(8,128)(2,1)S(1)} %shard_map.114.refs_0_.own_a, bf16[16,7296]{1,0:T(8,128)(2,1)S(1)} %collective-permute-done.2.refs_2_.y_a, bf16[16,7296]{1,0:T(8,128)(2,1)S(1)} %shard_map.115.refs_5_.own_b, ...), custom_call_target="tpu_custom_call" | custom-call | bytes 884736 | tf_op jit(solution)/shard_map/pallas_call | solution.py:254
  35.4 4.2 %all-to-all-start = ((bf16[8,2,48,576]{3,2,1,0:T(8,128)(2,1)}), bf16[8,2,48,576]{3,2,1,0:T(8,128)(2,1)S(1)}, u32[]{:S(2)}, u32[]{:S(2)}) async-start(bf16[8,2,48,576]{3,2,1,0:T(8,128)(2,1)} %get-tuple-element.47), calls=%async_computation | async-start | bytes 1966080 | tf_op jit(solution)/shard_map/all_to_all | solution.py:328
  39.7 8.2 %shard_map.116 = (bf16[48,7168]{1,0:T(8,128)(2,1)S(1)}, bf16[16,7168]{1,0:T(8,128)(2,1)S(1)}, bf16[48,7168]{1,0:T(8,128)(2,1)S(1)}, bf16[16,7168]{1,0:T(8,128)(2,1)S(1)}) custom-call(bf16[16,7296]{1,0:T(8,128)(2,1)S(1)} %shard_map.114.refs_0_.own_a, bf16[16,7296]{1,0:T(8,128)(2,1)S(1)} %collective-permute-done.1.refs_1_, ...), custom_call_target="tpu_custom_call" | custom-call | flops 2818572288 | bytes 23879680 | tf_op jit(solution)/shard_map/pallas_call | solution.py:46
  48.0 1.7 %collective-permute-start.19 = (bf16[16,3584]{1,0:T(8,128)(2,1)S(1)}, bf16[16,3584]{1,0:T(8,128)(2,1)S(1)}, u32[]{:S(2)}, u32[]{:S(2)}) collective-permute-start(bf16[16,3584]{1,0:T(8,128)(2,1)S(1)} %get-tuple-element.55), channel_id=1, source_target_pairs={{0,2},{1,3},{2,0},{3,1},{4,6},{5,7},{6,4},{7,5},{8,10},{9,11},{10,... | collective-permute-start | bytes 344072 | tf_op jit(solution)/shard_map/ppermute | solution.py:26
  49.6 2.0 %collective-permute-start.20 = (bf16[16,3584]{1,0:T(8,128)(2,1)S(1)}, bf16[16,3584]{1,0:T(8,128)(2,1)S(1)}, u32[]{:S(2)}, u32[]{:S(2)}) collective-permute-start(bf16[16,3584]{1,0:T(8,128)(2,1)S(1)} %get-tuple-element.54), channel_id=1, source_target_pairs={{0,4},{1,5},{2,6},{3,7},{4,0},{5,1},{6,2},{7,3},{8,12},{9,13},{10,... | collective-permute-start | bytes 344072 | tf_op jit(solution)/shard_map/ppermute | solution.py:26
  52.8 3.6 %collective-permute-done.20.got_b = bf16[16,3584]{1,0:T(8,128)(2,1)S(1)} collective-permute-done((bf16[16,3584]{1,0:T(8,128)(2,1)S(1)}, bf16[16,3584]{1,0:T(8,128)(2,1)S(1)}, u32[]{:S(2)}, u32[]{:S(2)}) %collective-permute-start.20) | collective-permute-done | bytes 114720 | tf_op jit(solution)/shard_map/ppermute | solution.py:26
  60.0 1.9 %collective-permute-start.17 = (bf16[16,7168]{1,0:T(8,128)(2,1)S(1)}, bf16[16,7168]{1,0:T(8,128)(2,1)S(1)}, u32[]{:S(2)}, u32[]{:S(2)}) collective-permute-start(bf16[16,7168]{1,0:T(8,128)(2,1)S(1)} %get-tuple-element.36), channel_id=1, source_target_pairs={{0,4},{1,5},{2,6},{3,7},{4,0},{5,1},{6,2},{7,3},{8,12},{9,13},{10,... | collective-permute-start | bytes 688136 | tf_op jit(solution)/shard_map/ppermute | solution.py:26
  62.6 1.8 %collective-permute-done.22.back_y = bf16[16,7168]{1,0:T(8,128)(2,1)S(1)} collective-permute-done((bf16[16,7168]{1,0:T(8,128)(2,1)S(1)}, bf16[16,7168]{1,0:T(8,128)(2,1)S(1)}, u32[]{:S(2)}, u32[]{:S(2)}) %collective-permute-start.22) | collective-permute-done | bytes 229408 | tf_op jit(solution)/shard_map/ppermute | solution.py:26
  64.4 2.6 %collective-permute-start.24 = (bf16[8,7168]{1,0:T(8,128)(2,1)S(1)}, bf16[8,7168]{1,0:T(8,128)(2,1)S(1)}, u32[]{:S(2)}, u32[]{:S(2)}) collective-permute-start(bf16[8,7168]{1,0:T(8,128)(2,1)S(1)} %get-tuple-element.45), channel_id=1, source_target_pairs={{0,24},{1,25},{2,26},{3,27},{4,28},{5,29},{6,30},{7,31},{8,16},{9,... | collective-permute-start | bytes 344072 | tf_op jit(solution)/shard_map/ppermute | solution.py:26
  67.6 1.4 %collective-permute-start.18 = (bf16[8,7168]{1,0:T(8,128)(2,1)S(1)}, bf16[8,7168]{1,0:T(8,128)(2,1)S(1)}, u32[]{:S(2)}, u32[]{:S(2)}) collective-permute-start(bf16[8,7168]{1,0:T(8,128)(2,1)S(1)} %get-tuple-element.38), channel_id=1, source_target_pairs={{0,8},{1,9},{2,10},{3,11},{4,12},{5,13},{6,14},{7,15},{8,0},{9,1},... | collective-permute-start | bytes 344072 | tf_op jit(solution)/shard_map/ppermute | solution.py:26
  69.1 2.0 %shard_map.122 = bf16[8,48,576]{2,1,0:T(8,128)(2,1)} custom-call(s32[64,128]{1,0:T(8,128)S(1)} %get-tuple-element.46.refs_0_, f32[8,1,576]{2,1,0:T(1,128)S(1)} %reshape.12.refs_1_, bf16[8,2,48,576]{3,2,1,0:T(8,128)(2,1)S(1)} %all-to-all-done.refs_2_), custom_call_target="tpu_custom_call" | custom-call | bytes 884736 | tf_op jit(solution)/shard_map/pallas_call | solution.py:275
  71.2 2.8 %collective-permute-done.23 = bf16[8,7168]{1,0:T(8,128)(2,1)S(1)} collective-permute-done((bf16[8,7168]{1,0:T(8,128)(2,1)S(1)}, bf16[8,7168]{1,0:T(8,128)(2,1)S(1)}, u32[]{:S(2)}, u32[]{:S(2)}) %collective-permute-start.23) | collective-permute-done | bytes 114720 | tf_op jit(solution)/shard_map/ppermute | solution.py:26
  (57 shorter events, 12.3 us)
Async XLA Ops:
  0.6 19.6 %collective-permute-start.5 = (bf16[7168,256]{1,0:T(8,128)(2,1)}, bf16[7168,256]{1,0:T(8,128)(2,1)S(1)}, u32[]{:S(2)}, u32[]{:S(2)}) collective-permute-start(bf16[7168,256]{1,0:T(8,128)(2,1)} %refs_10_.1), channel_id=1, source_target_pairs={{0,1},{1,0},{2,3},{3,2},{4,5},{5,4},{6,7},{7,6},{8,9},{9,8},{10,11... | collective-permute-start | bytes 11010056 | tf_op jit(solution)/shard_map/ppermute | solution.py:26
  1.1 19.1 %collective-permute-start.6 = (bf16[7168,256]{1,0:T(8,128)(2,1)}, bf16[7168,256]{1,0:T(8,128)(2,1)S(1)}, u32[]{:S(2)}, u32[]{:S(2)}) collective-permute-start(bf16[7168,256]{1,0:T(8,128)(2,1)} %refs_11_.1), channel_id=1, source_target_pairs={{0,1},{1,0},{2,3},{3,2},{4,5},{5,4},{6,7},{7,6},{8,9},{9,8},{10,11... | collective-permute-start | bytes 11010056 | tf_op jit(solution)/shard_map/ppermute | solution.py:26
  2.2 8.0 %collective-permute-start = (bf16[8,7296]{1,0:T(8,128)(2,1)S(1)}, bf16[8,7296]{1,0:T(8,128)(2,1)S(1)}, u32[]{:S(2)}, u32[]{:S(2)}) collective-permute-start(bf16[8,7296]{1,0:T(8,128)(2,1)S(1)} %shard_map.113.refs_0_), channel_id=1, source_target_pairs={{0,8},{1,9},{2,10},{3,11},{4,12},{5,13},{6,14},{7,15},{8,0},{9,1},... | collective-permute-start | bytes 350216 | tf_op jit(solution)/shard_map/ppermute | solution.py:26
  5.2 8.4 %collective-permute-start.3 = (bf16[8,7296]{1,0:T(8,128)(2,1)S(1)}, bf16[8,7296]{1,0:T(8,128)(2,1)S(1)}, u32[]{:S(2)}, u32[]{:S(2)}) collective-permute-start(bf16[8,7296]{1,0:T(8,128)(2,1)S(1)} %shard_map.113.refs_0_), channel_id=1, source_target_pairs={{0,16},{1,17},{2,18},{3,19},{4,20},{5,21},{6,22},{7,23},{8,24},{9,... | collective-permute-start | bytes 350216 | tf_op jit(solution)/shard_map/ppermute | solution.py:26
  10.2 10.0 %collective-permute-start.1 = (bf16[16,7296]{1,0:T(8,128)(2,1)S(1)}, bf16[16,7296]{1,0:T(8,128)(2,1)S(1)}, u32[]{:S(2)}, u32[]{:S(2)}) collective-permute-start(bf16[16,7296]{1,0:T(8,128)(2,1)S(1)} %shard_map.114.refs_0_.own_a), channel_id=1, source_target_pairs={{0,2},{1,3},{2,0},{3,1},{4,6},{5,7},{6,4},{7,5},{8,10},{9,11},{10,... | collective-permute-start | bytes 700424 | tf_op jit(solution)/shard_map/ppermute | solution.py:26
  12.1 8.1 %collective-permute-start.2 = (bf16[16,7296]{1,0:T(8,128)(2,1)S(1)}, bf16[16,7296]{1,0:T(8,128)(2,1)S(1)}, u32[]{:S(2)}, u32[]{:S(2)}) collective-permute-start(bf16[16,7296]{1,0:T(8,128)(2,1)S(1)} %shard_map.114.refs_0_.own_a), channel_id=1, source_target_pairs={{0,4},{1,5},{2,6},{3,7},{4,0},{5,1},{6,2},{7,3},{8,12},{9,13},{10,... | collective-permute-start | bytes 700424 | tf_op jit(solution)/shard_map/ppermute | solution.py:26
  13.6 6.6 %collective-permute-start.4 = (bf16[8,7296]{1,0:T(8,128)(2,1)S(1)}, bf16[8,7296]{1,0:T(8,128)(2,1)S(1)}, u32[]{:S(2)}, u32[]{:S(2)}) collective-permute-start(bf16[8,7296]{1,0:T(8,128)(2,1)S(1)} %shard_map.113.refs_0_), channel_id=1, source_target_pairs={{0,24},{1,25},{2,26},{3,27},{4,28},{5,29},{6,30},{7,31},{8,16},{9,... | collective-permute-start | bytes 350216 | tf_op jit(solution)/shard_map/ppermute | solution.py:26
  20.3 19.4 %collective-permute-start.13 = (bf16[256,7168]{1,0:T(8,128)(2,1)}, bf16[256,7168]{1,0:T(8,128)(2,1)}, u32[]{:S(2)}, u32[]{:S(2)}) collective-permute-start(bf16[256,7168]{1,0:T(8,128)(2,1)} %refs_12_.1), channel_id=1, source_target_pairs={{0,1},{1,0},{2,3},{3,2},{4,5},{5,4},{6,7},{7,6},{8,9},{9,8},{10,11... | collective-permute-start | bytes 11010056 | tf_op jit(solution)/shard_map/ppermute | solution.py:26
  22.0 7.7 %collective-permute-start.9 = (bf16[16,7296]{1,0:T(8,128)(2,1)S(1)}, bf16[16,7296]{1,0:T(8,128)(2,1)S(1)}, u32[]{:S(2)}, u32[]{:S(2)}) collective-permute-start(bf16[16,7296]{1,0:T(8,128)(2,1)S(1)} %shard_map.115.refs_5_.own_b), channel_id=1, source_target_pairs={{0,2},{1,3},{2,0},{3,1},{4,6},{5,7},{6,4},{7,5},{8,10},{9,11},{10,... | collective-permute-start | bytes 700424 | tf_op jit(solution)/shard_map/ppermute | solution.py:26
  23.5 8.6 %collective-permute-start.10 = (bf16[16,7296]{1,0:T(8,128)(2,1)S(1)}, bf16[16,7296]{1,0:T(8,128)(2,1)S(1)}, u32[]{:S(2)}, u32[]{:S(2)}) collective-permute-start(bf16[16,7296]{1,0:T(8,128)(2,1)S(1)} %shard_map.115.refs_5_.own_b), channel_id=1, source_target_pairs={{0,4},{1,5},{2,6},{3,7},{4,0},{5,1},{6,2},{7,3},{8,12},{9,13},{10,... | collective-permute-start | bytes 700424 | tf_op jit(solution)/shard_map/ppermute | solution.py:26
  25.0 14.6 %collective-permute-start.7 = (bf16[16,3584]{1,0:T(8,128)(2,1)S(1)}, bf16[16,3584]{1,0:T(8,128)(2,1)S(1)}, u32[]{:S(2)}, u32[]{:S(2)}) collective-permute-start(bf16[16,3584]{1,0:T(8,128)(2,1)S(1)} %slice.24), channel_id=1, source_target_pairs={{0,4},{1,5},{2,6},{3,7},{4,0},{5,1},{6,2},{7,3},{8,12},{9,13},{10,... | collective-permute-start | bytes 344072 | tf_op jit(solution)/shard_map/ppermute | solution.py:26
  25.6 14.0 %collective-permute-start.8 = (bf16[16,3584]{1,0:T(8,128)(2,1)S(1)}, bf16[16,3584]{1,0:T(8,128)(2,1)S(1)}, u32[]{:S(2)}, u32[]{:S(2)}) collective-permute-start(bf16[16,3584]{1,0:T(8,128)(2,1)S(1)} %slice.25), channel_id=1, source_target_pairs={{0,2},{1,3},{2,0},{3,1},{4,6},{5,7},{6,4},{7,5},{8,10},{9,11},{10,... | collective-permute-start | bytes 344072 | tf_op jit(solution)/shard_map/ppermute | solution.py:26
  29.8 9.9 %collective-permute-start.11 = (bf16[16,3584]{1,0:T(8,128)(2,1)S(1)}, bf16[16,3584]{1,0:T(8,128)(2,1)S(1)}, u32[]{:S(2)}, u32[]{:S(2)}) collective-permute-start(bf16[16,3584]{1,0:T(8,128)(2,1)S(1)} %slice.32), channel_id=1, source_target_pairs={{0,4},{1,5},{2,6},{3,7},{4,0},{5,1},{6,2},{7,3},{8,12},{9,13},{10,... | collective-permute-start | bytes 344072 | tf_op jit(solution)/shard_map/ppermute | solution.py:26
  32.1 7.5 %collective-permute-start.12 = (bf16[16,3584]{1,0:T(8,128)(2,1)S(1)}, bf16[16,3584]{1,0:T(8,128)(2,1)S(1)}, u32[]{:S(2)}, u32[]{:S(2)}) collective-permute-start(bf16[16,3584]{1,0:T(8,128)(2,1)S(1)} %slice.33), channel_id=1, source_target_pairs={{0,2},{1,3},{2,0},{3,1},{4,6},{5,7},{6,4},{7,5},{8,10},{9,11},{10,... | collective-permute-start | bytes 344072 | tf_op jit(solution)/shard_map/ppermute | solution.py:26
  35.4 33.7 %all-to-all-start = ((bf16[8,2,48,576]{3,2,1,0:T(8,128)(2,1)}), bf16[8,2,48,576]{3,2,1,0:T(8,128)(2,1)S(1)}, u32[]{:S(2)}, u32[]{:S(2)}) async-start(bf16[8,2,48,576]{3,2,1,0:T(8,128)(2,1)} %get-tuple-element.47), calls=%async_computation | async-start | bytes 1966080 | tf_op jit(solution)/shard_map/all_to_all | solution.py:328
  49.6 6.8 %collective-permute-start.20 = (bf16[16,3584]{1,0:T(8,128)(2,1)S(1)}, bf16[16,3584]{1,0:T(8,128)(2,1)S(1)}, u32[]{:S(2)}, u32[]{:S(2)}) collective-permute-start(bf16[16,3584]{1,0:T(8,128)(2,1)S(1)} %get-tuple-element.54), channel_id=1, source_target_pairs={{0,4},{1,5},{2,6},{3,7},{4,0},{5,1},{6,2},{7,3},{8,12},{9,13},{10,... | collective-permute-start | bytes 344072 | tf_op jit(solution)/shard_map/ppermute | solution.py:26
  51.7 6.5 %collective-permute-start.14 = (bf16[16,3584]{1,0:T(8,128)(2,1)S(1)}, bf16[16,3584]{1,0:T(8,128)(2,1)S(1)}, u32[]{:S(2)}, u32[]{:S(2)}) collective-permute-start(bf16[16,3584]{1,0:T(8,128)(2,1)S(1)} %get-tuple-element.53), channel_id=1, source_target_pairs={{0,2},{1,3},{2,0},{3,1},{4,6},{5,7},{6,4},{7,5},{8,10},{9,11},{10,... | collective-permute-start | bytes 344072 | tf_op jit(solution)/shard_map/ppermute | solution.py:26
  52.2 6.8 %collective-permute-start.15 = (bf16[16,3584]{1,0:T(8,128)(2,1)S(1)}, bf16[16,3584]{1,0:T(8,128)(2,1)S(1)}, u32[]{:S(2)}, u32[]{:S(2)}) collective-permute-start(bf16[16,3584]{1,0:T(8,128)(2,1)S(1)} %get-tuple-element.52), channel_id=1, source_target_pairs={{0,4},{1,5},{2,6},{3,7},{4,0},{5,1},{6,2},{7,3},{8,12},{9,13},{10,... | collective-permute-start | bytes 344072 | tf_op jit(solution)/shard_map/ppermute | solution.py:26
  57.1 7.2 %collective-permute-start.22 = (bf16[16,7168]{1,0:T(8,128)(2,1)S(1)}, bf16[16,7168]{1,0:T(8,128)(2,1)S(1)}, u32[]{:S(2)}, u32[]{:S(2)}) collective-permute-start(bf16[16,7168]{1,0:T(8,128)(2,1)S(1)} %get-tuple-element.43), channel_id=1, source_target_pairs={{0,4},{1,5},{2,6},{3,7},{4,0},{5,1},{6,2},{7,3},{8,12},{9,13},{10,... | collective-permute-start | bytes 688136 | tf_op jit(solution)/shard_map/ppermute | solution.py:26
  59.0 8.5 %collective-permute-start.16 = (bf16[16,7168]{1,0:T(8,128)(2,1)S(1)}, bf16[16,7168]{1,0:T(8,128)(2,1)S(1)}, u32[]{:S(2)}, u32[]{:S(2)}) collective-permute-start(bf16[16,7168]{1,0:T(8,128)(2,1)S(1)} %get-tuple-element.35), channel_id=1, source_target_pairs={{0,2},{1,3},{2,0},{3,1},{4,6},{5,7},{6,4},{7,5},{8,10},{9,11},{10,... | collective-permute-start | bytes 688136 | tf_op jit(solution)/shard_map/ppermute | solution.py:26
  60.0 7.5 %collective-permute-start.17 = (bf16[16,7168]{1,0:T(8,128)(2,1)S(1)}, bf16[16,7168]{1,0:T(8,128)(2,1)S(1)}, u32[]{:S(2)}, u32[]{:S(2)}) collective-permute-start(bf16[16,7168]{1,0:T(8,128)(2,1)S(1)} %get-tuple-element.36), channel_id=1, source_target_pairs={{0,4},{1,5},{2,6},{3,7},{4,0},{5,1},{6,2},{7,3},{8,12},{9,13},{10,... | collective-permute-start | bytes 688136 | tf_op jit(solution)/shard_map/ppermute | solution.py:26
  64.4 6.8 %collective-permute-start.24 = (bf16[8,7168]{1,0:T(8,128)(2,1)S(1)}, bf16[8,7168]{1,0:T(8,128)(2,1)S(1)}, u32[]{:S(2)}, u32[]{:S(2)}) collective-permute-start(bf16[8,7168]{1,0:T(8,128)(2,1)S(1)} %get-tuple-element.45), channel_id=1, source_target_pairs={{0,24},{1,25},{2,26},{3,27},{4,28},{5,29},{6,30},{7,31},{8,16},{9,... | collective-permute-start | bytes 344072 | tf_op jit(solution)/shard_map/ppermute | solution.py:26
  67.0 7.0 %collective-permute-start.23 = (bf16[8,7168]{1,0:T(8,128)(2,1)S(1)}, bf16[8,7168]{1,0:T(8,128)(2,1)S(1)}, u32[]{:S(2)}, u32[]{:S(2)}) collective-permute-start(bf16[8,7168]{1,0:T(8,128)(2,1)S(1)} %get-tuple-element.44), channel_id=1, source_target_pairs={{0,16},{1,17},{2,18},{3,19},{4,20},{5,21},{6,22},{7,23},{8,24},{9,... | collective-permute-start | bytes 344072 | tf_op jit(solution)/shard_map/ppermute | solution.py:26
  67.6 6.4 %collective-permute-start.18 = (bf16[8,7168]{1,0:T(8,128)(2,1)S(1)}, bf16[8,7168]{1,0:T(8,128)(2,1)S(1)}, u32[]{:S(2)}, u32[]{:S(2)}) collective-permute-start(bf16[8,7168]{1,0:T(8,128)(2,1)S(1)} %get-tuple-element.38), channel_id=1, source_target_pairs={{0,8},{1,9},{2,10},{3,11},{4,12},{5,13},{6,14},{7,15},{8,0},{9,1},... | collective-permute-start | bytes 344072 | tf_op jit(solution)/shard_map/ppermute | solution.py:26
  (7 other events, 79.4 us)

commit v6 on v5

--- a/solution.py
+++ b/solution.py
@@ -224,8 +224,8 @@
             first = jnp.where(hit & (count == 0), row, first)
             second = jnp.where(hit & (count == 1), row, second)
             count = count + hit.astype(jnp.int32)
-        for rank, pick in enumerate((first, second)):
-            out[beam ^ place, rank] = held[pick]
+        pair = [held[pick].astype(jnp.float32) for pick in (first, second)]
+        out[beam ^ place] = jnp.concatenate(pair, axis=1).astype(out.dtype)
 
 
 def unpacking_kernel(quad, facts, newest, arrived, out, scalars, sem):
@@ -243,7 +243,8 @@
         at = ((plane // planes) * 2 + side) * quad + (plane % planes) * rows + row
         bound = scalars[at, 1]
         token = lax.broadcasted_iota(jnp.int32, (tokens, width), 0)
-        old = arrived[parent, jnp.minimum(rank, CAP - 1)].astype(jnp.float32)
+        pair = arrived[parent].astype(jnp.float32)
+        old = jnp.where(rank == 0, pair[:, :width], pair[:, width:])
         value = jnp.where(token < bound, old, jnp.where(token == bound, newest[row], 0.0))
         out[row] = value.astype(out.dtype)
 
@@ -256,7 +257,7 @@
         in_specs=[whole] * len(blocks) + [pl.BlockSpec(memory_space=pltpu.HBM)],
         out_specs=[whole] * 2,
         out_shape=[
-            jax.ShapeDtypeStruct((BEAMS, CAP) + cache.shape[1:], cache.dtype),
+            jax.ShapeDtypeStruct((BEAMS, cache.shape[1], CAP * cache.shape[2]), cache.dtype),
             pltpu.VMEM(table, jnp.int32),
         ],
         scratch_shapes=[

time: 75 us -> 74.5 us (level)
  waiting for transfers between devices: 19.8 us -> 18.6 us
    ppermute x25, waiting for transfers between devices: 19.8 us -> 18.6 us  [swapped(): return lax.ppermute(value, 'ep', [(i, i ^ mask) for i in range(peers)])]
where the time goes in v6:
time: 74.5 us; the launch traced here: 74.3 us
  starting transfers between devices  38.2 us (51%)
  waiting for transfers between devices  18.6 us (25%)
  Pallas kernels  14 us (19%)
  local copies, waits for them, and re-layouts  1.75 us (2%)
  between operations  0.86 us (1%)
  other arithmetic  0.83 us (1%)
    ppermute x25, starting transfers between devices, swapped(): return lax.ppermute(value, 'ep', [(i, i ^ mask) for i in range(peers)])  33.9 us
    ppermute x25, waiting for transfers between devices, swapped(): return lax.ppermute(value, 'ep', [(i, i ^ mask) for i in range(peers)])  18.6 us
    pallas_call x7, Pallas kernels, whole_call(): pl.pallas_call(body, in_specs=[far if isinstance(a, tuple) else whole for...  8.61 us
    all_to_all x1, starting transfers between devices, dense_local(): lax.all_to_all(packets, 'ep', split_axis=0, concat_axis=0, axis_index_gro...  4.25 us
    pallas_call x1, Pallas kernels, packing_call(): pl.pallas_call(packing_kernel, in_specs=[whole] * len(blocks) + [pl.Block...  2.31 us
    pallas_call x1, Pallas kernels, unpacking_call(): pl.pallas_call(lambda *refs: unpacking_kernel(quad, *refs), in_specs=[who...  2.16 us
    unnamed x10, local copies, waits for them, and re-layouts  1.67 us
  transfers between devices with their start and end apart: 26, of which 10 were waited for; matrix products, arithmetic and copies ran while one was open for 0% of the time, Pallas kernels for 19%

profile of v6, /device:TPU:0, one launch (start us, length us, event | category | flops | bytes accessed | tf_op | source)
XLA Modules:
  0.0 74.3 jit_solution(8912153170232272896)
XLA Ops:
  2.2 3.1 %collective-permute-start = (bf16[8,7296]{1,0:T(8,128)(2,1)S(1)}, bf16[8,7296]{1,0:T(8,128)(2,1)S(1)}, u32[]{:S(2)}, u32[]{:S(2)}) collective-permute-start(bf16[8,7296]{1,0:T(8,128)(2,1)S(1)} %shard_map.113.refs_0_), channel_id=1, source_target_pairs={{0,8},{1,9},{2,10},{3,11},{4,12},{5,13},{6,14},{7,15},{8,0},{9,1},... | collective-permute-start | bytes 350216 | tf_op jit(solution)/shard_map/ppermute | solution.py:26
  5.2 2.6 %collective-permute-start.3 = (bf16[8,7296]{1,0:T(8,128)(2,1)S(1)}, bf16[8,7296]{1,0:T(8,128)(2,1)S(1)}, u32[]{:S(2)}, u32[]{:S(2)}) collective-permute-start(bf16[8,7296]{1,0:T(8,128)(2,1)S(1)} %shard_map.113.refs_0_), channel_id=1, source_target_pairs={{0,16},{1,17},{2,18},{3,19},{4,20},{5,21},{6,22},{7,23},{8,24},{9,... | collective-permute-start | bytes 350216 | tf_op jit(solution)/shard_map/ppermute | solution.py:26
  7.8 2.3 %collective-permute-done.refs_1_ = bf16[8,7296]{1,0:T(8,128)(2,1)S(1)} collective-permute-done((bf16[8,7296]{1,0:T(8,128)(2,1)S(1)}, bf16[8,7296]{1,0:T(8,128)(2,1)S(1)}, u32[]{:S(2)}, u32[]{:S(2)}) %collective-permute-start) | collective-permute-done | bytes 116768 | tf_op jit(solution)/shard_map/ppermute | solution.py:26
  10.2 1.9 %collective-permute-start.1 = (bf16[16,7296]{1,0:T(8,128)(2,1)S(1)}, bf16[16,7296]{1,0:T(8,128)(2,1)S(1)}, u32[]{:S(2)}, u32[]{:S(2)}) collective-permute-start(bf16[16,7296]{1,0:T(8,128)(2,1)S(1)} %shard_map.114.refs_0_.own_a), channel_id=1, source_target_pairs={{0,2},{1,3},{2,0},{3,1},{4,6},{5,7},{6,4},{7,5},{8,10},{9,11},{10,... | collective-permute-start | bytes 700424 | tf_op jit(solution)/shard_map/ppermute | solution.py:26
  12.1 1.5 %collective-permute-start.2 = (bf16[16,7296]{1,0:T(8,128)(2,1)S(1)}, bf16[16,7296]{1,0:T(8,128)(2,1)S(1)}, u32[]{:S(2)}, u32[]{:S(2)}) collective-permute-start(bf16[16,7296]{1,0:T(8,128)(2,1)S(1)} %shard_map.114.refs_0_.own_a), channel_id=1, source_target_pairs={{0,4},{1,5},{2,6},{3,7},{4,0},{5,1},{6,2},{7,3},{8,12},{9,13},{10,... | collective-permute-start | bytes 700424 | tf_op jit(solution)/shard_map/ppermute | solution.py:26
  13.6 3.2 %collective-permute-start.4 = (bf16[8,7296]{1,0:T(8,128)(2,1)S(1)}, bf16[8,7296]{1,0:T(8,128)(2,1)S(1)}, u32[]{:S(2)}, u32[]{:S(2)}) collective-permute-start(bf16[8,7296]{1,0:T(8,128)(2,1)S(1)} %shard_map.113.refs_0_), channel_id=1, source_target_pairs={{0,24},{1,25},{2,26},{3,27},{4,28},{5,29},{6,30},{7,31},{8,16},{9,... | collective-permute-start | bytes 350216 | tf_op jit(solution)/shard_map/ppermute | solution.py:26
  16.8 3.4 %collective-permute-done.4.refs_1_ = bf16[8,7296]{1,0:T(8,128)(2,1)S(1)} collective-permute-done((bf16[8,7296]{1,0:T(8,128)(2,1)S(1)}, bf16[8,7296]{1,0:T(8,128)(2,1)S(1)}, u32[]{:S(2)}, u32[]{:S(2)}) %collective-permute-start.4) | collective-permute-done | bytes 116768 | tf_op jit(solution)/shard_map/ppermute | solution.py:26
  20.4 1.6 %copy-done = bf16[7168,256]{1,0:T(8,128)(2,1)} copy-done((bf16[7168,256]{1,0:T(8,128)(2,1)}, bf16[7168,256]{1,0:T(8,128)(2,1)S(1)}, u32[]{:S(2)}) %copy-start) | copy-done | bytes 3670040
  22.0 1.5 %collective-permute-start.9 = (bf16[16,7296]{1,0:T(8,128)(2,1)S(1)}, bf16[16,7296]{1,0:T(8,128)(2,1)S(1)}, u32[]{:S(2)}, u32[]{:S(2)}) collective-permute-start(bf16[16,7296]{1,0:T(8,128)(2,1)S(1)} %shard_map.115.refs_5_.own_b), channel_id=1, source_target_pairs={{0,2},{1,3},{2,0},{3,1},{4,6},{5,7},{6,4},{7,5},{8,10},{9,11},{10,... | collective-permute-start | bytes 700424 | tf_op jit(solution)/shard_map/ppermute | solution.py:26
  23.5 1.5 %collective-permute-start.10 = (bf16[16,7296]{1,0:T(8,128)(2,1)S(1)}, bf16[16,7296]{1,0:T(8,128)(2,1)S(1)}, u32[]{:S(2)}, u32[]{:S(2)}) collective-permute-start(bf16[16,7296]{1,0:T(8,128)(2,1)S(1)} %shard_map.115.refs_5_.own_b), channel_id=1, source_target_pairs={{0,4},{1,5},{2,6},{3,7},{4,0},{5,1},{6,2},{7,3},{8,12},{9,13},{10,... | collective-permute-start | bytes 700424 | tf_op jit(solution)/shard_map/ppermute | solution.py:26
  26.8 2.9 %collective-permute-done.9.refs_6_ = bf16[16,7296]{1,0:T(8,128)(2,1)S(1)} collective-permute-done((bf16[16,7296]{1,0:T(8,128)(2,1)S(1)}, bf16[16,7296]{1,0:T(8,128)(2,1)S(1)}, u32[]{:S(2)}, u32[]{:S(2)}) %collective-permute-start.9) | collective-permute-done | bytes 233504 | tf_op jit(solution)/shard_map/ppermute | solution.py:26
  29.8 1.6 %collective-permute-start.11 = (bf16[16,3584]{1,0:T(8,128)(2,1)S(1)}, bf16[16,3584]{1,0:T(8,128)(2,1)S(1)}, u32[]{:S(2)}, u32[]{:S(2)}) collective-permute-start(bf16[16,3584]{1,0:T(8,128)(2,1)S(1)} %slice.32), channel_id=1, source_target_pairs={{0,4},{1,5},{2,6},{3,7},{4,0},{5,1},{6,2},{7,3},{8,12},{9,13},{10,... | collective-permute-start | bytes 344072 | tf_op jit(solution)/shard_map/ppermute | solution.py:26
  33.1 2.3 %shard_map.121 = (bf16[8,48,1152]{2,1,0:T(8,128)(2,1)}, s32[64,128]{1,0:T(8,128)S(1)}) custom-call(bf16[16,7296]{1,0:T(8,128)(2,1)S(1)} %shard_map.114.refs_0_.own_a, bf16[16,7296]{1,0:T(8,128)(2,1)S(1)} %collective-permute-done.2.refs_2_.y_a, bf16[16,7296]{1,0:T(8,128)(2,1)S(1)} %shard_map.115.refs_5_.own_b, ...), custom_call_target="tpu_custom_call" | custom-call | bytes 884736 | tf_op jit(solution)/shard_map/pallas_call | solution.py:255
  35.4 4.2 %all-to-all-start = ((bf16[8,48,1152]{2,1,0:T(8,128)(2,1)}), bf16[8,48,1152]{2,1,0:T(8,128)(2,1)S(1)}, u32[]{:S(2)}, u32[]{:S(2)}) async-start(bf16[8,48,1152]{2,1,0:T(8,128)(2,1)} %get-tuple-element.47), calls=%async_computation | async-start | bytes 1769472 | tf_op jit(solution)/shard_map/all_to_all | solution.py:329
  39.7 8.2 %shard_map.116 = (bf16[48,7168]{1,0:T(8,128)(2,1)S(1)}, bf16[16,7168]{1,0:T(8,128)(2,1)S(1)}, bf16[48,7168]{1,0:T(8,128)(2,1)S(1)}, bf16[16,7168]{1,0:T(8,128)(2,1)S(1)}) custom-call(bf16[16,7296]{1,0:T(8,128)(2,1)S(1)} %shard_map.114.refs_0_.own_a, bf16[16,7296]{1,0:T(8,128)(2,1)S(1)} %collective-permute-done.1.refs_1_, ...), custom_call_target="tpu_custom_call" | custom-call | flops 2818572288 | bytes 23879680 | tf_op jit(solution)/shard_map/pallas_call | solution.py:46
  48.0 1.7 %collective-permute-start.19 = (bf16[16,3584]{1,0:T(8,128)(2,1)S(1)}, bf16[16,3584]{1,0:T(8,128)(2,1)S(1)}, u32[]{:S(2)}, u32[]{:S(2)}) collective-permute-start(bf16[16,3584]{1,0:T(8,128)(2,1)S(1)} %get-tuple-element.55), channel_id=1, source_target_pairs={{0,2},{1,3},{2,0},{3,1},{4,6},{5,7},{6,4},{7,5},{8,10},{9,11},{10,... | collective-permute-start | bytes 344072 | tf_op jit(solution)/shard_map/ppermute | solution.py:26
  49.7 2.0 %collective-permute-start.20 = (bf16[16,3584]{1,0:T(8,128)(2,1)S(1)}, bf16[16,3584]{1,0:T(8,128)(2,1)S(1)}, u32[]{:S(2)}, u32[]{:S(2)}) collective-permute-start(bf16[16,3584]{1,0:T(8,128)(2,1)S(1)} %get-tuple-element.54), channel_id=1, source_target_pairs={{0,4},{1,5},{2,6},{3,7},{4,0},{5,1},{6,2},{7,3},{8,12},{9,13},{10,... | collective-permute-start | bytes 344072 | tf_op jit(solution)/shard_map/ppermute | solution.py:26
  52.2 1.4 %collective-permute-done.19.got_a = bf16[16,3584]{1,0:T(8,128)(2,1)S(1)} collective-permute-done((bf16[16,3584]{1,0:T(8,128)(2,1)S(1)}, bf16[16,3584]{1,0:T(8,128)(2,1)S(1)}, u32[]{:S(2)}, u32[]{:S(2)}) %collective-permute-start.19) | collective-permute-done | bytes 114720 | tf_op jit(solution)/shard_map/ppermute | solution.py:26
  53.6 2.7 %collective-permute-done.20.got_b = bf16[16,3584]{1,0:T(8,128)(2,1)S(1)} collective-permute-done((bf16[16,3584]{1,0:T(8,128)(2,1)S(1)}, bf16[16,3584]{1,0:T(8,128)(2,1)S(1)}, u32[]{:S(2)}, u32[]{:S(2)}) %collective-permute-start.20) | collective-permute-done | bytes 114720 | tf_op jit(solution)/shard_map/ppermute | solution.py:26
  57.4 1.8 %collective-permute-start.22 = (bf16[16,7168]{1,0:T(8,128)(2,1)S(1)}, bf16[16,7168]{1,0:T(8,128)(2,1)S(1)}, u32[]{:S(2)}, u32[]{:S(2)}) collective-permute-start(bf16[16,7168]{1,0:T(8,128)(2,1)S(1)} %get-tuple-element.43), channel_id=1, source_target_pairs={{0,4},{1,5},{2,6},{3,7},{4,0},{5,1},{6,2},{7,3},{8,12},{9,13},{10,... | collective-permute-start | bytes 688136 | tf_op jit(solution)/shard_map/ppermute | solution.py:26
  59.2 2.0 %collective-permute-start.16 = (bf16[16,7168]{1,0:T(8,128)(2,1)S(1)}, bf16[16,7168]{1,0:T(8,128)(2,1)S(1)}, u32[]{:S(2)}, u32[]{:S(2)}) collective-permute-start(bf16[16,7168]{1,0:T(8,128)(2,1)S(1)} %get-tuple-element.35), channel_id=1, source_target_pairs={{0,2},{1,3},{2,0},{3,1},{4,6},{5,7},{6,4},{7,5},{8,10},{9,11},{10,... | collective-permute-start | bytes 688136 | tf_op jit(solution)/shard_map/ppermute | solution.py:26
  63.7 3.2 %collective-permute-start.24 = (bf16[8,7168]{1,0:T(8,128)(2,1)S(1)}, bf16[8,7168]{1,0:T(8,128)(2,1)S(1)}, u32[]{:S(2)}, u32[]{:S(2)}) collective-permute-start(bf16[8,7168]{1,0:T(8,128)(2,1)S(1)} %get-tuple-element.45), channel_id=1, source_target_pairs={{0,24},{1,25},{2,26},{3,27},{4,28},{5,29},{6,30},{7,31},{8,16},{9,... | collective-permute-start | bytes 344072 | tf_op jit(solution)/shard_map/ppermute | solution.py:26
  68.4 2.2 %shard_map.122 = bf16[8,48,576]{2,1,0:T(8,128)(2,1)} custom-call(s32[64,128]{1,0:T(8,128)S(1)} %get-tuple-element.46.refs_0_, f32[8,1,576]{2,1,0:T(1,128)S(1)} %reshape.12.refs_1_, bf16[8,48,1152]{2,1,0:T(8,128)(2,1)S(1)} %all-to-all-done.refs_2_), custom_call_target="tpu_custom_call" | custom-call | bytes 884736 | tf_op jit(solution)/shard_map/pallas_call | solution.py:276
  70.6 2.9 %collective-permute-done.23 = bf16[8,7168]{1,0:T(8,128)(2,1)S(1)} collective-permute-done((bf16[8,7168]{1,0:T(8,128)(2,1)S(1)}, bf16[8,7168]{1,0:T(8,128)(2,1)S(1)}, u32[]{:S(2)}, u32[]{:S(2)}) %collective-permute-start.23) | collective-permute-done | bytes 114720 | tf_op jit(solution)/shard_map/ppermute | solution.py:26
  (57 shorter events, 11.7 us)
Async XLA Ops:
  0.6 19.6 %collective-permute-start.5 = (bf16[7168,256]{1,0:T(8,128)(2,1)}, bf16[7168,256]{1,0:T(8,128)(2,1)S(1)}, u32[]{:S(2)}, u32[]{:S(2)}) collective-permute-start(bf16[7168,256]{1,0:T(8,128)(2,1)} %refs_10_.1), channel_id=1, source_target_pairs={{0,1},{1,0},{2,3},{3,2},{4,5},{5,4},{6,7},{7,6},{8,9},{9,8},{10,11... | collective-permute-start | bytes 11010056 | tf_op jit(solution)/shard_map/ppermute | solution.py:26
  1.1 19.1 %collective-permute-start.6 = (bf16[7168,256]{1,0:T(8,128)(2,1)}, bf16[7168,256]{1,0:T(8,128)(2,1)S(1)}, u32[]{:S(2)}, u32[]{:S(2)}) collective-permute-start(bf16[7168,256]{1,0:T(8,128)(2,1)} %refs_11_.1), channel_id=1, source_target_pairs={{0,1},{1,0},{2,3},{3,2},{4,5},{5,4},{6,7},{7,6},{8,9},{9,8},{10,11... | collective-permute-start | bytes 11010056 | tf_op jit(solution)/shard_map/ppermute | solution.py:26
  2.2 8.0 %collective-permute-start = (bf16[8,7296]{1,0:T(8,128)(2,1)S(1)}, bf16[8,7296]{1,0:T(8,128)(2,1)S(1)}, u32[]{:S(2)}, u32[]{:S(2)}) collective-permute-start(bf16[8,7296]{1,0:T(8,128)(2,1)S(1)} %shard_map.113.refs_0_), channel_id=1, source_target_pairs={{0,8},{1,9},{2,10},{3,11},{4,12},{5,13},{6,14},{7,15},{8,0},{9,1},... | collective-permute-start | bytes 350216 | tf_op jit(solution)/shard_map/ppermute | solution.py:26
  5.2 8.4 %collective-permute-start.3 = (bf16[8,7296]{1,0:T(8,128)(2,1)S(1)}, bf16[8,7296]{1,0:T(8,128)(2,1)S(1)}, u32[]{:S(2)}, u32[]{:S(2)}) collective-permute-start(bf16[8,7296]{1,0:T(8,128)(2,1)S(1)} %shard_map.113.refs_0_), channel_id=1, source_target_pairs={{0,16},{1,17},{2,18},{3,19},{4,20},{5,21},{6,22},{7,23},{8,24},{9,... | collective-permute-start | bytes 350216 | tf_op jit(solution)/shard_map/ppermute | solution.py:26
  10.2 10.0 %collective-permute-start.1 = (bf16[16,7296]{1,0:T(8,128)(2,1)S(1)}, bf16[16,7296]{1,0:T(8,128)(2,1)S(1)}, u32[]{:S(2)}, u32[]{:S(2)}) collective-permute-start(bf16[16,7296]{1,0:T(8,128)(2,1)S(1)} %shard_map.114.refs_0_.own_a), channel_id=1, source_target_pairs={{0,2},{1,3},{2,0},{3,1},{4,6},{5,7},{6,4},{7,5},{8,10},{9,11},{10,... | collective-permute-start | bytes 700424 | tf_op jit(solution)/shard_map/ppermute | solution.py:26
  12.1 8.1 %collective-permute-start.2 = (bf16[16,7296]{1,0:T(8,128)(2,1)S(1)}, bf16[16,7296]{1,0:T(8,128)(2,1)S(1)}, u32[]{:S(2)}, u32[]{:S(2)}) collective-permute-start(bf16[16,7296]{1,0:T(8,128)(2,1)S(1)} %shard_map.114.refs_0_.own_a), channel_id=1, source_target_pairs={{0,4},{1,5},{2,6},{3,7},{4,0},{5,1},{6,2},{7,3},{8,12},{9,13},{10,... | collective-permute-start | bytes 700424 | tf_op jit(solution)/shard_map/ppermute | solution.py:26
  13.6 6.6 %collective-permute-start.4 = (bf16[8,7296]{1,0:T(8,128)(2,1)S(1)}, bf16[8,7296]{1,0:T(8,128)(2,1)S(1)}, u32[]{:S(2)}, u32[]{:S(2)}) collective-permute-start(bf16[8,7296]{1,0:T(8,128)(2,1)S(1)} %shard_map.113.refs_0_), channel_id=1, source_target_pairs={{0,24},{1,25},{2,26},{3,27},{4,28},{5,29},{6,30},{7,31},{8,16},{9,... | collective-permute-start | bytes 350216 | tf_op jit(solution)/shard_map/ppermute | solution.py:26
  20.3 19.4 %collective-permute-start.13 = (bf16[256,7168]{1,0:T(8,128)(2,1)}, bf16[256,7168]{1,0:T(8,128)(2,1)}, u32[]{:S(2)}, u32[]{:S(2)}) collective-permute-start(bf16[256,7168]{1,0:T(8,128)(2,1)} %refs_12_.1), channel_id=1, source_target_pairs={{0,1},{1,0},{2,3},{3,2},{4,5},{5,4},{6,7},{7,6},{8,9},{9,8},{10,11... | collective-permute-start | bytes 11010056 | tf_op jit(solution)/shard_map/ppermute | solution.py:26
  22.0 7.7 %collective-permute-start.9 = (bf16[16,7296]{1,0:T(8,128)(2,1)S(1)}, bf16[16,7296]{1,0:T(8,128)(2,1)S(1)}, u32[]{:S(2)}, u32[]{:S(2)}) collective-permute-start(bf16[16,7296]{1,0:T(8,128)(2,1)S(1)} %shard_map.115.refs_5_.own_b), channel_id=1, source_target_pairs={{0,2},{1,3},{2,0},{3,1},{4,6},{5,7},{6,4},{7,5},{8,10},{9,11},{10,... | collective-permute-start | bytes 700424 | tf_op jit(solution)/shard_map/ppermute | solution.py:26
  23.5 8.6 %collective-permute-start.10 = (bf16[16,7296]{1,0:T(8,128)(2,1)S(1)}, bf16[16,7296]{1,0:T(8,128)(2,1)S(1)}, u32[]{:S(2)}, u32[]{:S(2)}) collective-permute-start(bf16[16,7296]{1,0:T(8,128)(2,1)S(1)} %shard_map.115.refs_5_.own_b), channel_id=1, source_target_pairs={{0,4},{1,5},{2,6},{3,7},{4,0},{5,1},{6,2},{7,3},{8,12},{9,13},{10,... | collective-permute-start | bytes 700424 | tf_op jit(solution)/shard_map/ppermute | solution.py:26
  25.0 14.6 %collective-permute-start.7 = (bf16[16,3584]{1,0:T(8,128)(2,1)S(1)}, bf16[16,3584]{1,0:T(8,128)(2,1)S(1)}, u32[]{:S(2)}, u32[]{:S(2)}) collective-permute-start(bf16[16,3584]{1,0:T(8,128)(2,1)S(1)} %slice.24), channel_id=1, source_target_pairs={{0,4},{1,5},{2,6},{3,7},{4,0},{5,1},{6,2},{7,3},{8,12},{9,13},{10,... | collective-permute-start | bytes 344072 | tf_op jit(solution)/shard_map/ppermute | solution.py:26
  25.6 14.1 %collective-permute-start.8 = (bf16[16,3584]{1,0:T(8,128)(2,1)S(1)}, bf16[16,3584]{1,0:T(8,128)(2,1)S(1)}, u32[]{:S(2)}, u32[]{:S(2)}) collective-permute-start(bf16[16,3584]{1,0:T(8,128)(2,1)S(1)} %slice.25), channel_id=1, source_target_pairs={{0,2},{1,3},{2,0},{3,1},{4,6},{5,7},{6,4},{7,5},{8,10},{9,11},{10,... | collective-permute-start | bytes 344072 | tf_op jit(solution)/shard_map/ppermute | solution.py:26
  29.8 9.9 %collective-permute-start.11 = (bf16[16,3584]{1,0:T(8,128)(2,1)S(1)}, bf16[16,3584]{1,0:T(8,128)(2,1)S(1)}, u32[]{:S(2)}, u32[]{:S(2)}) collective-permute-start(bf16[16,3584]{1,0:T(8,128)(2,1)S(1)} %slice.32), channel_id=1, source_target_pairs={{0,4},{1,5},{2,6},{3,7},{4,0},{5,1},{6,2},{7,3},{8,12},{9,13},{10,... | collective-permute-start | bytes 344072 | tf_op jit(solution)/shard_map/ppermute | solution.py:26
  32.1 7.6 %collective-permute-start.12 = (bf16[16,3584]{1,0:T(8,128)(2,1)S(1)}, bf16[16,3584]{1,0:T(8,128)(2,1)S(1)}, u32[]{:S(2)}, u32[]{:S(2)}) collective-permute-start(bf16[16,3584]{1,0:T(8,128)(2,1)S(1)} %slice.33), channel_id=1, source_target_pairs={{0,2},{1,3},{2,0},{3,1},{4,6},{5,7},{6,4},{7,5},{8,10},{9,11},{10,... | collective-permute-start | bytes 344072 | tf_op jit(solution)/shard_map/ppermute | solution.py:26
  35.4 33.0 %all-to-all-start = ((bf16[8,48,1152]{2,1,0:T(8,128)(2,1)}), bf16[8,48,1152]{2,1,0:T(8,128)(2,1)S(1)}, u32[]{:S(2)}, u32[]{:S(2)}) async-start(bf16[8,48,1152]{2,1,0:T(8,128)(2,1)} %get-tuple-element.47), calls=%async_computation | async-start | bytes 1769472 | tf_op jit(solution)/shard_map/all_to_all | solution.py:329
  49.7 6.6 %collective-permute-start.20 = (bf16[16,3584]{1,0:T(8,128)(2,1)S(1)}, bf16[16,3584]{1,0:T(8,128)(2,1)S(1)}, u32[]{:S(2)}, u32[]{:S(2)}) collective-permute-start(bf16[16,3584]{1,0:T(8,128)(2,1)S(1)} %get-tuple-element.54), channel_id=1, source_target_pairs={{0,4},{1,5},{2,6},{3,7},{4,0},{5,1},{6,2},{7,3},{8,12},{9,13},{10,... | collective-permute-start | bytes 344072 | tf_op jit(solution)/shard_map/ppermute | solution.py:26
  51.7 7.4 %collective-permute-start.14 = (bf16[16,3584]{1,0:T(8,128)(2,1)S(1)}, bf16[16,3584]{1,0:T(8,128)(2,1)S(1)}, u32[]{:S(2)}, u32[]{:S(2)}) collective-permute-start(bf16[16,3584]{1,0:T(8,128)(2,1)S(1)} %get-tuple-element.53), channel_id=1, source_target_pairs={{0,2},{1,3},{2,0},{3,1},{4,6},{5,7},{6,4},{7,5},{8,10},{9,11},{10,... | collective-permute-start | bytes 344072 | tf_op jit(solution)/shard_map/ppermute | solution.py:26
  52.2 7.0 %collective-permute-start.15 = (bf16[16,3584]{1,0:T(8,128)(2,1)S(1)}, bf16[16,3584]{1,0:T(8,128)(2,1)S(1)}, u32[]{:S(2)}, u32[]{:S(2)}) collective-permute-start(bf16[16,3584]{1,0:T(8,128)(2,1)S(1)} %get-tuple-element.52), channel_id=1, source_target_pairs={{0,4},{1,5},{2,6},{3,7},{4,0},{5,1},{6,2},{7,3},{8,12},{9,13},{10,... | collective-permute-start | bytes 344072 | tf_op jit(solution)/shard_map/ppermute | solution.py:26
  56.4 6.1 %collective-permute-start.21 = (bf16[16,7168]{1,0:T(8,128)(2,1)S(1)}, bf16[16,7168]{1,0:T(8,128)(2,1)S(1)}, u32[]{:S(2)}, u32[]{:S(2)}) collective-permute-start(bf16[16,7168]{1,0:T(8,128)(2,1)S(1)} %get-tuple-element.42), channel_id=1, source_target_pairs={{0,2},{1,3},{2,0},{3,1},{4,6},{5,7},{6,4},{7,5},{8,10},{9,11},{10,... | collective-permute-start | bytes 688136 | tf_op jit(solution)/shard_map/ppermute | solution.py:26
  57.4 6.3 %collective-permute-start.22 = (bf16[16,7168]{1,0:T(8,128)(2,1)S(1)}, bf16[16,7168]{1,0:T(8,128)(2,1)S(1)}, u32[]{:S(2)}, u32[]{:S(2)}) collective-permute-start(bf16[16,7168]{1,0:T(8,128)(2,1)S(1)} %get-tuple-element.43), channel_id=1, source_target_pairs={{0,4},{1,5},{2,6},{3,7},{4,0},{5,1},{6,2},{7,3},{8,12},{9,13},{10,... | collective-permute-start | bytes 688136 | tf_op jit(solution)/shard_map/ppermute | solution.py:26
  59.2 7.6 %collective-permute-start.16 = (bf16[16,7168]{1,0:T(8,128)(2,1)S(1)}, bf16[16,7168]{1,0:T(8,128)(2,1)S(1)}, u32[]{:S(2)}, u32[]{:S(2)}) collective-permute-start(bf16[16,7168]{1,0:T(8,128)(2,1)S(1)} %get-tuple-element.35), channel_id=1, source_target_pairs={{0,2},{1,3},{2,0},{3,1},{4,6},{5,7},{6,4},{7,5},{8,10},{9,11},{10,... | collective-permute-start | bytes 688136 | tf_op jit(solution)/shard_map/ppermute | solution.py:26
  63.7 6.9 %collective-permute-start.24 = (bf16[8,7168]{1,0:T(8,128)(2,1)S(1)}, bf16[8,7168]{1,0:T(8,128)(2,1)S(1)}, u32[]{:S(2)}, u32[]{:S(2)}) collective-permute-start(bf16[8,7168]{1,0:T(8,128)(2,1)S(1)} %get-tuple-element.45), channel_id=1, source_target_pairs={{0,24},{1,25},{2,26},{3,27},{4,28},{5,29},{6,30},{7,31},{8,16},{9,... | collective-permute-start | bytes 344072 | tf_op jit(solution)/shard_map/ppermute | solution.py:26
  66.9 6.6 %collective-permute-start.23 = (bf16[8,7168]{1,0:T(8,128)(2,1)S(1)}, bf16[8,7168]{1,0:T(8,128)(2,1)S(1)}, u32[]{:S(2)}, u32[]{:S(2)}) collective-permute-start(bf16[8,7168]{1,0:T(8,128)(2,1)S(1)} %get-tuple-element.44), channel_id=1, source_target_pairs={{0,16},{1,17},{2,18},{3,19},{4,20},{5,21},{6,22},{7,23},{8,24},{9,... | collective-permute-start | bytes 344072 | tf_op jit(solution)/shard_map/ppermute | solution.py:26
  67.4 6.1 %collective-permute-start.18 = (bf16[8,7168]{1,0:T(8,128)(2,1)S(1)}, bf16[8,7168]{1,0:T(8,128)(2,1)S(1)}, u32[]{:S(2)}, u32[]{:S(2)}) collective-permute-start(bf16[8,7168]{1,0:T(8,128)(2,1)S(1)} %get-tuple-element.38), channel_id=1, source_target_pairs={{0,8},{1,9},{2,10},{3,11},{4,12},{5,13},{6,14},{7,15},{8,0},{9,1},... | collective-permute-start | bytes 344072 | tf_op jit(solution)/shard_map/ppermute | solution.py:26
  (7 other events, 77.8 us)

commit v7 on v6

--- a/solution.py
+++ b/solution.py
@@ -112,13 +112,11 @@
     quad = groups[0][0].shape[0]
     cuts = [slice(step * chunk, (step + 1) * chunk) for step in range(STEPS)]
     copies = {}
-    for core in range(2):
-        for step, cut in enumerate(cuts):
-            for i in range(2):
-                at = 3 * core + i
-                copies[at, step] = pltpu.make_async_copy(
-                    sources[at].at[cut, :], held[at].at[cut, :], sems.at[at, step]
-                )
+    for step, cut in enumerate(cuts):
+        for at in (0, 1, 3, 4):
+            copies[at, step] = pltpu.make_async_copy(
+                sources[at].at[cut, :], held[at].at[cut, :], sems.at[at, step]
+            )
     for step, cut in enumerate(cuts):
         for at in (2, 5):
             copies[at, step] = pltpu.make_async_copy(
@@ -126,23 +124,23 @@
             )
     for copy in copies.values():
         copy.start()
-    for core in range(2):
-        units = slice(core * hid, (core + 1) * hid)
-        for step, cut in enumerate(cuts):
-            blocks = []
-            for own, from_x, from_y, left, right in groups:
-                corner = left[:, cut] if cut.stop <= half else right[:, cut.start - half : cut.stop - half]
-                blocks += [own[:, cut], from_x[:, cut], from_y[:, cut], corner]
-            block = jnp.concatenate(blocks, axis=0)
+    for step, cut in enumerate(cuts):
+        blocks = []
+        for own, from_x, from_y, left, right in groups:
+            corner = left[:, cut] if cut.stop <= half else right[:, cut.start - half : cut.stop - half]
+            blocks += [own[:, cut], from_x[:, cut], from_y[:, cut], corner]
+        block = jnp.concatenate(blocks, axis=0)
+        for core in range(2):
+            units = slice(core * hid, (core + 1) * hid)
             copies[3 * core, step].wait()
             gate = dot32(block, held[3 * core][cut, :])
             copies[3 * core + 1, step].wait()
             up = dot32(block, held[3 * core + 1][cut, :])
             if step:
-                gate, up = gate_sum[...] + gate, up_sum[...] + up
+                gate, up = gate_sum[:, units] + gate, up_sum[:, units] + up
             if step < STEPS - 1:
-                gate_sum[...] = gate
-                up_sum[...] = up
+                gate_sum[:, units] = gate
+                up_sum[:, units] = up
             else:
                 act[:, units] = (gate / (1.0 + jnp.exp(-gate)) * up).astype(act.dtype)
     for step, cut in enumerate(cuts):
@@ -161,8 +159,8 @@
     bf16, f32 = jnp.bfloat16, jnp.float32
     outs = [((3 * quad, d), bf16), ((quad, d), bf16)] * 2
     scratch = [pltpu.VMEM(w.shape, w.dtype) for w in weights] + [
-        pltpu.VMEM((8 * quad, hid), f32),
-        pltpu.VMEM((8 * quad, hid), f32),
+        pltpu.VMEM((8 * quad, 2 * hid), f32),
+        pltpu.VMEM((8 * quad, 2 * hid), f32),
         pltpu.VMEM((8 * quad, 2 * hid), bf16),
         pltpu.SemaphoreType.DMA((6, STEPS)),
     ]

time: 74.5 us -> 74.3 us (level)
  no operation moved by 1% of the time
where the time goes in v7:
time: 74.3 us; the launch traced here: 74.1 us
  starting transfers between devices  38.1 us (51%)
  waiting for transfers between devices  18.7 us (25%)
  Pallas kernels  13.9 us (19%)
  local copies, waits for them, and re-layouts  1.75 us (2%)
  between operations  0.86 us (1%)
  other arithmetic  0.83 us (1%)
    ppermute x25, starting transfers between devices, swapped(): return lax.ppermute(value, 'ep', [(i, i ^ mask) for i in range(peers)])  33.9 us
    ppermute x25, waiting for transfers between devices, swapped(): return lax.ppermute(value, 'ep', [(i, i ^ mask) for i in range(peers)])  18.7 us
    pallas_call x7, Pallas kernels, whole_call(): pl.pallas_call(body, in_specs=[far if isinstance(a, tuple) else whole for...  8.48 us
    all_to_all x1, starting transfers between devices, dense_local(): lax.all_to_all(packets, 'ep', split_axis=0, concat_axis=0, axis_index_gro...  4.25 us
    pallas_call x1, Pallas kernels, packing_call(): pl.pallas_call(packing_kernel, in_specs=[whole] * len(blocks) + [pl.Block...  2.31 us
    pallas_call x1, Pallas kernels, unpacking_call(): pl.pallas_call(lambda *refs: unpacking_kernel(quad, *refs), in_specs=[who...  2.16 us
    unnamed x10, local copies, waits for them, and re-layouts  1.67 us
  transfers between devices with their start and end apart: 26, of which 10 were waited for; matrix products, arithmetic and copies ran while one was open for 0% of the time, Pallas kernels for 19%

profile of v7, /device:TPU:0, one launch (start us, length us, event | category | flops | bytes accessed | tf_op | source)
XLA Modules:
  0.0 74.1 jit_solution(3121350103589355431)
XLA Ops:
  2.2 3.1 %collective-permute-start = (bf16[8,7296]{1,0:T(8,128)(2,1)S(1)}, bf16[8,7296]{1,0:T(8,128)(2,1)S(1)}, u32[]{:S(2)}, u32[]{:S(2)}) collective-permute-start(bf16[8,7296]{1,0:T(8,128)(2,1)S(1)} %shard_map.113.refs_0_), channel_id=1, source_target_pairs={{0,8},{1,9},{2,10},{3,11},{4,12},{5,13},{6,14},{7,15},{8,0},{9,1},... | collective-permute-start | bytes 350216 | tf_op jit(solution)/shard_map/ppermute | solution.py:26
  5.2 2.6 %collective-permute-start.3 = (bf16[8,7296]{1,0:T(8,128)(2,1)S(1)}, bf16[8,7296]{1,0:T(8,128)(2,1)S(1)}, u32[]{:S(2)}, u32[]{:S(2)}) collective-permute-start(bf16[8,7296]{1,0:T(8,128)(2,1)S(1)} %shard_map.113.refs_0_), channel_id=1, source_target_pairs={{0,16},{1,17},{2,18},{3,19},{4,20},{5,21},{6,22},{7,23},{8,24},{9,... | collective-permute-start | bytes 350216 | tf_op jit(solution)/shard_map/ppermute | solution.py:26
  7.8 2.3 %collective-permute-done.refs_1_ = bf16[8,7296]{1,0:T(8,128)(2,1)S(1)} collective-permute-done((bf16[8,7296]{1,0:T(8,128)(2,1)S(1)}, bf16[8,7296]{1,0:T(8,128)(2,1)S(1)}, u32[]{:S(2)}, u32[]{:S(2)}) %collective-permute-start) | collective-permute-done | bytes 116768 | tf_op jit(solution)/shard_map/ppermute | solution.py:26
  10.2 1.9 %collective-permute-start.1 = (bf16[16,7296]{1,0:T(8,128)(2,1)S(1)}, bf16[16,7296]{1,0:T(8,128)(2,1)S(1)}, u32[]{:S(2)}, u32[]{:S(2)}) collective-permute-start(bf16[16,7296]{1,0:T(8,128)(2,1)S(1)} %shard_map.114.refs_0_.own_a), channel_id=1, source_target_pairs={{0,2},{1,3},{2,0},{3,1},{4,6},{5,7},{6,4},{7,5},{8,10},{9,11},{10,... | collective-permute-start | bytes 700424 | tf_op jit(solution)/shard_map/ppermute | solution.py:26
  12.1 1.5 %collective-permute-start.2 = (bf16[16,7296]{1,0:T(8,128)(2,1)S(1)}, bf16[16,7296]{1,0:T(8,128)(2,1)S(1)}, u32[]{:S(2)}, u32[]{:S(2)}) collective-permute-start(bf16[16,7296]{1,0:T(8,128)(2,1)S(1)} %shard_map.114.refs_0_.own_a), channel_id=1, source_target_pairs={{0,4},{1,5},{2,6},{3,7},{4,0},{5,1},{6,2},{7,3},{8,12},{9,13},{10,... | collective-permute-start | bytes 700424 | tf_op jit(solution)/shard_map/ppermute | solution.py:26
  13.6 3.2 %collective-permute-start.4 = (bf16[8,7296]{1,0:T(8,128)(2,1)S(1)}, bf16[8,7296]{1,0:T(8,128)(2,1)S(1)}, u32[]{:S(2)}, u32[]{:S(2)}) collective-permute-start(bf16[8,7296]{1,0:T(8,128)(2,1)S(1)} %shard_map.113.refs_0_), channel_id=1, source_target_pairs={{0,24},{1,25},{2,26},{3,27},{4,28},{5,29},{6,30},{7,31},{8,16},{9,... | collective-permute-start | bytes 350216 | tf_op jit(solution)/shard_map/ppermute | solution.py:26
  16.8 3.4 %collective-permute-done.4.refs_1_ = bf16[8,7296]{1,0:T(8,128)(2,1)S(1)} collective-permute-done((bf16[8,7296]{1,0:T(8,128)(2,1)S(1)}, bf16[8,7296]{1,0:T(8,128)(2,1)S(1)}, u32[]{:S(2)}, u32[]{:S(2)}) %collective-permute-start.4) | collective-permute-done | bytes 116768 | tf_op jit(solution)/shard_map/ppermute | solution.py:26
  20.4 1.6 %copy-done = bf16[7168,256]{1,0:T(8,128)(2,1)} copy-done((bf16[7168,256]{1,0:T(8,128)(2,1)}, bf16[7168,256]{1,0:T(8,128)(2,1)S(1)}, u32[]{:S(2)}) %copy-start) | copy-done | bytes 3670040
  22.0 1.5 %collective-permute-start.9 = (bf16[16,7296]{1,0:T(8,128)(2,1)S(1)}, bf16[16,7296]{1,0:T(8,128)(2,1)S(1)}, u32[]{:S(2)}, u32[]{:S(2)}) collective-permute-start(bf16[16,7296]{1,0:T(8,128)(2,1)S(1)} %shard_map.115.refs_5_.own_b), channel_id=1, source_target_pairs={{0,2},{1,3},{2,0},{3,1},{4,6},{5,7},{6,4},{7,5},{8,10},{9,11},{10,... | collective-permute-start | bytes 700424 | tf_op jit(solution)/shard_map/ppermute | solution.py:26
  23.5 1.5 %collective-permute-start.10 = (bf16[16,7296]{1,0:T(8,128)(2,1)S(1)}, bf16[16,7296]{1,0:T(8,128)(2,1)S(1)}, u32[]{:S(2)}, u32[]{:S(2)}) collective-permute-start(bf16[16,7296]{1,0:T(8,128)(2,1)S(1)} %shard_map.115.refs_5_.own_b), channel_id=1, source_target_pairs={{0,4},{1,5},{2,6},{3,7},{4,0},{5,1},{6,2},{7,3},{8,12},{9,13},{10,... | collective-permute-start | bytes 700424 | tf_op jit(solution)/shard_map/ppermute | solution.py:26
  25.6 1.2 %collective-permute-start.8 = (bf16[16,3584]{1,0:T(8,128)(2,1)S(1)}, bf16[16,3584]{1,0:T(8,128)(2,1)S(1)}, u32[]{:S(2)}, u32[]{:S(2)}) collective-permute-start(bf16[16,3584]{1,0:T(8,128)(2,1)S(1)} %slice.25), channel_id=1, source_target_pairs={{0,2},{1,3},{2,0},{3,1},{4,6},{5,7},{6,4},{7,5},{8,10},{9,11},{10,... | collective-permute-start | bytes 344072 | tf_op jit(solution)/shard_map/ppermute | solution.py:26
  26.8 2.9 %collective-permute-done.9.refs_6_ = bf16[16,7296]{1,0:T(8,128)(2,1)S(1)} collective-permute-done((bf16[16,7296]{1,0:T(8,128)(2,1)S(1)}, bf16[16,7296]{1,0:T(8,128)(2,1)S(1)}, u32[]{:S(2)}, u32[]{:S(2)}) %collective-permute-start.9) | collective-permute-done | bytes 233504 | tf_op jit(solution)/shard_map/ppermute | solution.py:26
  29.8 1.6 %collective-permute-start.11 = (bf16[16,3584]{1,0:T(8,128)(2,1)S(1)}, bf16[16,3584]{1,0:T(8,128)(2,1)S(1)}, u32[]{:S(2)}, u32[]{:S(2)}) collective-permute-start(bf16[16,3584]{1,0:T(8,128)(2,1)S(1)} %slice.32), channel_id=1, source_target_pairs={{0,4},{1,5},{2,6},{3,7},{4,0},{5,1},{6,2},{7,3},{8,12},{9,13},{10,... | collective-permute-start | bytes 344072 | tf_op jit(solution)/shard_map/ppermute | solution.py:26
  33.1 2.3 %shard_map.121 = (bf16[8,48,1152]{2,1,0:T(8,128)(2,1)}, s32[64,128]{1,0:T(8,128)S(1)}) custom-call(bf16[16,7296]{1,0:T(8,128)(2,1)S(1)} %shard_map.114.refs_0_.own_a, bf16[16,7296]{1,0:T(8,128)(2,1)S(1)} %collective-permute-done.2.refs_2_.y_a, bf16[16,7296]{1,0:T(8,128)(2,1)S(1)} %shard_map.115.refs_5_.own_b, ...), custom_call_target="tpu_custom_call" | custom-call | bytes 884736 | tf_op jit(solution)/shard_map/pallas_call | solution.py:253
  35.4 4.2 %all-to-all-start = ((bf16[8,48,1152]{2,1,0:T(8,128)(2,1)}), bf16[8,48,1152]{2,1,0:T(8,128)(2,1)S(1)}, u32[]{:S(2)}, u32[]{:S(2)}) async-start(bf16[8,48,1152]{2,1,0:T(8,128)(2,1)} %get-tuple-element.47), calls=%async_computation | async-start | bytes 1769472 | tf_op jit(solution)/shard_map/all_to_all | solution.py:327
  39.7 8.1 %shard_map.116 = (bf16[48,7168]{1,0:T(8,128)(2,1)S(1)}, bf16[16,7168]{1,0:T(8,128)(2,1)S(1)}, bf16[48,7168]{1,0:T(8,128)(2,1)S(1)}, bf16[16,7168]{1,0:T(8,128)(2,1)S(1)}) custom-call(bf16[16,7296]{1,0:T(8,128)(2,1)S(1)} %shard_map.114.refs_0_.own_a, bf16[16,7296]{1,0:T(8,128)(2,1)S(1)} %collective-permute-done.1.refs_1_, ...), custom_call_target="tpu_custom_call" | custom-call | flops 2818572288 | bytes 23879680 | tf_op jit(solution)/shard_map/pallas_call | solution.py:46
  47.9 1.7 %collective-permute-start.19 = (bf16[16,3584]{1,0:T(8,128)(2,1)S(1)}, bf16[16,3584]{1,0:T(8,128)(2,1)S(1)}, u32[]{:S(2)}, u32[]{:S(2)}) collective-permute-start(bf16[16,3584]{1,0:T(8,128)(2,1)S(1)} %get-tuple-element.55), channel_id=1, source_target_pairs={{0,2},{1,3},{2,0},{3,1},{4,6},{5,7},{6,4},{7,5},{8,10},{9,11},{10,... | collective-permute-start | bytes 344072 | tf_op jit(solution)/shard_map/ppermute | solution.py:26
  49.5 2.0 %collective-permute-start.20 = (bf16[16,3584]{1,0:T(8,128)(2,1)S(1)}, bf16[16,3584]{1,0:T(8,128)(2,1)S(1)}, u32[]{:S(2)}, u32[]{:S(2)}) collective-permute-start(bf16[16,3584]{1,0:T(8,128)(2,1)S(1)} %get-tuple-element.54), channel_id=1, source_target_pairs={{0,4},{1,5},{2,6},{3,7},{4,0},{5,1},{6,2},{7,3},{8,12},{9,13},{10,... | collective-permute-start | bytes 344072 | tf_op jit(solution)/shard_map/ppermute | solution.py:26
  53.3 3.0 %collective-permute-done.20.got_b = bf16[16,3584]{1,0:T(8,128)(2,1)S(1)} collective-permute-done((bf16[16,3584]{1,0:T(8,128)(2,1)S(1)}, bf16[16,3584]{1,0:T(8,128)(2,1)S(1)}, u32[]{:S(2)}, u32[]{:S(2)}) %collective-permute-start.20) | collective-permute-done | bytes 114720 | tf_op jit(solution)/shard_map/ppermute | solution.py:26
  57.2 1.8 %collective-permute-start.22 = (bf16[16,7168]{1,0:T(8,128)(2,1)S(1)}, bf16[16,7168]{1,0:T(8,128)(2,1)S(1)}, u32[]{:S(2)}, u32[]{:S(2)}) collective-permute-start(bf16[16,7168]{1,0:T(8,128)(2,1)S(1)} %get-tuple-element.43), channel_id=1, source_target_pairs={{0,4},{1,5},{2,6},{3,7},{4,0},{5,1},{6,2},{7,3},{8,12},{9,13},{10,... | collective-permute-start | bytes 688136 | tf_op jit(solution)/shard_map/ppermute | solution.py:26
  59.1 2.0 %collective-permute-start.16 = (bf16[16,7168]{1,0:T(8,128)(2,1)S(1)}, bf16[16,7168]{1,0:T(8,128)(2,1)S(1)}, u32[]{:S(2)}, u32[]{:S(2)}) collective-permute-start(bf16[16,7168]{1,0:T(8,128)(2,1)S(1)} %get-tuple-element.35), channel_id=1, source_target_pairs={{0,2},{1,3},{2,0},{3,1},{4,6},{5,7},{6,4},{7,5},{8,10},{9,11},{10,... | collective-permute-start | bytes 688136 | tf_op jit(solution)/shard_map/ppermute | solution.py:26
  63.7 3.0 %collective-permute-start.24 = (bf16[8,7168]{1,0:T(8,128)(2,1)S(1)}, bf16[8,7168]{1,0:T(8,128)(2,1)S(1)}, u32[]{:S(2)}, u32[]{:S(2)}) collective-permute-start(bf16[8,7168]{1,0:T(8,128)(2,1)S(1)} %get-tuple-element.45), channel_id=1, source_target_pairs={{0,24},{1,25},{2,26},{3,27},{4,28},{5,29},{6,30},{7,31},{8,16},{9,... | collective-permute-start | bytes 344072 | tf_op jit(solution)/shard_map/ppermute | solution.py:26
  68.4 2.2 %shard_map.122 = bf16[8,48,576]{2,1,0:T(8,128)(2,1)} custom-call(s32[64,128]{1,0:T(8,128)S(1)} %get-tuple-element.46.refs_0_, f32[8,1,576]{2,1,0:T(1,128)S(1)} %reshape.12.refs_1_, bf16[8,48,1152]{2,1,0:T(8,128)(2,1)S(1)} %all-to-all-done.refs_2_), custom_call_target="tpu_custom_call" | custom-call | bytes 884736 | tf_op jit(solution)/shard_map/pallas_call | solution.py:274
  70.6 2.7 %collective-permute-done.23 = bf16[8,7168]{1,0:T(8,128)(2,1)S(1)} collective-permute-done((bf16[8,7168]{1,0:T(8,128)(2,1)S(1)}, bf16[8,7168]{1,0:T(8,128)(2,1)S(1)}, u32[]{:S(2)}, u32[]{:S(2)}) %collective-permute-start.23) | collective-permute-done | bytes 114720 | tf_op jit(solution)/shard_map/ppermute | solution.py:26
  (57 shorter events, 11.9 us)
Async XLA Ops:
  0.6 19.6 %collective-permute-start.5 = (bf16[7168,256]{1,0:T(8,128)(2,1)}, bf16[7168,256]{1,0:T(8,128)(2,1)S(1)}, u32[]{:S(2)}, u32[]{:S(2)}) collective-permute-start(bf16[7168,256]{1,0:T(8,128)(2,1)} %refs_10_.1), channel_id=1, source_target_pairs={{0,1},{1,0},{2,3},{3,2},{4,5},{5,4},{6,7},{7,6},{8,9},{9,8},{10,11... | collective-permute-start | bytes 11010056 | tf_op jit(solution)/shard_map/ppermute | solution.py:26
  1.1 19.1 %collective-permute-start.6 = (bf16[7168,256]{1,0:T(8,128)(2,1)}, bf16[7168,256]{1,0:T(8,128)(2,1)S(1)}, u32[]{:S(2)}, u32[]{:S(2)}) collective-permute-start(bf16[7168,256]{1,0:T(8,128)(2,1)} %refs_11_.1), channel_id=1, source_target_pairs={{0,1},{1,0},{2,3},{3,2},{4,5},{5,4},{6,7},{7,6},{8,9},{9,8},{10,11... | collective-permute-start | bytes 11010056 | tf_op jit(solution)/shard_map/ppermute | solution.py:26
  2.2 8.0 %collective-permute-start = (bf16[8,7296]{1,0:T(8,128)(2,1)S(1)}, bf16[8,7296]{1,0:T(8,128)(2,1)S(1)}, u32[]{:S(2)}, u32[]{:S(2)}) collective-permute-start(bf16[8,7296]{1,0:T(8,128)(2,1)S(1)} %shard_map.113.refs_0_), channel_id=1, source_target_pairs={{0,8},{1,9},{2,10},{3,11},{4,12},{5,13},{6,14},{7,15},{8,0},{9,1},... | collective-permute-start | bytes 350216 | tf_op jit(solution)/shard_map/ppermute | solution.py:26
  5.2 8.4 %collective-permute-start.3 = (bf16[8,7296]{1,0:T(8,128)(2,1)S(1)}, bf16[8,7296]{1,0:T(8,128)(2,1)S(1)}, u32[]{:S(2)}, u32[]{:S(2)}) collective-permute-start(bf16[8,7296]{1,0:T(8,128)(2,1)S(1)} %shard_map.113.refs_0_), channel_id=1, source_target_pairs={{0,16},{1,17},{2,18},{3,19},{4,20},{5,21},{6,22},{7,23},{8,24},{9,... | collective-permute-start | bytes 350216 | tf_op jit(solution)/shard_map/ppermute | solution.py:26
  10.2 10.0 %collective-permute-start.1 = (bf16[16,7296]{1,0:T(8,128)(2,1)S(1)}, bf16[16,7296]{1,0:T(8,128)(2,1)S(1)}, u32[]{:S(2)}, u32[]{:S(2)}) collective-permute-start(bf16[16,7296]{1,0:T(8,128)(2,1)S(1)} %shard_map.114.refs_0_.own_a), channel_id=1, source_target_pairs={{0,2},{1,3},{2,0},{3,1},{4,6},{5,7},{6,4},{7,5},{8,10},{9,11},{10,... | collective-permute-start | bytes 700424 | tf_op jit(solution)/shard_map/ppermute | solution.py:26
  12.1 8.1 %collective-permute-start.2 = (bf16[16,7296]{1,0:T(8,128)(2,1)S(1)}, bf16[16,7296]{1,0:T(8,128)(2,1)S(1)}, u32[]{:S(2)}, u32[]{:S(2)}) collective-permute-start(bf16[16,7296]{1,0:T(8,128)(2,1)S(1)} %shard_map.114.refs_0_.own_a), channel_id=1, source_target_pairs={{0,4},{1,5},{2,6},{3,7},{4,0},{5,1},{6,2},{7,3},{8,12},{9,13},{10,... | collective-permute-start | bytes 700424 | tf_op jit(solution)/shard_map/ppermute | solution.py:26
  13.6 6.6 %collective-permute-start.4 = (bf16[8,7296]{1,0:T(8,128)(2,1)S(1)}, bf16[8,7296]{1,0:T(8,128)(2,1)S(1)}, u32[]{:S(2)}, u32[]{:S(2)}) collective-permute-start(bf16[8,7296]{1,0:T(8,128)(2,1)S(1)} %shard_map.113.refs_0_), channel_id=1, source_target_pairs={{0,24},{1,25},{2,26},{3,27},{4,28},{5,29},{6,30},{7,31},{8,16},{9,... | collective-permute-start | bytes 350216 | tf_op jit(solution)/shard_map/ppermute | solution.py:26
  20.3 19.4 %collective-permute-start.13 = (bf16[256,7168]{1,0:T(8,128)(2,1)}, bf16[256,7168]{1,0:T(8,128)(2,1)}, u32[]{:S(2)}, u32[]{:S(2)}) collective-permute-start(bf16[256,7168]{1,0:T(8,128)(2,1)} %refs_12_.1), channel_id=1, source_target_pairs={{0,1},{1,0},{2,3},{3,2},{4,5},{5,4},{6,7},{7,6},{8,9},{9,8},{10,11... | collective-permute-start | bytes 11010056 | tf_op jit(solution)/shard_map/ppermute | solution.py:26
  22.0 7.7 %collective-permute-start.9 = (bf16[16,7296]{1,0:T(8,128)(2,1)S(1)}, bf16[16,7296]{1,0:T(8,128)(2,1)S(1)}, u32[]{:S(2)}, u32[]{:S(2)}) collective-permute-start(bf16[16,7296]{1,0:T(8,128)(2,1)S(1)} %shard_map.115.refs_5_.own_b), channel_id=1, source_target_pairs={{0,2},{1,3},{2,0},{3,1},{4,6},{5,7},{6,4},{7,5},{8,10},{9,11},{10,... | collective-permute-start | bytes 700424 | tf_op jit(solution)/shard_map/ppermute | solution.py:26
  23.5 8.6 %collective-permute-start.10 = (bf16[16,7296]{1,0:T(8,128)(2,1)S(1)}, bf16[16,7296]{1,0:T(8,128)(2,1)S(1)}, u32[]{:S(2)}, u32[]{:S(2)}) collective-permute-start(bf16[16,7296]{1,0:T(8,128)(2,1)S(1)} %shard_map.115.refs_5_.own_b), channel_id=1, source_target_pairs={{0,4},{1,5},{2,6},{3,7},{4,0},{5,1},{6,2},{7,3},{8,12},{9,13},{10,... | collective-permute-start | bytes 700424 | tf_op jit(solution)/shard_map/ppermute | solution.py:26
  25.0 14.6 %collective-permute-start.7 = (bf16[16,3584]{1,0:T(8,128)(2,1)S(1)}, bf16[16,3584]{1,0:T(8,128)(2,1)S(1)}, u32[]{:S(2)}, u32[]{:S(2)}) collective-permute-start(bf16[16,3584]{1,0:T(8,128)(2,1)S(1)} %slice.24), channel_id=1, source_target_pairs={{0,4},{1,5},{2,6},{3,7},{4,0},{5,1},{6,2},{7,3},{8,12},{9,13},{10,... | collective-permute-start | bytes 344072 | tf_op jit(solution)/shard_map/ppermute | solution.py:26
  25.6 14.1 %collective-permute-start.8 = (bf16[16,3584]{1,0:T(8,128)(2,1)S(1)}, bf16[16,3584]{1,0:T(8,128)(2,1)S(1)}, u32[]{:S(2)}, u32[]{:S(2)}) collective-permute-start(bf16[16,3584]{1,0:T(8,128)(2,1)S(1)} %slice.25), channel_id=1, source_target_pairs={{0,2},{1,3},{2,0},{3,1},{4,6},{5,7},{6,4},{7,5},{8,10},{9,11},{10,... | collective-permute-start | bytes 344072 | tf_op jit(solution)/shard_map/ppermute | solution.py:26
  29.8 9.9 %collective-permute-start.11 = (bf16[16,3584]{1,0:T(8,128)(2,1)S(1)}, bf16[16,3584]{1,0:T(8,128)(2,1)S(1)}, u32[]{:S(2)}, u32[]{:S(2)}) collective-permute-start(bf16[16,3584]{1,0:T(8,128)(2,1)S(1)} %slice.32), channel_id=1, source_target_pairs={{0,4},{1,5},{2,6},{3,7},{4,0},{5,1},{6,2},{7,3},{8,12},{9,13},{10,... | collective-permute-start | bytes 344072 | tf_op jit(solution)/shard_map/ppermute | solution.py:26
  32.1 7.6 %collective-permute-start.12 = (bf16[16,3584]{1,0:T(8,128)(2,1)S(1)}, bf16[16,3584]{1,0:T(8,128)(2,1)S(1)}, u32[]{:S(2)}, u32[]{:S(2)}) collective-permute-start(bf16[16,3584]{1,0:T(8,128)(2,1)S(1)} %slice.33), channel_id=1, source_target_pairs={{0,2},{1,3},{2,0},{3,1},{4,6},{5,7},{6,4},{7,5},{8,10},{9,11},{10,... | collective-permute-start | bytes 344072 | tf_op jit(solution)/shard_map/ppermute | solution.py:26
  35.4 33.0 %all-to-all-start = ((bf16[8,48,1152]{2,1,0:T(8,128)(2,1)}), bf16[8,48,1152]{2,1,0:T(8,128)(2,1)S(1)}, u32[]{:S(2)}, u32[]{:S(2)}) async-start(bf16[8,48,1152]{2,1,0:T(8,128)(2,1)} %get-tuple-element.47), calls=%async_computation | async-start | bytes 1769472 | tf_op jit(solution)/shard_map/all_to_all | solution.py:327
  49.5 6.7 %collective-permute-start.20 = (bf16[16,3584]{1,0:T(8,128)(2,1)S(1)}, bf16[16,3584]{1,0:T(8,128)(2,1)S(1)}, u32[]{:S(2)}, u32[]{:S(2)}) collective-permute-start(bf16[16,3584]{1,0:T(8,128)(2,1)S(1)} %get-tuple-element.54), channel_id=1, source_target_pairs={{0,4},{1,5},{2,6},{3,7},{4,0},{5,1},{6,2},{7,3},{8,12},{9,13},{10,... | collective-permute-start | bytes 344072 | tf_op jit(solution)/shard_map/ppermute | solution.py:26
  51.6 7.4 %collective-permute-start.14 = (bf16[16,3584]{1,0:T(8,128)(2,1)S(1)}, bf16[16,3584]{1,0:T(8,128)(2,1)S(1)}, u32[]{:S(2)}, u32[]{:S(2)}) collective-permute-start(bf16[16,3584]{1,0:T(8,128)(2,1)S(1)} %get-tuple-element.53), channel_id=1, source_target_pairs={{0,2},{1,3},{2,0},{3,1},{4,6},{5,7},{6,4},{7,5},{8,10},{9,11},{10,... | collective-permute-start | bytes 344072 | tf_op jit(solution)/shard_map/ppermute | solution.py:26
  52.1 6.9 %collective-permute-start.15 = (bf16[16,3584]{1,0:T(8,128)(2,1)S(1)}, bf16[16,3584]{1,0:T(8,128)(2,1)S(1)}, u32[]{:S(2)}, u32[]{:S(2)}) collective-permute-start(bf16[16,3584]{1,0:T(8,128)(2,1)S(1)} %get-tuple-element.52), channel_id=1, source_target_pairs={{0,4},{1,5},{2,6},{3,7},{4,0},{5,1},{6,2},{7,3},{8,12},{9,13},{10,... | collective-permute-start | bytes 344072 | tf_op jit(solution)/shard_map/ppermute | solution.py:26
  56.3 6.1 %collective-permute-start.21 = (bf16[16,7168]{1,0:T(8,128)(2,1)S(1)}, bf16[16,7168]{1,0:T(8,128)(2,1)S(1)}, u32[]{:S(2)}, u32[]{:S(2)}) collective-permute-start(bf16[16,7168]{1,0:T(8,128)(2,1)S(1)} %get-tuple-element.42), channel_id=1, source_target_pairs={{0,2},{1,3},{2,0},{3,1},{4,6},{5,7},{6,4},{7,5},{8,10},{9,11},{10,... | collective-permute-start | bytes 688136 | tf_op jit(solution)/shard_map/ppermute | solution.py:26
  57.2 6.4 %collective-permute-start.22 = (bf16[16,7168]{1,0:T(8,128)(2,1)S(1)}, bf16[16,7168]{1,0:T(8,128)(2,1)S(1)}, u32[]{:S(2)}, u32[]{:S(2)}) collective-permute-start(bf16[16,7168]{1,0:T(8,128)(2,1)S(1)} %get-tuple-element.43), channel_id=1, source_target_pairs={{0,4},{1,5},{2,6},{3,7},{4,0},{5,1},{6,2},{7,3},{8,12},{9,13},{10,... | collective-permute-start | bytes 688136 | tf_op jit(solution)/shard_map/ppermute | solution.py:26
  59.1 7.7 %collective-permute-start.16 = (bf16[16,7168]{1,0:T(8,128)(2,1)S(1)}, bf16[16,7168]{1,0:T(8,128)(2,1)S(1)}, u32[]{:S(2)}, u32[]{:S(2)}) collective-permute-start(bf16[16,7168]{1,0:T(8,128)(2,1)S(1)} %get-tuple-element.35), channel_id=1, source_target_pairs={{0,2},{1,3},{2,0},{3,1},{4,6},{5,7},{6,4},{7,5},{8,10},{9,11},{10,... | collective-permute-start | bytes 688136 | tf_op jit(solution)/shard_map/ppermute | solution.py:26
  63.7 6.9 %collective-permute-start.24 = (bf16[8,7168]{1,0:T(8,128)(2,1)S(1)}, bf16[8,7168]{1,0:T(8,128)(2,1)S(1)}, u32[]{:S(2)}, u32[]{:S(2)}) collective-permute-start(bf16[8,7168]{1,0:T(8,128)(2,1)S(1)} %get-tuple-element.45), channel_id=1, source_target_pairs={{0,24},{1,25},{2,26},{3,27},{4,28},{5,29},{6,30},{7,31},{8,16},{9,... | collective-permute-start | bytes 344072 | tf_op jit(solution)/shard_map/ppermute | solution.py:26
  66.7 6.6 %collective-permute-start.23 = (bf16[8,7168]{1,0:T(8,128)(2,1)S(1)}, bf16[8,7168]{1,0:T(8,128)(2,1)S(1)}, u32[]{:S(2)}, u32[]{:S(2)}) collective-permute-start(bf16[8,7168]{1,0:T(8,128)(2,1)S(1)} %get-tuple-element.44), channel_id=1, source_target_pairs={{0,16},{1,17},{2,18},{3,19},{4,20},{5,21},{6,22},{7,23},{8,24},{9,... | collective-permute-start | bytes 344072 | tf_op jit(solution)/shard_map/ppermute | solution.py:26
  67.2 6.1 %collective-permute-start.18 = (bf16[8,7168]{1,0:T(8,128)(2,1)S(1)}, bf16[8,7168]{1,0:T(8,128)(2,1)S(1)}, u32[]{:S(2)}, u32[]{:S(2)}) collective-permute-start(bf16[8,7168]{1,0:T(8,128)(2,1)S(1)} %get-tuple-element.38), channel_id=1, source_target_pairs={{0,8},{1,9},{2,10},{3,11},{4,12},{5,13},{6,14},{7,15},{8,0},{9,1},... | collective-permute-start | bytes 344072 | tf_op jit(solution)/shard_map/ppermute | solution.py:26
  (7 other events, 78.0 us)
